TPU v7x, 512 devices: a whole 4x8x8 slice. The times are simulated.
512 devices in a mesh: rows: 32 (over y, x), cols: 16 (over z, core).
Axes of the slice: x: 4, y: 8, z: 8, core: 2. Of those that a mesh axis runs over, the one named last changes fastest.
Arguments:
- micrograph: float32 [2048, 32768], P('rows', 'cols'), may hold values from -6 to 6
- thresholds: float32 [4, 3], replicated, may hold values from 0.2 to 1.5
Outputs:
- denoised: float32 [2048, 32768], P('rows', 'cols')
All inputs are finite; a program needn't handle non-finite values.
Results may differ from a plain program's by a relative error of at most 0.00002.
Values sent between devices are 32-bit elements; how exact they have to be, the bound alone decides.
No kernel may reach another device: no remote copies, remote signals or barrier semaphores. Data moves between devices by JAX's collectives and lax.ppermute only.
A program may use at most 64 MiB of HBM per device.

v0:
```python
import functools

import jax
import jax.numpy as jnp
from jax import lax
from jax.experimental import pallas as pl
from jax.experimental.pallas import tpu as pltpu
from jax.sharding import PartitionSpec as P

LEVELS = 4

step_one = -1.586134342
step_two = -0.05298011854
step_three = 0.8829110762
step_four = 0.4435068522
band_gain = 1.149604398
inv_gain = 1.0 / band_gain

ROWS, COLS = 64, 2048
WIDE = (1152, 640, 384, 256)
EDGE = (64, 32, 16, 8)
TALL = (96, 48, 24, 16)
OWN = (32, 16, 8, 4)


def soften(coeffs, limit):
    return coeffs - jnp.clip(coeffs, -limit, limit)


def patch(shifted, source, axis, index, flag):
    unit = 8 if axis == 0 else 128
    lo = index // unit * unit
    hi = min(lo + unit, shifted.shape[axis])
    cut = functools.partial(lax.slice_in_dim, axis=axis)
    tile = cut(shifted, lo, hi)
    here = (lax.broadcasted_iota(jnp.int32, tile.shape, axis) == index - lo) & flag
    tile = jnp.where(here, cut(source, lo, hi), tile)
    parts = [cut(shifted, 0, lo)] if lo else []
    parts.append(tile)
    if hi < shifted.shape[axis]:
        parts.append(cut(shifted, hi, shifted.shape[axis]))
    return jnp.concatenate(parts, axis) if len(parts) > 1 else tile


def neighbours(axis, first, count, at_start, at_end):
    def before(odd):
        return patch(pltpu.roll(odd, 1, axis), odd, axis, first, at_start)

    def after(even):
        rolled = pltpu.roll(even, even.shape[axis] - 1, axis)
        return patch(rolled, even, axis, first + count - 1, at_end)

    return before, after


def forward_lift(even, odd, near):
    before, after = near
    odd = odd + step_one * (even + after(even))
    even = even + step_two * (before(odd) + odd)
    odd = odd + step_three * (even + after(even))
    even = even + step_four * (before(odd) + odd)
    return even * band_gain, odd * inv_gain


def inverse_lift(low, high, near):
    before, after = near
    even = low * inv_gain
    odd = high * band_gain
    even = even - step_four * (before(odd) + odd)
    odd = odd - step_three * (even + after(even))
    even = even - step_two * (before(odd) + odd)
    odd = odd - step_one * (even + after(even))
    return even, odd


def pairing(transpose):
    a = lax.broadcasted_iota(jnp.int32, (256, 256), 1 if not transpose else 0)
    b = lax.broadcasted_iota(jnp.int32, (256, 256), 0 if not transpose else 1)
    target = jnp.where(a < 128, 2 * a, 2 * a - 255)
    return jnp.where(b == target, 1.0, 0.0).astype(jnp.bfloat16)


def permuted(x, matrix):
    rows = x.shape[0]
    high = x.astype(jnp.bfloat16)
    rest = x - high.astype(jnp.float32)
    middle = rest.astype(jnp.bfloat16)
    last = (rest - middle.astype(jnp.float32)).astype(jnp.bfloat16)
    out = jnp.dot(
        jnp.concatenate([high, middle, last], 0), matrix, preferred_element_type=jnp.float32
    )
    return (out[:rows] + out[rows : 2 * rows]) + out[2 * rows :]


def tiles(width, body):
    def step(t, carry):
        body(t, pl.ds(pl.multiple_of(t * 128, 128), 128))
        return carry

    lax.fori_loop(0, width // 128, step, 0)


def row_groups(rows, body):
    def step(t, carry):
        body(pl.ds(pl.multiple_of(t * 8, 8), 8))
        return carry

    lax.fori_loop(0, rows // 8, step, 0)


def joined(ref, rows, width):
    return jnp.concatenate([ref[k, rows] for k in range(width // 128)], 1)


def spread(ref, rows, value):
    for k in range(value.shape[1] // 128):
        ref[k, rows] = value[:, 128 * k : 128 * k + 128]


def ends(axis):
    position = lax.axis_index(axis)
    return position % 2 == 0, position == 0, position == lax.axis_size(axis) - 1


def columns_kernel(x_ref, odd_ref, even_ref, send_ref, high_ref, e_ref, o_ref):
    is_even, at_start, at_end = ends("cols")
    matrix = pairing(False)
    left = jnp.where(is_even, odd_ref[:, 128:], even_ref[:, 128:])
    right = jnp.where(is_even, even_ref[:, :128], odd_ref[:, :128])
    for k in range(9):
        if k == 0:
            chunk = jnp.concatenate([left, x_ref[:, :128]], 1)
        elif k == 8:
            chunk = jnp.concatenate([x_ref[:, COLS - 128 :], right], 1)
        else:
            chunk = x_ref[:, 256 * k - 128 : 256 * k + 128]
        both = permuted(chunk, matrix)
        e_ref[:, 128 * k : 128 * k + 128] = both[:, :128]
        o_ref[:, 128 * k : 128 * k + 128] = both[:, 128:]
    near = neighbours(1, EDGE[0], 1024, at_start, at_end)

    def lift(g):
        low, high = forward_lift(e_ref[g, :], o_ref[g, :], near)
        send_ref[g, :] = low
        high_ref[g, :] = high

    row_groups(ROWS, lift)
    send_ref[64:72, :] = high_ref[0:8, :]
    send_ref[72:80, :] = high_ref[56:64, :]


def forward_kernel(t_ref, own_ref, high_ref, odd_ref, even_ref, pack_even, pack_odd, *rest):
    outs, (l_ref, h_ref, b_ref, e_ref, o_ref) = rest[:13], rest[13:]
    is_even, at_start, at_end = ends("rows")
    _, left_end, right_end = ends("cols")
    matrix = pairing(False)

    def gather(t, s):
        l_ref[t, 0:64] = jnp.where(is_even, odd_ref[0:64, s], even_ref[0:64, s])
        l_ref[t, 64:128] = own_ref[0:64, s]
        l_ref[t, 128:192] = jnp.where(is_even, even_ref[0:64, s], odd_ref[0:64, s])
        h_ref[t, 8:16] = jnp.where(is_even, odd_ref[72:80, s], even_ref[72:80, s])
        h_ref[t, 16:80] = high_ref[:, s]
        h_ref[t, 80:88] = jnp.where(is_even, even_ref[64:72, s], odd_ref[64:72, s])

    tiles(WIDE[0], gather)

    def share(level, kind, s, coeffs):
        own = OWN[level]
        outs[3 * level + kind][4 : 4 + own, s] = coeffs
        edge = 2 if level == 0 else 4
        first, last = coeffs[:edge], coeffs[own - edge :]
        at = 2 * kind if level == 0 else 8 + 4 * kind
        lanes = s
        shift = (0, 0, 640, 1024)[level]
        if shift:
            lanes = pl.ds(pl.multiple_of(s.start + shift, 128), 128)
        pack_even[at : at + edge, lanes] = jnp.where(is_even, last, first)
        pack_odd[at : at + edge, lanes] = jnp.where(is_even, first, last)

    for level in range(LEVELS):
        tall, own = TALL[level], OWN[level]
        begin = (32, 16, 8, 4)[level]
        near = neighbours(0, begin, own, at_start, at_end)
        h_tall, h_begin = (48, 8) if level == 0 else (tall, begin)
        h_near = neighbours(0, h_begin, own, at_start, at_end)

        def lift_low(t, s, level=level, tall=tall, own=own, begin=begin, near=near):
            low, high = forward_lift(
                l_ref[t, pl.ds(0, tall, stride=2)], l_ref[t, pl.ds(1, tall, stride=2)], near
            )
            share(level, 1, s, soften(high[begin : begin + own], t_ref[level, 1]))
            if level < LEVELS - 1:
                b_ref[0:tall, s] = low
            else:
                share(level, 3, s, low[begin : begin + own])

        def lift_high(t, s, level=level, own=own, tall=h_tall, begin=h_begin, near=h_near):
            low, high = forward_lift(
                h_ref[t, pl.ds(0, tall, stride=2)], h_ref[t, pl.ds(1, tall, stride=2)], near
            )
            share(level, 0, s, soften(low[begin : begin + own], t_ref[level, 0]))
            share(level, 2, s, soften(high[begin : begin + own], t_ref[level, 2]))

        tiles(WIDE[level], lift_low)
        tiles(WIDE[level], lift_high)
        if level == LEVELS - 1:
            break
        rows = max(tall, 32)
        if tall < rows:
            b_ref[tall:rows, : WIDE[level]] = jnp.zeros((rows - tall, WIDE[level]), jnp.float32)
        wide = WIDE[level + 1]
        if 2 * wide > WIDE[level]:
            b_ref[0:rows, WIDE[level] : 2 * wide] = jnp.zeros((rows, 2 * wide - WIDE[level]), jnp.float32)
        for k in range(wide // 128):
            both = permuted(b_ref[0:rows, 256 * k : 256 * k + 256], matrix)
            e_ref[0:rows, 128 * k : 128 * k + 128] = both[:, :128]
            o_ref[0:rows, 128 * k : 128 * k + 128] = both[:, 128:]
        along = neighbours(1, EDGE[level + 1], 1024 >> (level + 1), left_end, right_end)

        def lift_across(g, wide=wide, along=along):
            low, high = forward_lift(e_ref[g, :wide], o_ref[g, :wide], along)
            spread(l_ref, g, low)
            spread(h_ref, g, high)

        row_groups(rows, lift_across)


def inverse_kernel(odd_ref, even_ref, *rest):
    ins, out_ref, (p_ref, v_ref, w_ref, r_ref), kept = rest[:13], rest[13], rest[14:18], rest[18:]
    is_even, at_start, at_end = ends("rows")
    _, left_end, right_end = ends("cols")
    matrix = pairing(True)

    def choose(t, s):
        up = jnp.where(is_even, odd_ref[:, s], even_ref[:, s])
        down = jnp.where(is_even, even_ref[:, s], odd_ref[:, s])
        p_ref[0:24, s] = up
        p_ref[24:48, s] = down

    tiles(1280, choose)
    for level in range(LEVELS - 1, -1, -1):
        own = OWN[level]
        long = max(own + 8, 16)
        near = neighbours(0, 4, own, at_start, at_end)
        shift = (0, 0, 640, 1024)[level]
        edge = 2 if level == 0 else 4

        def halo(kind, s, level=level, own=own, edge=edge, shift=shift):
            source, target = ins[3 * level + kind], kept[kind]
            at = 2 * kind if level == 0 else 8 + 4 * kind
            lanes = s
            if shift:
                lanes = pl.ds(pl.multiple_of(s.start + shift, 128), 128)
            target[0 : own + 8, s] = source[0 : own + 8, s]
            target[4 - edge : 4, s] = p_ref[at : at + edge, lanes]
            target[4 + own : 4 + own + edge, s] = p_ref[24 + at : 24 + at + edge, lanes]

        def lift_down(t, s, level=level, long=long, near=near, halo=halo):
            for kind in range(4 if level == LEVELS - 1 else 3):
                halo(kind, s)
            low = kept[3][0:long, s] if level == LEVELS - 1 else r_ref[4 : 4 + long, s]
            even, odd = inverse_lift(low, kept[1][0:long, s], near)
            v_ref[t, pl.ds(0, long, stride=2)] = even
            v_ref[t, pl.ds(1, long, stride=2)] = odd
            even, odd = inverse_lift(kept[0][0:long, s], kept[2][0:long, s], near)
            w_ref[t, pl.ds(0, long, stride=2)] = even
            w_ref[t, pl.ds(1, long, stride=2)] = odd

        wide = WIDE[level]
        tiles(wide, lift_down)
        along = neighbours(1, EDGE[level], 1024 >> level, left_end, right_end)
        first, rows = (8, 64) if level == 0 else (0, 2 * long)

        def lift_across(g, wide=wide, along=along, first=first):
            at = pl.ds(pl.multiple_of(g.start + first, 8), 8)
            even, odd = inverse_lift(joined(v_ref, at, wide), joined(w_ref, at, wide), along)
            spread(v_ref, at, even)
            spread(w_ref, at, odd)

        row_groups(rows, lift_across)
        for k in range(wide // 128):
            cut = slice(first, first + rows)
            both = permuted(jnp.concatenate([v_ref[k, cut], w_ref[k, cut]], 1), matrix)
            if level:
                r_ref[0:rows, 256 * k : 256 * k + 256] = both
            elif k == 0:
                out_ref[:, :128] = both[:, 128:]
            elif k == 8:
                out_ref[:, COLS - 128 :] = both[:, :128]
            else:
                out_ref[:, 256 * k - 128 : 256 * k + 128] = both


def swaps(axis, offset):
    count = lax.axis_size(axis)
    pairs = []
    for i in range(offset, count - 1, 2):
        pairs += [(i, i + 1), (i + 1, i)]
    return pairs


def exchange(for_even, for_odd, axis):
    even = lax.ppermute(for_even, axis, swaps(axis, 0))
    odd = lax.ppermute(for_odd, axis, swaps(axis, 1))
    return odd, even


def f32(*shape):
    return jax.ShapeDtypeStruct(shape, jnp.float32)


def scratch(*shape):
    return pltpu.VMEM(shape, jnp.float32)


def call(kernel, outs, scratches, *args, scalars=0):
    vmem = pl.BlockSpec(memory_space=pltpu.VMEM)
    smem = pl.BlockSpec(memory_space=pltpu.SMEM)
    return pl.pallas_call(
        kernel,
        out_shape=outs,
        in_specs=[smem] * scalars + [vmem] * (len(args) - scalars),
        out_specs=jax.tree.map(lambda _: vmem, outs),
        scratch_shapes=scratches,
        compiler_params=pltpu.CompilerParams(vmem_limit_bytes=16 * 2**20),
    )(*args)


def local(micrograph, thresholds):
    edges = jnp.concatenate([micrograph[:, :128], micrograph[:, COLS - 128 :]], 1)
    odd, even = exchange(edges, edges, "cols")
    block, high = call(
        columns_kernel,
        (f32(80, 1152), f32(64, 1152)),
        [scratch(64, 1152), scratch(64, 1152)],
        micrograph,
        odd,
        even,
    )
    odd, even = exchange(block, block, "rows")
    shapes = [f32(OWN[level] + 8, WIDE[level]) for level in range(LEVELS) for _ in range(3)]
    shapes.append(shapes[-1])
    pack_even, pack_odd, *bands = call(
        forward_kernel,
        (f32(24, 1280), f32(24, 1280), *shapes),
        [
            scratch(9, 192, 128),
            scratch(9, 96, 128),
            scratch(96, 1280),
            scratch(96, 640),
            scratch(96, 640),
        ],
        thresholds,
        block,
        high,
        odd,
        even,
        scalars=1,
    )
    odd, even = exchange(pack_even, pack_odd, "rows")
    return call(
        inverse_kernel,
        f32(ROWS, COLS),
        [scratch(48, 1280), scratch(9, 80, 128), scratch(9, 80, 128), scratch(48, 1280)]
        + [scratch(40, 1152)] * 3
        + [scratch(16, 256)],
        odd,
        even,
        *bands,
    )


def solution(mesh):
    placed = (P("rows", "cols"), P())
    return jax.shard_map(
        local, mesh=mesh, in_specs=placed, out_specs=P("rows", "cols"), check_vma=False
    )
```

profile of v0, /device:TPU:222, one launch (start us, length us, event | category | flops | bytes accessed | tf_op | source)
XLA Modules:
  0.0 62.6 jit_solution(14377258507805678826)
XLA Ops:
  0.0 0.8 %fusion = (f32[64,128]{1,0:T(8,128)S(1)}, f32[64,128]{1,0:T(8,128)S(1)}) fusion(f32[64,2048]{1,0:T(8,128)} %x_ref.1), kind=kLoop, calls=%fused_computation.1 | loop fusion | bytes 131072 | tf_op jit(solution)/shard_map/slice | solution.py:331
  0.8 1.9 %collective-permute-start.1 = (f32[64,256]{1,0:T(8,128)S(1)}, f32[64,256]{1,0:T(8,128)S(1)}, u32[]{:S(2)}, u32[]{:S(2)}) collective-permute-start(f32[64,256]{1,0:T(8,128)S(1)} %pad_maximum_fusion), channel_id=1, source_target_pairs={{0,1},{1,0},{2,3},{3,2},{4,5},{5,4},{6,7},{7,6},{8,9},{9,8},{10,11... | collective-permute-start | bytes 196616 | tf_op jit(solution)/shard_map/ppermute | solution.py:304
  2.7 1.9 %collective-permute-start = (f32[64,256]{1,0:T(8,128)S(1)}, f32[64,256]{1,0:T(8,128)S(1)}, u32[]{:S(2)}, u32[]{:S(2)}) collective-permute-start(f32[64,256]{1,0:T(8,128)S(1)} %pad_maximum_fusion), channel_id=1, source_target_pairs={{1,2},{2,1},{3,4},{4,3},{5,6},{6,5},{7,8},{8,7},{9,10},{10,9},{11,... | collective-permute-start | bytes 196616 | tf_op jit(solution)/shard_map/ppermute | solution.py:305
  4.6 0.0 collective-permute-done.1.even_ref
  4.7 3.6 %collective-permute-done.odd_ref = f32[64,256]{1,0:T(8,128)S(1)} collective-permute-done((f32[64,256]{1,0:T(8,128)S(1)}, f32[64,256]{1,0:T(8,128)S(1)}, u32[]{:S(2)}, u32[]{:S(2)}) %collective-permute-start) | collective-permute-done | bytes 65568 | tf_op jit(solution)/shard_map/ppermute | solution.py:305
  8.3 0.0 copy-start
  8.3 1.0 %copy-done = f32[64,2048]{1,0:T(8,128)S(1)} copy-done((f32[64,2048]{1,0:T(8,128)S(1)}, f32[64,2048]{1,0:T(8,128)}, u32[]{:S(2)}) %copy-start) | copy-done | bytes 524312
  9.3 2.8 %shard_map.28 = (f32[80,1152]{1,0:T(8,128)S(1)}, f32[64,1152]{1,0:T(8,128)S(1)}) custom-call(f32[64,2048]{1,0:T(8,128)S(1)} %copy-done, f32[64,256]{1,0:T(8,128)S(1)} %collective-permute-done.odd_ref, f32[64,256]{1,0:T(8,128)S(1)} %collective-permute-done.1.even_ref), custom_call_target="tpu_custom_call" | custom-call | tf_op jit(solution)/shard_map/pallas_call | solution.py:320
  12.2 0.0 copy-start.1
  12.2 2.7 %collective-permute-start.3 = (f32[80,1152]{1,0:T(8,128)S(1)}, f32[80,1152]{1,0:T(8,128)S(1)}, u32[]{:S(2)}, u32[]{:S(2)}) collective-permute-start(f32[80,1152]{1,0:T(8,128)S(1)} %get-tuple-element.22.own_ref), channel_id=1, source_target_pairs={{0,16},{16,0},{32,48},{48,32},{64,80},{80,64},{96,112},{112,96},{1... | collective-permute-start | bytes 1105928 | tf_op jit(solution)/shard_map/ppermute | solution.py:304
  14.9 5.3 %collective-permute-start.2 = (f32[80,1152]{1,0:T(8,128)S(1)}, f32[80,1152]{1,0:T(8,128)S(1)}, u32[]{:S(2)}, u32[]{:S(2)}) collective-permute-start(f32[80,1152]{1,0:T(8,128)S(1)} %get-tuple-element.22.own_ref), channel_id=1, source_target_pairs={{16,32},{32,16},{48,64},{64,48},{80,96},{96,80},{112,128},{128,112... | collective-permute-start | bytes 1105928 | tf_op jit(solution)/shard_map/ppermute | solution.py:305
  20.2 4.4 %collective-permute-done.3.even_ref = f32[80,1152]{1,0:T(8,128)S(1)} collective-permute-done((f32[80,1152]{1,0:T(8,128)S(1)}, f32[80,1152]{1,0:T(8,128)S(1)}, u32[]{:S(2)}, u32[]{:S(2)}) %collective-permute-start.3) | collective-permute-done | bytes 368672 | tf_op jit(solution)/shard_map/ppermute | solution.py:304
  24.6 6.4 %collective-permute-done.2.odd_ref = f32[80,1152]{1,0:T(8,128)S(1)} collective-permute-done((f32[80,1152]{1,0:T(8,128)S(1)}, f32[80,1152]{1,0:T(8,128)S(1)}, u32[]{:S(2)}, u32[]{:S(2)}) %collective-permute-start.2) | collective-permute-done | bytes 368672 | tf_op jit(solution)/shard_map/ppermute | solution.py:305
  30.9 0.0 copy-done.1
  31.0 9.4 %shard_map.29 = (f32[24,1280]{1,0:T(8,128)S(1)}, f32[24,1280]{1,0:T(8,128)S(1)}, f32[40,1152]{1,0:T(8,128)S(1)}, f32[40,1152]{1,0:T(8,128)S(1)}, f32[40,1152]{1,...) custom-call(f32[4,3]{1,0:T(4,128)S(1)} %copy-done.1, ...), custom_call_target="tpu_custom_call" | custom-call | tf_op jit(solution)/shard_map/pallas_call | solution.py:320
  40.4 5.3 %collective-permute-start.4 = (f32[24,1280]{1,0:T(8,128)S(1)}, f32[24,1280]{1,0:T(8,128)S(1)}, u32[]{:S(2)}, u32[]{:S(2)}) collective-permute-start(f32[24,1280]{1,0:T(8,128)S(1)} %get-tuple-element.24), channel_id=1, source_target_pairs={{16,32},{32,16},{48,64},{64,48},{80,96},{96,80},{112,128},{128,112... | collective-permute-start | bytes 368648 | tf_op jit(solution)/shard_map/ppermute | solution.py:305
  45.7 1.9 %collective-permute-start.5 = (f32[24,1280]{1,0:T(8,128)S(1)}, f32[24,1280]{1,0:T(8,128)S(1)}, u32[]{:S(2)}, u32[]{:S(2)}) collective-permute-start(f32[24,1280]{1,0:T(8,128)S(1)} %get-tuple-element.25), channel_id=1, source_target_pairs={{0,16},{16,0},{32,48},{48,32},{64,80},{80,64},{96,112},{112,96},{1... | collective-permute-start | bytes 368648 | tf_op jit(solution)/shard_map/ppermute | solution.py:304
  47.6 3.7 %collective-permute-done.4.odd_ref = f32[24,1280]{1,0:T(8,128)S(1)} collective-permute-done((f32[24,1280]{1,0:T(8,128)S(1)}, f32[24,1280]{1,0:T(8,128)S(1)}, u32[]{:S(2)}, u32[]{:S(2)}) %collective-permute-start.4) | collective-permute-done | bytes 122912 | tf_op jit(solution)/shard_map/ppermute | solution.py:305
  51.3 1.7 %collective-permute-done.5.even_ref = f32[24,1280]{1,0:T(8,128)S(1)} collective-permute-done((f32[24,1280]{1,0:T(8,128)S(1)}, f32[24,1280]{1,0:T(8,128)S(1)}, u32[]{:S(2)}, u32[]{:S(2)}) %collective-permute-start.5) | collective-permute-done | bytes 122912 | tf_op jit(solution)/shard_map/ppermute | solution.py:304
  53.0 9.6 %shard_map.30 = f32[64,2048]{1,0:T(8,128)} custom-call(f32[24,1280]{1,0:T(8,128)S(1)} %collective-permute-done.4.odd_ref, f32[24,1280]{1,0:T(8,128)S(1)} %collective-permute-done.5.even_ref, f32[40,1152]{1,0:T(8,128)S(1)} %get-tuple-element.26.rest_0_, f32[40,1152]{1,0:T(8,128)S(1)} %get-tuple-element.27.rest_1_, f32[40,1152]{1,0:T(8,128)S(1)} %get-tuple-element.28.rest_2_, ...), custom_call_target="tpu_custom_call" | custom-call | tf_op jit(solution)/shard_map/pallas_call | solution.py:320
  (1 shorter events, 0.0 us)
Async XLA Ops:
  0.8 3.9 %collective-permute-start.1 = (f32[64,256]{1,0:T(8,128)S(1)}, f32[64,256]{1,0:T(8,128)S(1)}, u32[]{:S(2)}, u32[]{:S(2)}) collective-permute-start(f32[64,256]{1,0:T(8,128)S(1)} %pad_maximum_fusion), channel_id=1, source_target_pairs={{0,1},{1,0},{2,3},{3,2},{4,5},{5,4},{6,7},{7,6},{8,9},{9,8},{10,11... | collective-permute-start | bytes 196616 | tf_op jit(solution)/shard_map/ppermute | solution.py:304
  2.7 5.6 %collective-permute-start = (f32[64,256]{1,0:T(8,128)S(1)}, f32[64,256]{1,0:T(8,128)S(1)}, u32[]{:S(2)}, u32[]{:S(2)}) collective-permute-start(f32[64,256]{1,0:T(8,128)S(1)} %pad_maximum_fusion), channel_id=1, source_target_pairs={{1,2},{2,1},{3,4},{4,3},{5,6},{6,5},{7,8},{8,7},{9,10},{10,9},{11,... | collective-permute-start | bytes 196616 | tf_op jit(solution)/shard_map/ppermute | solution.py:305
  8.3 1.0 %copy-start = (f32[64,2048]{1,0:T(8,128)S(1)}, f32[64,2048]{1,0:T(8,128)}, u32[]{:S(2)}) copy-start(f32[64,2048]{1,0:T(8,128)} %x_ref.1) | copy-start | bytes 1572868
  12.2 18.8 %copy-start.1 = (f32[4,3]{1,0:T(4,128)S(1)}, f32[4,3]{1,0:T(4,128)}, u32[]{:S(2)}) copy-start(f32[4,3]{1,0:T(4,128)} %t_ref.1) | copy-start | bytes 148
  12.2 12.4 %collective-permute-start.3 = (f32[80,1152]{1,0:T(8,128)S(1)}, f32[80,1152]{1,0:T(8,128)S(1)}, u32[]{:S(2)}, u32[]{:S(2)}) collective-permute-start(f32[80,1152]{1,0:T(8,128)S(1)} %get-tuple-element.22.own_ref), channel_id=1, source_target_pairs={{0,16},{16,0},{32,48},{48,32},{64,80},{80,64},{96,112},{112,96},{1... | collective-permute-start | bytes 1105928 | tf_op jit(solution)/shard_map/ppermute | solution.py:304
  14.9 16.0 %collective-permute-start.2 = (f32[80,1152]{1,0:T(8,128)S(1)}, f32[80,1152]{1,0:T(8,128)S(1)}, u32[]{:S(2)}, u32[]{:S(2)}) collective-permute-start(f32[80,1152]{1,0:T(8,128)S(1)} %get-tuple-element.22.own_ref), channel_id=1, source_target_pairs={{16,32},{32,16},{48,64},{64,48},{80,96},{96,80},{112,128},{128,112... | collective-permute-start | bytes 1105928 | tf_op jit(solution)/shard_map/ppermute | solution.py:305
  40.4 10.9 %collective-permute-start.4 = (f32[24,1280]{1,0:T(8,128)S(1)}, f32[24,1280]{1,0:T(8,128)S(1)}, u32[]{:S(2)}, u32[]{:S(2)}) collective-permute-start(f32[24,1280]{1,0:T(8,128)S(1)} %get-tuple-element.24), channel_id=1, source_target_pairs={{16,32},{32,16},{48,64},{64,48},{80,96},{96,80},{112,128},{128,112... | collective-permute-start | bytes 368648 | tf_op jit(solution)/shard_map/ppermute | solution.py:305
  45.7 7.3 %collective-permute-start.5 = (f32[24,1280]{1,0:T(8,128)S(1)}, f32[24,1280]{1,0:T(8,128)S(1)}, u32[]{:S(2)}, u32[]{:S(2)}) collective-permute-start(f32[24,1280]{1,0:T(8,128)S(1)} %get-tuple-element.25), channel_id=1, source_target_pairs={{0,16},{16,0},{32,48},{48,32},{64,80},{80,64},{96,112},{112,96},{1... | collective-permute-start | bytes 368648 | tf_op jit(solution)/shard_map/ppermute | solution.py:304
where the time goes:
time: 62.9 us; the launch traced here: 62.6 us
  Pallas kernels  21.8 us (35%)
  waiting for transfers between devices  19.8 us (31%)
  starting transfers between devices  19.1 us (30%)
  local copies, waits for them, and re-layouts  1.83 us (3%)
    pallas_call x3, Pallas kernels, call(): pl.pallas_call(kernel, out_shape=outs, in_specs=[smem] * scalars + [vmem]...  21.8 us
    ppermute x3, waiting for transfers between devices, exchange(): odd = lax.ppermute(for_odd, axis, swaps(axis, 1))  13.7 us
    ppermute x3, starting transfers between devices, exchange(): odd = lax.ppermute(for_odd, axis, swaps(axis, 1))  12.5 us
    ppermute x3, starting transfers between devices, exchange(): even = lax.ppermute(for_even, axis, swaps(axis, 0))  6.57 us
    ppermute x3, waiting for transfers between devices, exchange(): even = lax.ppermute(for_even, axis, swaps(axis, 0))  6.04 us
  transfers between devices with their start and end apart: 6, of which 5 were waited for; matrix products, arithmetic and copies ran while one was open for 0% of the time, Pallas kernels for 0%

commit v1 on v0

--- a/solution.py
+++ b/solution.py
@@ -100,12 +100,15 @@
     lax.fori_loop(0, width // 128, step, 0)
 
 
-def row_groups(rows, body):
+def row_groups(rows, size, body):
     def step(t, carry):
-        body(pl.ds(pl.multiple_of(t * 8, 8), 8))
+        body(pl.ds(pl.multiple_of(t * size, 8), size))
         return carry
 
-    lax.fori_loop(0, rows // 8, step, 0)
+    if size == rows:
+        body(pl.ds(0, rows))
+    else:
+        lax.fori_loop(0, rows // size, step, 0)
 
 
 def joined(ref, rows, width):
@@ -122,31 +125,45 @@
     return position % 2 == 0, position == 0, position == lax.axis_size(axis) - 1
 
 
-def columns_kernel(x_ref, odd_ref, even_ref, send_ref, high_ref, e_ref, o_ref):
+def edges_kernel(x_ref, for_even, for_odd, sems):
+    is_even = ends("cols")[0]
+    right = jnp.where(is_even, COLS - 128, 0)
+    copies = []
+    for k, (at, out) in enumerate(((right, for_even), (COLS - 128 - right, for_odd))):
+        lanes = pl.ds(pl.multiple_of(at, 128), 128)
+        copies.append(pltpu.make_async_copy(x_ref.at[:, lanes], out, sems.at[k]))
+        copies[-1].start()
+    for copy in copies:
+        copy.wait()
+
+
+def inner_kernel(x_ref, e_ref, o_ref, edge_ref):
+    matrix = pairing(False)
+    for k in range(7):
+        both = permuted(x_ref[:, 256 * k + 128 : 256 * k + 384], matrix)
+        e_ref[:, 128 * k : 128 * k + 128] = both[:, :128]
+        o_ref[:, 128 * k : 128 * k + 128] = both[:, 128:]
+    edge_ref[:, :128] = x_ref[:, :128]
+    edge_ref[:, 128:] = x_ref[:, COLS - 128 :]
+
+
+def columns_kernel(e_ref, o_ref, edge_ref, odd_ref, even_ref, send_ref, high_ref):
     is_even, at_start, at_end = ends("cols")
     matrix = pairing(False)
-    left = jnp.where(is_even, odd_ref[:, 128:], even_ref[:, 128:])
-    right = jnp.where(is_even, even_ref[:, :128], odd_ref[:, :128])
-    for k in range(9):
-        if k == 0:
-            chunk = jnp.concatenate([left, x_ref[:, :128]], 1)
-        elif k == 8:
-            chunk = jnp.concatenate([x_ref[:, COLS - 128 :], right], 1)
-        else:
-            chunk = x_ref[:, 256 * k - 128 : 256 * k + 128]
-        both = permuted(chunk, matrix)
-        e_ref[:, 128 * k : 128 * k + 128] = both[:, :128]
-        o_ref[:, 128 * k : 128 * k + 128] = both[:, 128:]
+    left = jnp.where(is_even, odd_ref[...], even_ref[...])
+    right = jnp.where(is_even, even_ref[...], odd_ref[...])
+    first = permuted(jnp.concatenate([left, edge_ref[:, :128]], 1), matrix)
+    last = permuted(jnp.concatenate([edge_ref[:, 128:], right], 1), matrix)
     near = neighbours(1, EDGE[0], 1024, at_start, at_end)
-
-    def lift(g):
-        low, high = forward_lift(e_ref[g, :], o_ref[g, :], near)
-        send_ref[g, :] = low
-        high_ref[g, :] = high
-
-    row_groups(ROWS, lift)
-    send_ref[64:72, :] = high_ref[0:8, :]
-    send_ref[72:80, :] = high_ref[56:64, :]
+    low, high = forward_lift(
+        jnp.concatenate([first[:, :128], e_ref[...], last[:, :128]], 1),
+        jnp.concatenate([first[:, 128:], o_ref[...], last[:, 128:]], 1),
+        near,
+    )
+    send_ref[0:64, :] = low
+    high_ref[...] = high
+    send_ref[64:72, :] = high[0:8]
+    send_ref[72:80, :] = high[56:64]
 
 
 def forward_kernel(t_ref, own_ref, high_ref, odd_ref, even_ref, pack_even, pack_odd, *rest):
@@ -223,7 +240,7 @@
             spread(l_ref, g, low)
             spread(h_ref, g, high)
 
-        row_groups(rows, lift_across)
+        row_groups(rows, rows, lift_across)
 
 
 def inverse_kernel(odd_ref, even_ref, *rest):
@@ -273,12 +290,12 @@
         first, rows = (8, 64) if level == 0 else (0, 2 * long)
 
         def lift_across(g, wide=wide, along=along, first=first):
-            at = pl.ds(pl.multiple_of(g.start + first, 8), 8)
+            at = pl.ds(g.start + first, g.size)
             even, odd = inverse_lift(joined(v_ref, at, wide), joined(w_ref, at, wide), along)
             spread(v_ref, at, even)
             spread(w_ref, at, odd)
 
-        row_groups(rows, lift_across)
+        row_groups(rows, rows, lift_across)
         for k in range(wide // 128):
             cut = slice(first, first + rows)
             both = permuted(jnp.concatenate([v_ref[k, cut], w_ref[k, cut]], 1), matrix)
@@ -314,30 +331,37 @@
     return pltpu.VMEM(shape, jnp.float32)
 
 
-def call(kernel, outs, scratches, *args, scalars=0):
+def call(kernel, outs, scratches, *args, scalars=0, space=pltpu.VMEM, cost=None):
     vmem = pl.BlockSpec(memory_space=pltpu.VMEM)
     smem = pl.BlockSpec(memory_space=pltpu.SMEM)
     return pl.pallas_call(
         kernel,
         out_shape=outs,
-        in_specs=[smem] * scalars + [vmem] * (len(args) - scalars),
+        in_specs=[smem] * scalars + [pl.BlockSpec(memory_space=space)] * (len(args) - scalars),
         out_specs=jax.tree.map(lambda _: vmem, outs),
         scratch_shapes=scratches,
         compiler_params=pltpu.CompilerParams(vmem_limit_bytes=16 * 2**20),
+        cost_estimate=cost,
     )(*args)
 
 
 def local(micrograph, thresholds):
-    edges = jnp.concatenate([micrograph[:, :128], micrograph[:, COLS - 128 :]], 1)
-    odd, even = exchange(edges, edges, "cols")
-    block, high = call(
-        columns_kernel,
-        (f32(80, 1152), f32(64, 1152)),
-        [scratch(64, 1152), scratch(64, 1152)],
+    for_even, for_odd = call(
+        edges_kernel,
+        (f32(ROWS, 128), f32(ROWS, 128)),
+        [pltpu.SemaphoreType.DMA((2,))],
         micrograph,
-        odd,
-        even,
-    )
+        space=pltpu.HBM,
+    )
+    odd, even = exchange(for_even, for_odd, "cols")
+    inner = call(
+        inner_kernel,
+        (f32(ROWS, 896), f32(ROWS, 896), f32(ROWS, 256)),
+        [],
+        micrograph,
+        cost=pl.CostEstimate(flops=2 * 10**9, bytes_accessed=4 * 10**6, transcendentals=0),
+    )
+    block, high = call(columns_kernel, (f32(80, 1152), f32(64, 1152)), [], *inner, odd, even)
     odd, even = exchange(block, block, "rows")
     shapes = [f32(OWN[level] + 8, WIDE[level]) for level in range(LEVELS) for _ in range(3)]
     shapes.append(shapes[-1])

time: 62.9 us -> 49 us (0.78)
  Pallas kernels: 21.8 us -> 9.02 us
  waiting for transfers between devices: 19.8 us -> 15.8 us
  starting transfers between devices: 19.1 us -> 22.7 us
  local copies, waits for them, and re-layouts: 1.83 us -> 1.05 us
    pallas_call x3 -> x5, Pallas kernels: 21.8 us -> 9.02 us  [call(): pl.pallas_call(kernel, out_shape=outs, in_specs=[smem] * scalars + [pl.Bl...]
    ppermute x3, waiting for transfers between devices: 13.7 us -> 8.66 us  [exchange(): odd = lax.ppermute(for_odd, axis, swaps(axis, 1))]
    ppermute x3, starting transfers between devices: 6.57 us -> 10.3 us  [exchange(): even = lax.ppermute(for_even, axis, swaps(axis, 0))]
    ppermute x3, waiting for transfers between devices: 6.04 us -> 7.14 us  [exchange(): even = lax.ppermute(for_even, axis, swaps(axis, 0))]
    slice x1 -> x0, local copies, waits for them, and re-layouts: 0.78 us -> none  [local(): micrograph[:, :128]]
  transfers between devices with their start and end apart: 6 -> 6, of which waited for: 5 -> 5; matrix products, arithmetic and copies ran while one was open for 0% -> 0% of each run, Pallas kernels for 0% -> 1%
where the time goes in v1:
time: 49 us; the launch traced here: 48.7 us
  starting transfers between devices  22.7 us (46%)
  waiting for transfers between devices  15.8 us (32%)
  Pallas kernels  9.02 us (18%)
  local copies, waits for them, and re-layouts  1.05 us (2%)
    ppermute x3, starting transfers between devices, exchange(): odd = lax.ppermute(for_odd, axis, swaps(axis, 1))  12.5 us
    ppermute x3, starting transfers between devices, exchange(): even = lax.ppermute(for_even, axis, swaps(axis, 0))  10.3 us
    pallas_call x5, Pallas kernels, call(): pl.pallas_call(kernel, out_shape=outs, in_specs=[smem] * scalars + [pl.Bl...  9.02 us
    ppermute x3, waiting for transfers between devices, exchange(): odd = lax.ppermute(for_odd, axis, swaps(axis, 1))  8.66 us
    ppermute x3, waiting for transfers between devices, exchange(): even = lax.ppermute(for_even, axis, swaps(axis, 0))  7.14 us
    unnamed x4, local copies, waits for them, and re-layouts  1.05 us
  transfers between devices with their start and end apart: 6, of which 5 were waited for; matrix products, arithmetic and copies ran while one was open for 0% of the time, Pallas kernels for 1%

profile of v1, /device:TPU:222, one launch (start us, length us, event | category | flops | bytes accessed | tf_op | source)
XLA Modules:
  0.0 48.7 jit_solution(5321774366484237078)
XLA Ops:
  0.0 0.0 copy-start
  0.0 1.0 %copy-done = f32[64,2048]{1,0:T(8,128)S(1)} copy-done((f32[64,2048]{1,0:T(8,128)S(1)}, f32[64,2048]{1,0:T(8,128)}, u32[]{:S(2)}) %copy-start) | copy-done | bytes 524312
  1.1 1.9 %collective-permute-start = (f32[64,128]{1,0:T(8,128)S(1)}, f32[64,128]{1,0:T(8,128)S(1)}, u32[]{:S(2)}, u32[]{:S(2)}) collective-permute-start(f32[64,128]{1,0:T(8,128)S(1)} %get-tuple-element.30), channel_id=1, source_target_pairs={{1,2},{2,1},{3,4},{4,3},{5,6},{6,5},{7,8},{8,7},{9,10},{10,9},{11,... | collective-permute-start | bytes 98312 | tf_op jit(solution)/shard_map/ppermute | solution.py:322
  3.0 5.6 %collective-permute-start.1 = (f32[64,128]{1,0:T(8,128)S(1)}, f32[64,128]{1,0:T(8,128)S(1)}, u32[]{:S(2)}, u32[]{:S(2)}) collective-permute-start(f32[64,128]{1,0:T(8,128)S(1)} %get-tuple-element.31), channel_id=1, source_target_pairs={{0,1},{1,0},{2,3},{3,2},{4,5},{5,4},{6,7},{7,6},{8,9},{9,8},{10,11... | collective-permute-start | bytes 98312 | tf_op jit(solution)/shard_map/ppermute | solution.py:321
  8.6 0.4 shard_map.28
  9.0 0.0 collective-permute-done.odd_ref
  9.0 0.5 collective-permute-done.1.even_ref
  9.5 0.6 %shard_map.30 = (f32[80,1152]{1,0:T(8,128)S(1)}, f32[64,1152]{1,0:T(8,128)S(1)}) custom-call(f32[64,896]{1,0:T(8,128)S(1)} %get-tuple-element.27.e_ref, f32[64,896]{1,0:T(8,128)S(1)} %get-tuple-element.28.o_ref, f32[64,256]{1,0:T(8,128)S(1)} %get-tuple-element.29.edge_ref, f32[64,128]{1,0:T(8,128)S(1)} %collective-permute-done.odd_ref, ...), custom_call_target="tpu_custom_call" | custom-call | tf_op jit(solution)/shard_map/pallas_call | solution.py:337
  10.0 0.0 copy-start.1
  10.0 2.7 %collective-permute-start.3 = (f32[80,1152]{1,0:T(8,128)S(1)}, f32[80,1152]{1,0:T(8,128)S(1)}, u32[]{:S(2)}, u32[]{:S(2)}) collective-permute-start(f32[80,1152]{1,0:T(8,128)S(1)} %get-tuple-element.32.own_ref), channel_id=1, source_target_pairs={{0,16},{16,0},{32,48},{48,32},{64,80},{80,64},{96,112},{112,96},{1... | collective-permute-start | bytes 1105928 | tf_op jit(solution)/shard_map/ppermute | solution.py:321
  12.8 5.3 %collective-permute-start.2 = (f32[80,1152]{1,0:T(8,128)S(1)}, f32[80,1152]{1,0:T(8,128)S(1)}, u32[]{:S(2)}, u32[]{:S(2)}) collective-permute-start(f32[80,1152]{1,0:T(8,128)S(1)} %get-tuple-element.32.own_ref), channel_id=1, source_target_pairs={{16,32},{32,16},{48,64},{64,48},{80,96},{96,80},{112,128},{128,112... | collective-permute-start | bytes 1105928 | tf_op jit(solution)/shard_map/ppermute | solution.py:322
  18.0 4.7 %collective-permute-done.3.even_ref = f32[80,1152]{1,0:T(8,128)S(1)} collective-permute-done((f32[80,1152]{1,0:T(8,128)S(1)}, f32[80,1152]{1,0:T(8,128)S(1)}, u32[]{:S(2)}, u32[]{:S(2)}) %collective-permute-start.3) | collective-permute-done | bytes 368672 | tf_op jit(solution)/shard_map/ppermute | solution.py:321
  22.8 5.8 %collective-permute-done.2.odd_ref = f32[80,1152]{1,0:T(8,128)S(1)} collective-permute-done((f32[80,1152]{1,0:T(8,128)S(1)}, f32[80,1152]{1,0:T(8,128)S(1)}, u32[]{:S(2)}, u32[]{:S(2)}) %collective-permute-start.2) | collective-permute-done | bytes 368672 | tf_op jit(solution)/shard_map/ppermute | solution.py:322
  28.5 0.0 copy-done.1
  28.5 3.8 %shard_map.31 = (f32[24,1280]{1,0:T(8,128)S(1)}, f32[24,1280]{1,0:T(8,128)S(1)}, f32[40,1152]{1,0:T(8,128)S(1)}, f32[40,1152]{1,0:T(8,128)S(1)}, f32[40,1152]{1,...) custom-call(f32[4,3]{1,0:T(4,128)S(1)} %copy-done.1, ...), custom_call_target="tpu_custom_call" | custom-call | tf_op jit(solution)/shard_map/pallas_call | solution.py:337
  32.4 5.3 %collective-permute-start.4 = (f32[24,1280]{1,0:T(8,128)S(1)}, f32[24,1280]{1,0:T(8,128)S(1)}, u32[]{:S(2)}, u32[]{:S(2)}) collective-permute-start(f32[24,1280]{1,0:T(8,128)S(1)} %get-tuple-element.34), channel_id=1, source_target_pairs={{16,32},{32,16},{48,64},{64,48},{80,96},{96,80},{112,128},{128,112... | collective-permute-start | bytes 368648 | tf_op jit(solution)/shard_map/ppermute | solution.py:322
  37.7 1.9 %collective-permute-start.5 = (f32[24,1280]{1,0:T(8,128)S(1)}, f32[24,1280]{1,0:T(8,128)S(1)}, u32[]{:S(2)}, u32[]{:S(2)}) collective-permute-start(f32[24,1280]{1,0:T(8,128)S(1)} %get-tuple-element.35), channel_id=1, source_target_pairs={{0,16},{16,0},{32,48},{48,32},{64,80},{80,64},{96,112},{112,96},{1... | collective-permute-start | bytes 368648 | tf_op jit(solution)/shard_map/ppermute | solution.py:321
  39.6 2.9 %collective-permute-done.4.odd_ref = f32[24,1280]{1,0:T(8,128)S(1)} collective-permute-done((f32[24,1280]{1,0:T(8,128)S(1)}, f32[24,1280]{1,0:T(8,128)S(1)}, u32[]{:S(2)}, u32[]{:S(2)}) %collective-permute-start.4) | collective-permute-done | bytes 122912 | tf_op jit(solution)/shard_map/ppermute | solution.py:322
  42.5 2.0 %collective-permute-done.5.even_ref = f32[24,1280]{1,0:T(8,128)S(1)} collective-permute-done((f32[24,1280]{1,0:T(8,128)S(1)}, f32[24,1280]{1,0:T(8,128)S(1)}, u32[]{:S(2)}, u32[]{:S(2)}) %collective-permute-start.5) | collective-permute-done | bytes 122912 | tf_op jit(solution)/shard_map/ppermute | solution.py:321
  44.4 4.3 %shard_map.32 = f32[64,2048]{1,0:T(8,128)} custom-call(f32[24,1280]{1,0:T(8,128)S(1)} %collective-permute-done.4.odd_ref, f32[24,1280]{1,0:T(8,128)S(1)} %collective-permute-done.5.even_ref, f32[40,1152]{1,0:T(8,128)S(1)} %get-tuple-element.36.rest_0_, f32[40,1152]{1,0:T(8,128)S(1)} %get-tuple-element.37.rest_1_, f32[40,1152]{1,0:T(8,128)S(1)} %get-tuple-element.38.rest_2_, ...), custom_call_target="tpu_custom_call" | custom-call | tf_op jit(solution)/shard_map/pallas_call | solution.py:337
  (1 shorter events, 0.0 us)
Async XLA Ops:
  0.0 1.0 %copy-start = (f32[64,2048]{1,0:T(8,128)S(1)}, f32[64,2048]{1,0:T(8,128)}, u32[]{:S(2)}) copy-start(f32[64,2048]{1,0:T(8,128)} %x_ref.3) | copy-start | bytes 1572868
  1.1 7.9 %collective-permute-start = (f32[64,128]{1,0:T(8,128)S(1)}, f32[64,128]{1,0:T(8,128)S(1)}, u32[]{:S(2)}, u32[]{:S(2)}) collective-permute-start(f32[64,128]{1,0:T(8,128)S(1)} %get-tuple-element.30), channel_id=1, source_target_pairs={{1,2},{2,1},{3,4},{4,3},{5,6},{6,5},{7,8},{8,7},{9,10},{10,9},{11,... | collective-permute-start | bytes 98312 | tf_op jit(solution)/shard_map/ppermute | solution.py:322
  3.0 6.4 %collective-permute-start.1 = (f32[64,128]{1,0:T(8,128)S(1)}, f32[64,128]{1,0:T(8,128)S(1)}, u32[]{:S(2)}, u32[]{:S(2)}) collective-permute-start(f32[64,128]{1,0:T(8,128)S(1)} %get-tuple-element.31), channel_id=1, source_target_pairs={{0,1},{1,0},{2,3},{3,2},{4,5},{5,4},{6,7},{7,6},{8,9},{9,8},{10,11... | collective-permute-start | bytes 98312 | tf_op jit(solution)/shard_map/ppermute | solution.py:321
  10.0 18.5 %copy-start.1 = (f32[4,3]{1,0:T(4,128)S(1)}, f32[4,3]{1,0:T(4,128)}, u32[]{:S(2)}) copy-start(f32[4,3]{1,0:T(4,128)} %t_ref.1) | copy-start | bytes 148
  10.0 12.7 %collective-permute-start.3 = (f32[80,1152]{1,0:T(8,128)S(1)}, f32[80,1152]{1,0:T(8,128)S(1)}, u32[]{:S(2)}, u32[]{:S(2)}) collective-permute-start(f32[80,1152]{1,0:T(8,128)S(1)} %get-tuple-element.32.own_ref), channel_id=1, source_target_pairs={{0,16},{16,0},{32,48},{48,32},{64,80},{80,64},{96,112},{112,96},{1... | collective-permute-start | bytes 1105928 | tf_op jit(solution)/shard_map/ppermute | solution.py:321
  12.8 15.8 %collective-permute-start.2 = (f32[80,1152]{1,0:T(8,128)S(1)}, f32[80,1152]{1,0:T(8,128)S(1)}, u32[]{:S(2)}, u32[]{:S(2)}) collective-permute-start(f32[80,1152]{1,0:T(8,128)S(1)} %get-tuple-element.32.own_ref), channel_id=1, source_target_pairs={{16,32},{32,16},{48,64},{64,48},{80,96},{96,80},{112,128},{128,112... | collective-permute-start | bytes 1105928 | tf_op jit(solution)/shard_map/ppermute | solution.py:322
  32.4 10.1 %collective-permute-start.4 = (f32[24,1280]{1,0:T(8,128)S(1)}, f32[24,1280]{1,0:T(8,128)S(1)}, u32[]{:S(2)}, u32[]{:S(2)}) collective-permute-start(f32[24,1280]{1,0:T(8,128)S(1)} %get-tuple-element.34), channel_id=1, source_target_pairs={{16,32},{32,16},{48,64},{64,48},{80,96},{96,80},{112,128},{128,112... | collective-permute-start | bytes 368648 | tf_op jit(solution)/shard_map/ppermute | solution.py:322
  37.7 6.8 %collective-permute-start.5 = (f32[24,1280]{1,0:T(8,128)S(1)}, f32[24,1280]{1,0:T(8,128)S(1)}, u32[]{:S(2)}, u32[]{:S(2)}) collective-permute-start(f32[24,1280]{1,0:T(8,128)S(1)} %get-tuple-element.35), channel_id=1, source_target_pairs={{0,16},{16,0},{32,48},{48,32},{64,80},{80,64},{96,112},{112,96},{1... | collective-permute-start | bytes 368648 | tf_op jit(solution)/shard_map/ppermute | solution.py:321

commit v2 on v1

--- a/solution.py
+++ b/solution.py
@@ -19,12 +19,12 @@
 ROWS, COLS = 64, 2048
 WIDE = (1152, 640, 384, 256)
 EDGE = (64, 32, 16, 8)
-TALL = (96, 48, 24, 16)
+TALL = (96, 48, 24, 12)
 OWN = (32, 16, 8, 4)
 
 
 def soften(coeffs, limit):
-    return coeffs - jnp.clip(coeffs, -limit, limit)
+    return coeffs - jnp.minimum(jnp.maximum(coeffs, -limit), limit)
 
 
 def patch(shifted, source, axis, index, flag):
@@ -137,7 +137,10 @@
         copy.wait()
 
 
-def inner_kernel(x_ref, e_ref, o_ref, edge_ref):
+def inner_kernel(t_ref, x_ref, e_ref, o_ref, edge_ref, limit_ref):
+    for level in range(LEVELS):
+        for kind in range(3):
+            limit_ref[3 * level + kind : 3 * level + kind + 1, :] = jnp.full((1, 128), t_ref[level, kind])
     matrix = pairing(False)
     for k in range(7):
         both = permuted(x_ref[:, 256 * k + 128 : 256 * k + 384], matrix)
@@ -147,7 +150,9 @@
     edge_ref[:, 128:] = x_ref[:, COLS - 128 :]
 
 
-def columns_kernel(e_ref, o_ref, edge_ref, odd_ref, even_ref, send_ref, high_ref):
+def columns_kernel(
+    e_ref, o_ref, edge_ref, odd_ref, even_ref, for_even, for_odd, low_ref, high_ref, low_low_ref, low_high_ref
+):
     is_even, at_start, at_end = ends("cols")
     matrix = pairing(False)
     left = jnp.where(is_even, odd_ref[...], even_ref[...])
@@ -160,27 +165,60 @@
         jnp.concatenate([first[:, 128:], o_ref[...], last[:, 128:]], 1),
         near,
     )
-    send_ref[0:64, :] = low
-    high_ref[...] = high
-    send_ref[64:72, :] = high[0:8]
-    send_ref[72:80, :] = high[56:64]
-
-
-def forward_kernel(t_ref, own_ref, high_ref, odd_ref, even_ref, pack_even, pack_odd, *rest):
-    outs, (l_ref, h_ref, b_ref, e_ref, o_ref) = rest[:13], rest[13:]
+    spread(low_ref, slice(None), low)
+    spread(high_ref, slice(None), high)
+    wide = WIDE[1]
+    low = jnp.concatenate([low, jnp.zeros((ROWS, 2 * wide - WIDE[0]), jnp.float32)], 1)
+    both = [permuted(low[:, 256 * k : 256 * k + 256], matrix) for k in range(wide // 128)]
+    low, high = forward_lift(
+        jnp.concatenate([x[:, :128] for x in both], 1),
+        jnp.concatenate([x[:, 128:] for x in both], 1),
+        neighbours(1, EDGE[1], 512, at_start, at_end),
+    )
+    spread(low_low_ref, slice(None), low)
+    spread(low_high_ref, slice(None), high)
+    below = ends("rows")[0].astype(jnp.int32)
+    for pack, last in ((for_even, below), (for_odd, 1 - below)):
+        for t in range(wide // 128):
+            pack[t, 0:60] = low_low_ref[t, pl.ds(4 * last, 60)]
+            pack[t, 60:72] = low_high_ref[t, pl.ds(52 * last, 12)]
+        for j in range(18):
+            source = low_ref if j < 9 else high_ref
+            t, row = edge_place(j)
+            pack[t, row : row + 4] = source[j % 9, pl.ds(60 * last, 4)]
+
+
+def edge_place(j):
+    return j // 4, 72 + 4 * (j % 4)
+
+
+def forward_kernel(
+    limit_ref, own_low, own_high, own_low_low, own_low_high, odd_ref, even_ref, pack_even, pack_odd, *rest
+):
+    outs, (l_ref, h_ref, ll_ref, lh_ref, b_ref, e_ref, o_ref) = rest[:13], rest[13:]
     is_even, at_start, at_end = ends("rows")
     _, left_end, right_end = ends("cols")
     matrix = pairing(False)
 
-    def gather(t, s):
-        l_ref[t, 0:64] = jnp.where(is_even, odd_ref[0:64, s], even_ref[0:64, s])
-        l_ref[t, 64:128] = own_ref[0:64, s]
-        l_ref[t, 128:192] = jnp.where(is_even, even_ref[0:64, s], odd_ref[0:64, s])
-        h_ref[t, 8:16] = jnp.where(is_even, odd_ref[72:80, s], even_ref[72:80, s])
-        h_ref[t, 16:80] = high_ref[:, s]
-        h_ref[t, 80:88] = jnp.where(is_even, even_ref[64:72, s], odd_ref[64:72, s])
-
-    tiles(WIDE[0], gather)
+    def above(t, rows):
+        return jnp.where(is_even, odd_ref[t, rows], even_ref[t, rows])
+
+    def under(t, rows):
+        return jnp.where(is_even, even_ref[t, rows], odd_ref[t, rows])
+
+    for t in range(WIDE[1] // 128):
+        ll_ref[t, 4:64] = above(t, slice(0, 60))
+        ll_ref[t, 64:128] = own_low_low[t]
+        ll_ref[t, 128:188] = under(t, slice(0, 60))
+        lh_ref[t, 4:16] = above(t, slice(60, 72))
+        lh_ref[t, 16:80] = own_low_high[t]
+        lh_ref[t, 80:92] = under(t, slice(60, 72))
+    for j in range(18):
+        target, own = (l_ref, own_low) if j < 9 else (h_ref, own_high)
+        t, row = edge_place(j)
+        target[j % 9, 12:16] = above(t, slice(row, row + 4))
+        target[j % 9, 16:80] = own[j % 9]
+        target[j % 9, 80:84] = under(t, slice(row, row + 4))
 
     def share(level, kind, s, coeffs):
         own = OWN[level]
@@ -195,52 +233,57 @@
         pack_even[at : at + edge, lanes] = jnp.where(is_even, last, first)
         pack_odd[at : at + edge, lanes] = jnp.where(is_even, first, last)
 
-    for level in range(LEVELS):
-        tall, own = TALL[level], OWN[level]
-        begin = (32, 16, 8, 4)[level]
+    def lifted(ref, t, tall, begin, own):
         near = neighbours(0, begin, own, at_start, at_end)
-        h_tall, h_begin = (48, 8) if level == 0 else (tall, begin)
-        h_near = neighbours(0, h_begin, own, at_start, at_end)
-
-        def lift_low(t, s, level=level, tall=tall, own=own, begin=begin, near=near):
-            low, high = forward_lift(
-                l_ref[t, pl.ds(0, tall, stride=2)], l_ref[t, pl.ds(1, tall, stride=2)], near
+        return forward_lift(ref[t, pl.ds(0, tall, stride=2)], ref[t, pl.ds(1, tall, stride=2)], near)
+
+    def lift_low(t, s, level, tall, begin):
+        own = OWN[level]
+        low, high = lifted(l_ref, t, tall, begin, own)
+        share(level, 1, s, soften(high[begin : begin + own], limit_ref[3 * level + 1 : 3 * level + 2, :]))
+        if level == LEVELS - 1:
+            share(level, 3, s, low[begin : begin + own])
+        elif level:
+            b_ref[0:tall, s] = low
+
+    def lift_high(t, s, level, tall, begin):
+        own = OWN[level]
+        low, high = lifted(h_ref, t, tall, begin, own)
+        share(level, 0, s, soften(low[begin : begin + own], limit_ref[3 * level + 0 : 3 * level + 1, :]))
+        share(level, 2, s, soften(high[begin : begin + own], limit_ref[3 * level + 2 : 3 * level + 3, :]))
+
+    def lift_both(level, low_tall, low_begin, high_tall, high_begin):
+        tiles(WIDE[level], lambda t, s: lift_low(t, s, level, low_tall, low_begin))
+        tiles(WIDE[level], lambda t, s: lift_high(t, s, level, high_tall, high_begin))
+
+    lift_both(0, 48, 8, 48, 8)
+
+    def lift_next(t, s):
+        l_ref[t] = lifted(ll_ref, t, 96, 32, 32)[0]
+        h_ref[t, 0:48] = lifted(lh_ref, t, 48, 8, 32)[0]
+
+    tiles(WIDE[1], lift_next)
+    lift_both(1, 48, 16, 24, 4)
+    for level in (2, 3):
+        tall, begin = TALL[level], OWN[level]
+        rows = max(2 * tall, 32)
+        if 2 * tall < rows:
+            b_ref[2 * tall : rows, : WIDE[level - 1]] = jnp.zeros(
+                (rows - 2 * tall, WIDE[level - 1]), jnp.float32
             )
-            share(level, 1, s, soften(high[begin : begin + own], t_ref[level, 1]))
-            if level < LEVELS - 1:
-                b_ref[0:tall, s] = low
-            else:
-                share(level, 3, s, low[begin : begin + own])
-
-        def lift_high(t, s, level=level, own=own, tall=h_tall, begin=h_begin, near=h_near):
-            low, high = forward_lift(
-                h_ref[t, pl.ds(0, tall, stride=2)], h_ref[t, pl.ds(1, tall, stride=2)], near
-            )
-            share(level, 0, s, soften(low[begin : begin + own], t_ref[level, 0]))
-            share(level, 2, s, soften(high[begin : begin + own], t_ref[level, 2]))
-
-        tiles(WIDE[level], lift_low)
-        tiles(WIDE[level], lift_high)
-        if level == LEVELS - 1:
-            break
-        rows = max(tall, 32)
-        if tall < rows:
-            b_ref[tall:rows, : WIDE[level]] = jnp.zeros((rows - tall, WIDE[level]), jnp.float32)
-        wide = WIDE[level + 1]
-        if 2 * wide > WIDE[level]:
-            b_ref[0:rows, WIDE[level] : 2 * wide] = jnp.zeros((rows, 2 * wide - WIDE[level]), jnp.float32)
+        wide = WIDE[level]
+        b_ref[0:rows, WIDE[level - 1] : 2 * wide] = jnp.zeros(
+            (rows, 2 * wide - WIDE[level - 1]), jnp.float32
+        )
         for k in range(wide // 128):
             both = permuted(b_ref[0:rows, 256 * k : 256 * k + 256], matrix)
             e_ref[0:rows, 128 * k : 128 * k + 128] = both[:, :128]
             o_ref[0:rows, 128 * k : 128 * k + 128] = both[:, 128:]
-        along = neighbours(1, EDGE[level + 1], 1024 >> (level + 1), left_end, right_end)
-
-        def lift_across(g, wide=wide, along=along):
-            low, high = forward_lift(e_ref[g, :wide], o_ref[g, :wide], along)
-            spread(l_ref, g, low)
-            spread(h_ref, g, high)
-
-        row_groups(rows, rows, lift_across)
+        along = neighbours(1, EDGE[level], 1024 >> level, left_end, right_end)
+        low, high = forward_lift(e_ref[0:rows, :wide], o_ref[0:rows, :wide], along)
+        spread(l_ref, slice(0, rows), low)
+        spread(h_ref, slice(0, rows), high)
+        lift_both(level, rows // 2, begin, rows // 2, begin)
 
 
 def inverse_kernel(odd_ref, even_ref, *rest):
@@ -354,33 +397,43 @@
         space=pltpu.HBM,
     )
     odd, even = exchange(for_even, for_odd, "cols")
-    inner = call(
+    *inner, limits = call(
         inner_kernel,
-        (f32(ROWS, 896), f32(ROWS, 896), f32(ROWS, 256)),
+        (f32(ROWS, 896), f32(ROWS, 896), f32(ROWS, 256), f32(16, 128)),
         [],
+        thresholds,
         micrograph,
+        scalars=1,
         cost=pl.CostEstimate(flops=2 * 10**9, bytes_accessed=4 * 10**6, transcendentals=0),
     )
-    block, high = call(columns_kernel, (f32(80, 1152), f32(64, 1152)), [], *inner, odd, even)
-    odd, even = exchange(block, block, "rows")
+    for_even, for_odd, *own = call(
+        columns_kernel,
+        (f32(5, 88, 128), f32(5, 88, 128))
+        + (f32(9, ROWS, 128), f32(9, ROWS, 128), f32(5, ROWS, 128), f32(5, ROWS, 128)),
+        [],
+        *inner,
+        odd,
+        even,
+    )
+    odd, even = exchange(for_even, for_odd, "rows")
     shapes = [f32(OWN[level] + 8, WIDE[level]) for level in range(LEVELS) for _ in range(3)]
     shapes.append(shapes[-1])
     pack_even, pack_odd, *bands = call(
         forward_kernel,
         (f32(24, 1280), f32(24, 1280), *shapes),
         [
-            scratch(9, 192, 128),
             scratch(9, 96, 128),
-            scratch(96, 1280),
-            scratch(96, 640),
-            scratch(96, 640),
+            scratch(9, 96, 128),
+            scratch(5, 192, 128),
+            scratch(5, 96, 128),
+            scratch(48, 768),
+            scratch(48, 384),
+            scratch(48, 384),
         ],
-        thresholds,
-        block,
-        high,
+        limits,
+        *own,
         odd,
         even,
-        scalars=1,
     )
     odd, even = exchange(pack_even, pack_odd, "rows")
     return call(

time: 49 us -> 43.3 us (0.88)
  the two profiles are of different devices: /device:TPU:222 before, /device:TPU:224 now
where the time goes in v2:
time: 43.3 us; the launch traced here: 43 us
  starting transfers between devices  21 us (48%)
  waiting for transfers between devices  11.8 us (27%)
  Pallas kernels  9.01 us (21%)
  local copies, waits for them, and re-layouts  1.05 us (2%)
    ppermute x3, starting transfers between devices, exchange(): odd = lax.ppermute(for_odd, axis, swaps(axis, 1))  11.2 us
    ppermute x3, starting transfers between devices, exchange(): even = lax.ppermute(for_even, axis, swaps(axis, 0))  9.75 us
    ppermute x3, waiting for transfers between devices, exchange(): odd = lax.ppermute(for_odd, axis, swaps(axis, 1))  9.58 us
    pallas_call x5, Pallas kernels, call(): pl.pallas_call(kernel, out_shape=outs, in_specs=[smem] * scalars + [pl.Bl...  9.01 us
    ppermute x3, waiting for transfers between devices, exchange(): even = lax.ppermute(for_even, axis, swaps(axis, 0))  2.26 us
    unnamed x6, local copies, waits for them, and re-layouts  1.05 us
  transfers between devices with their start and end apart: 6, of which 4 were waited for; matrix products, arithmetic and copies ran while one was open for 0% of the time, Pallas kernels for 2%

profile of v2, /device:TPU:224, one launch (start us, length us, event | category | flops | bytes accessed | tf_op | source)
XLA Modules:
  0.0 43.0 jit_solution(16124346754151820371)
XLA Ops:
  0.0 0.0 copy-start
  0.0 1.0 %copy-done = f32[64,2048]{1,0:T(8,128)S(1)} copy-done((f32[64,2048]{1,0:T(8,128)S(1)}, f32[64,2048]{1,0:T(8,128)}, u32[]{:S(2)}) %copy-start) | copy-done | bytes 524312
  1.0 0.0 copy-start.1
  1.1 0.0 copy-start.2
  1.1 2.1 %collective-permute-start = (f32[64,128]{1,0:T(8,128)S(1)}, f32[64,128]{1,0:T(8,128)S(1)}, u32[]{:S(2)}, u32[]{:S(2)}) collective-permute-start(f32[64,128]{1,0:T(8,128)S(1)} %get-tuple-element.36), channel_id=1, source_target_pairs={{1,2},{2,1},{3,4},{4,3},{5,6},{6,5},{7,8},{8,7},{9,10},{10,9},{11,... | collective-permute-start | bytes 98312 | tf_op jit(solution)/shard_map/ppermute | solution.py:365
  3.2 5.6 %collective-permute-start.1 = (f32[64,128]{1,0:T(8,128)S(1)}, f32[64,128]{1,0:T(8,128)S(1)}, u32[]{:S(2)}, u32[]{:S(2)}) collective-permute-start(f32[64,128]{1,0:T(8,128)S(1)} %get-tuple-element.37), channel_id=1, source_target_pairs={{0,1},{1,0},{2,3},{3,2},{4,5},{5,4},{6,7},{7,6},{8,9},{9,8},{10,11... | collective-permute-start | bytes 98312 | tf_op jit(solution)/shard_map/ppermute | solution.py:364
  8.8 0.0 copy-done.1
  8.8 0.0 copy-done.2
  8.8 0.9 %shard_map.28 = (f32[64,896]{1,0:T(8,128)S(1)}, f32[64,896]{1,0:T(8,128)S(1)}, f32[64,256]{1,0:T(8,128)S(1)}, f32[16,128]{1,0:T(8,128)S(1)}) custom-call(f32[4,3]{1,0:T(4,128)S(1)} %copy-done.2, f32[64,2048]{1,0:T(8,128)S(1)} %copy-done.1), custom_call_target="tpu_custom_call" | custom-call | flops 2000000000 | bytes 4000000 | tf_op jit(solution)/shard_map/pallas_call | solution.py:380
  9.7 0.0 collective-permute-done.odd_ref
  9.7 0.0 collective-permute-done.1.even_ref
  9.7 1.3 %shard_map.30 = (f32[5,88,128]{2,1,0:T(8,128)S(1)}, f32[5,88,128]{2,1,0:T(8,128)S(1)}, f32[9,64,128]{2,1,0:T(8,128)S(1)}, f32[9,64,128]{2,1,0:T(8,128)S(1)}, f32...) custom-call(f32[64,896]{1,0:T(8,128)S(1)} %get-tuple-element.33.e_ref, f32[64,896]{1,0:T(8,128)S(1)} %get-tuple-element.34.o_ref, ...), custom_call_target="tpu_custom_call" | custom-call | tf_op jit(solution)/shard_map/pallas_call | solution.py:380
  11.0 4.6 %collective-permute-start.2 = (f32[5,88,128]{2,1,0:T(8,128)S(1)}, f32[5,88,128]{2,1,0:T(8,128)S(1)}, u32[]{:S(2)}, u32[]{:S(2)}) collective-permute-start(f32[5,88,128]{2,1,0:T(8,128)S(1)} %get-tuple-element.42), channel_id=1, source_target_pairs={{16,32},{32,16},{48,64},{64,48},{80,96},{96,80},{112,128},{128,112... | collective-permute-start | bytes 675848 | tf_op jit(solution)/shard_map/ppermute | solution.py:365
  15.6 2.2 %collective-permute-start.3 = (f32[5,88,128]{2,1,0:T(8,128)S(1)}, f32[5,88,128]{2,1,0:T(8,128)S(1)}, u32[]{:S(2)}, u32[]{:S(2)}) collective-permute-start(f32[5,88,128]{2,1,0:T(8,128)S(1)} %get-tuple-element.43), channel_id=1, source_target_pairs={{0,16},{16,0},{32,48},{48,32},{64,80},{80,64},{96,112},{112,96},{1... | collective-permute-start | bytes 675848 | tf_op jit(solution)/shard_map/ppermute | solution.py:364
  17.8 6.0 %collective-permute-done.2.odd_ref = f32[5,88,128]{2,1,0:T(8,128)S(1)} collective-permute-done((f32[5,88,128]{2,1,0:T(8,128)S(1)}, f32[5,88,128]{2,1,0:T(8,128)S(1)}, u32[]{:S(2)}, u32[]{:S(2)}) %collective-permute-start.2) | collective-permute-done | bytes 225312 | tf_op jit(solution)/shard_map/ppermute | solution.py:365
  23.8 1.0 %collective-permute-done.3.even_ref = f32[5,88,128]{2,1,0:T(8,128)S(1)} collective-permute-done((f32[5,88,128]{2,1,0:T(8,128)S(1)}, f32[5,88,128]{2,1,0:T(8,128)S(1)}, u32[]{:S(2)}, u32[]{:S(2)}) %collective-permute-start.3) | collective-permute-done | bytes 225312 | tf_op jit(solution)/shard_map/ppermute | solution.py:364
  24.8 2.5 %shard_map.31 = (f32[24,1280]{1,0:T(8,128)S(1)}, f32[24,1280]{1,0:T(8,128)S(1)}, f32[40,1152]{1,0:T(8,128)S(1)}, f32[40,1152]{1,0:T(8,128)S(1)}, f32[40,1152]{1,...) custom-call(f32[16,128]{1,0:T(8,128)S(1)} %get-tuple-element.32.limi, ...), custom_call_target="tpu_custom_call" | custom-call | tf_op jit(solution)/shard_map/pallas_call | solution.py:380
  27.3 4.6 %collective-permute-start.4 = (f32[24,1280]{1,0:T(8,128)S(1)}, f32[24,1280]{1,0:T(8,128)S(1)}, u32[]{:S(2)}, u32[]{:S(2)}) collective-permute-start(f32[24,1280]{1,0:T(8,128)S(1)} %get-tuple-element.44), channel_id=1, source_target_pairs={{16,32},{32,16},{48,64},{64,48},{80,96},{96,80},{112,128},{128,112... | collective-permute-start | bytes 368648 | tf_op jit(solution)/shard_map/ppermute | solution.py:365
  32.0 1.9 %collective-permute-start.5 = (f32[24,1280]{1,0:T(8,128)S(1)}, f32[24,1280]{1,0:T(8,128)S(1)}, u32[]{:S(2)}, u32[]{:S(2)}) collective-permute-start(f32[24,1280]{1,0:T(8,128)S(1)} %get-tuple-element.45), channel_id=1, source_target_pairs={{0,16},{16,0},{32,48},{48,32},{64,80},{80,64},{96,112},{112,96},{1... | collective-permute-start | bytes 368648 | tf_op jit(solution)/shard_map/ppermute | solution.py:364
  33.9 3.5 %collective-permute-done.4.odd_ref = f32[24,1280]{1,0:T(8,128)S(1)} collective-permute-done((f32[24,1280]{1,0:T(8,128)S(1)}, f32[24,1280]{1,0:T(8,128)S(1)}, u32[]{:S(2)}, u32[]{:S(2)}) %collective-permute-start.4) | collective-permute-done | bytes 122912 | tf_op jit(solution)/shard_map/ppermute | solution.py:365
  37.4 1.3 %collective-permute-done.5.even_ref = f32[24,1280]{1,0:T(8,128)S(1)} collective-permute-done((f32[24,1280]{1,0:T(8,128)S(1)}, f32[24,1280]{1,0:T(8,128)S(1)}, u32[]{:S(2)}, u32[]{:S(2)}) %collective-permute-start.5) | collective-permute-done | bytes 122912 | tf_op jit(solution)/shard_map/ppermute | solution.py:364
  38.7 4.3 %shard_map.32 = f32[64,2048]{1,0:T(8,128)} custom-call(f32[24,1280]{1,0:T(8,128)S(1)} %collective-permute-done.4.odd_ref, f32[24,1280]{1,0:T(8,128)S(1)} %collective-permute-done.5.even_ref, f32[40,1152]{1,0:T(8,128)S(1)} %get-tuple-element.46.rest_0_, f32[40,1152]{1,0:T(8,128)S(1)} %get-tuple-element.47.rest_1_, f32[40,1152]{1,0:T(8,128)S(1)} %get-tuple-element.48.rest_2_, ...), custom_call_target="tpu_custom_call" | custom-call | tf_op jit(solution)/shard_map/pallas_call | solution.py:380
  (1 shorter events, 0.0 us)
Async XLA Ops:
  0.0 1.0 %copy-start = (f32[64,2048]{1,0:T(8,128)S(1)}, f32[64,2048]{1,0:T(8,128)}, u32[]{:S(2)}) copy-start(f32[64,2048]{1,0:T(8,128)} %x_ref.3) | copy-start | bytes 1572868
  1.0 7.7 %copy-start.1 = (f32[64,2048]{1,0:T(8,128)S(1)}, f32[64,2048]{1,0:T(8,128)}, u32[]{:S(2)}) copy-start(f32[64,2048]{1,0:T(8,128)} %x_ref.3) | copy-start | bytes 1572868
  1.1 7.7 %copy-start.2 = (f32[4,3]{1,0:T(4,128)S(1)}, f32[4,3]{1,0:T(4,128)}, u32[]{:S(2)}) copy-start(f32[4,3]{1,0:T(4,128)} %t_ref.1) | copy-start | bytes 148
  1.1 8.6 %collective-permute-start = (f32[64,128]{1,0:T(8,128)S(1)}, f32[64,128]{1,0:T(8,128)S(1)}, u32[]{:S(2)}, u32[]{:S(2)}) collective-permute-start(f32[64,128]{1,0:T(8,128)S(1)} %get-tuple-element.36), channel_id=1, source_target_pairs={{1,2},{2,1},{3,4},{4,3},{5,6},{6,5},{7,8},{8,7},{9,10},{10,9},{11,... | collective-permute-start | bytes 98312 | tf_op jit(solution)/shard_map/ppermute | solution.py:365
  3.2 6.6 %collective-permute-start.1 = (f32[64,128]{1,0:T(8,128)S(1)}, f32[64,128]{1,0:T(8,128)S(1)}, u32[]{:S(2)}, u32[]{:S(2)}) collective-permute-start(f32[64,128]{1,0:T(8,128)S(1)} %get-tuple-element.37), channel_id=1, source_target_pairs={{0,1},{1,0},{2,3},{3,2},{4,5},{5,4},{6,7},{7,6},{8,9},{9,8},{10,11... | collective-permute-start | bytes 98312 | tf_op jit(solution)/shard_map/ppermute | solution.py:364
  11.0 12.8 %collective-permute-start.2 = (f32[5,88,128]{2,1,0:T(8,128)S(1)}, f32[5,88,128]{2,1,0:T(8,128)S(1)}, u32[]{:S(2)}, u32[]{:S(2)}) collective-permute-start(f32[5,88,128]{2,1,0:T(8,128)S(1)} %get-tuple-element.42), channel_id=1, source_target_pairs={{16,32},{32,16},{48,64},{64,48},{80,96},{96,80},{112,128},{128,112... | collective-permute-start | bytes 675848 | tf_op jit(solution)/shard_map/ppermute | solution.py:365
  15.6 9.2 %collective-permute-start.3 = (f32[5,88,128]{2,1,0:T(8,128)S(1)}, f32[5,88,128]{2,1,0:T(8,128)S(1)}, u32[]{:S(2)}, u32[]{:S(2)}) collective-permute-start(f32[5,88,128]{2,1,0:T(8,128)S(1)} %get-tuple-element.43), channel_id=1, source_target_pairs={{0,16},{16,0},{32,48},{48,32},{64,80},{80,64},{96,112},{112,96},{1... | collective-permute-start | bytes 675848 | tf_op jit(solution)/shard_map/ppermute | solution.py:364
  27.3 10.1 %collective-permute-start.4 = (f32[24,1280]{1,0:T(8,128)S(1)}, f32[24,1280]{1,0:T(8,128)S(1)}, u32[]{:S(2)}, u32[]{:S(2)}) collective-permute-start(f32[24,1280]{1,0:T(8,128)S(1)} %get-tuple-element.44), channel_id=1, source_target_pairs={{16,32},{32,16},{48,64},{64,48},{80,96},{96,80},{112,128},{128,112... | collective-permute-start | bytes 368648 | tf_op jit(solution)/shard_map/ppermute | solution.py:365
  32.0 6.8 %collective-permute-start.5 = (f32[24,1280]{1,0:T(8,128)S(1)}, f32[24,1280]{1,0:T(8,128)S(1)}, u32[]{:S(2)}, u32[]{:S(2)}) collective-permute-start(f32[24,1280]{1,0:T(8,128)S(1)} %get-tuple-element.45), channel_id=1, source_target_pairs={{0,16},{16,0},{32,48},{48,32},{64,80},{80,64},{96,112},{112,96},{1... | collective-permute-start | bytes 368648 | tf_op jit(solution)/shard_map/ppermute | solution.py:364

commit v3 on v2

v3 whole, which is shorter than its diff:
```python
import functools

import jax
import jax.numpy as jnp
from jax import lax
from jax.experimental import pallas as pl
from jax.experimental.pallas import tpu as pltpu
from jax.sharding import PartitionSpec as P

LEVELS = 4

step_one = -1.586134342
step_two = -0.05298011854
step_three = 0.8829110762
step_four = 0.4435068522
band_gain = 1.149604398
inv_gain = 1.0 / band_gain

ROWS, COLS = 64, 2048
WIDE = (1152, 640, 384, 256)
EDGE = (64, 32, 16, 8)
OWN = (32, 16, 8, 4)


STEPS_FROM = 1152
GROUP = 64
MATRIX_FROM = 640


def combined(*terms):
    total = {}
    for factor, taps, moved in terms:
        for (sequence, offset), tap in taps.items():
            key = (sequence, offset + moved)
            total[key] = total.get(key, 0.0) + factor * tap
    return total


def lifted_taps(inverse):
    even, odd = {("even", 0): 1.0}, {("odd", 0): 1.0}
    if inverse:
        even, odd = combined((1.0 / band_gain, even, 0)), combined((band_gain, odd, 0))
        for to_even, to_odd in ((step_four, step_three), (step_two, step_one)):
            even = combined((1.0, even, 0), (-to_even, odd, 0), (-to_even, odd, -1))
            odd = combined((1.0, odd, 0), (-to_odd, even, 0), (-to_odd, even, 1))
        return even, odd
    for to_odd, to_even in ((step_one, step_two), (step_three, step_four)):
        odd = combined((1.0, odd, 0), (to_odd, even, 0), (to_odd, even, 1))
        even = combined((1.0, even, 0), (to_even, odd, 0), (to_even, odd, -1))
    return combined((band_gain, even, 0)), combined((1.0 / band_gain, odd, 0))


def lift_lanes(even, odd, first, count, at_start, at_end, inverse=False):
    rows, width = even.shape
    if width >= STEPS_FROM:
        near = neighbours(1, first, count, at_start, at_end)
        lift = inverse_lift if inverse else forward_lift
        groups = [slice(k, min(k + GROUP, rows)) for k in range(0, rows, GROUP)]
        parts = [lift(even[g], odd[g], near) for g in groups]
        return [jnp.concatenate(x, 0) if len(x) > 1 else x[0] for x in zip(*parts)]
    last = first + count - 1
    e, o = {0: even}, {0: odd}
    for x in (e, o):
        width = x[0].shape[1]
        for offset in (-2, -1, 1, 2):
            x[offset] = pltpu.roll(x[0], -offset % width, 1)
    fixed = lambda x, source, lane, flag: patch(x, source, 1, lane, flag)
    ends_of = {
        ("even", -1): [(e[1], first, at_start)],
        ("even", -2): [(e[2], first, at_start), (e[0], first + 1, at_start)],
        ("even", 1): [(e[0], last, at_end)],
        ("even", 2): [(e[-1], last, at_end), (e[1], last - 1, at_end)],
        ("odd", -1): [(o[0], first, at_start)],
        ("odd", -2): [(o[1], first, at_start), (o[-1], first + 1, at_start)],
        ("odd", 1): [(o[-1], last, at_end)],
        ("odd", 2): [(o[-2], last, at_end), (o[0], last - 1, at_end)],
    }
    shifted = {("even", 0): even, ("odd", 0): odd}
    for (sequence, offset), patches in ends_of.items():
        x = (e if sequence == "even" else o)[offset]
        for patch_of in patches:
            x = fixed(x, *patch_of)
        shifted[sequence, offset] = x
    out = []
    for taps in lifted_taps(inverse):
        by_tap = {}
        for key, tap in sorted(taps.items()):
            by_tap.setdefault(round(tap, 9), []).append((tap, shifted[key]))
        total = None
        for group in by_tap.values():
            term = sum((x for _, x in group[1:]), group[0][1]) * group[0][0]
            total = term if total is None else total + term
        out.append(total)
    return out


def soften(coeffs, limit):
    return coeffs - jnp.minimum(jnp.maximum(coeffs, -limit), limit)


def patch(shifted, source, axis, index, flag):
    unit = 8 if axis == 0 else 128
    lo = index // unit * unit
    hi = min(lo + unit, shifted.shape[axis])
    cut = functools.partial(lax.slice_in_dim, axis=axis)
    tile = cut(shifted, lo, hi)
    here = (lax.broadcasted_iota(jnp.int32, tile.shape, axis) == index - lo) & flag
    tile = jnp.where(here, cut(source, lo, hi), tile)
    parts = [cut(shifted, 0, lo)] if lo else []
    parts.append(tile)
    if hi < shifted.shape[axis]:
        parts.append(cut(shifted, hi, shifted.shape[axis]))
    return jnp.concatenate(parts, axis) if len(parts) > 1 else tile


def neighbours(axis, first, count, at_start, at_end):
    def before(odd):
        return patch(pltpu.roll(odd, 1, axis), odd, axis, first, at_start)

    def after(even):
        rolled = pltpu.roll(even, even.shape[axis] - 1, axis)
        return patch(rolled, even, axis, first + count - 1, at_end)

    return before, after


def forward_lift(even, odd, near):
    before, after = near
    odd = odd + step_one * (even + after(even))
    even = even + step_two * (before(odd) + odd)
    odd = odd + step_three * (even + after(even))
    even = even + step_four * (before(odd) + odd)
    return even * band_gain, odd * inv_gain


def inverse_lift(low, high, near):
    before, after = near
    even = low * inv_gain
    odd = high * band_gain
    even = even - step_four * (before(odd) + odd)
    odd = odd - step_three * (even + after(even))
    even = even - step_two * (before(odd) + odd)
    odd = odd - step_one * (even + after(even))
    return even, odd


def pairing(transpose):
    a = lax.broadcasted_iota(jnp.int32, (256, 256), 1 if not transpose else 0)
    b = lax.broadcasted_iota(jnp.int32, (256, 256), 0 if not transpose else 1)
    target = jnp.where(a < 128, 2 * a, 2 * a - 255)
    return jnp.where(b == target, 1.0, 0.0).astype(jnp.bfloat16)


def permuted(x, matrix):
    rows = x.shape[0]
    high = x.astype(jnp.bfloat16)
    rest = x - high.astype(jnp.float32)
    middle = rest.astype(jnp.bfloat16)
    last = (rest - middle.astype(jnp.float32)).astype(jnp.bfloat16)
    out = jnp.dot(
        jnp.concatenate([high, middle, last], 0), matrix, preferred_element_type=jnp.float32
    )
    return (out[:rows] + out[rows : 2 * rows]) + out[2 * rows :]


def picked(x, index):
    return jnp.take_along_axis(x, index, axis=1, mode="promise_in_bounds")


def split_pairs(x):
    if x.shape[1] < 2 * MATRIX_FROM:
        return split_by_picks(x)
    matrix = pairing(False)
    both = [permuted(x[:, k : k + 256], matrix) for k in range(0, x.shape[1], 256)]
    return jnp.concatenate([y[:, :128] for y in both], 1), jnp.concatenate([y[:, 128:] for y in both], 1)


def merge_pairs(even, odd):
    if even.shape[1] < MATRIX_FROM:
        return merge_by_picks(even, odd)
    matrix = pairing(True)
    return jnp.concatenate(
        [
            permuted(jnp.concatenate([even[:, k : k + 128], odd[:, k : k + 128]], 1), matrix)
            for k in range(0, even.shape[1], 128)
        ],
        1,
    )


def split_by_picks(x):
    rows = x.shape[0]
    lane = lax.broadcasted_iota(jnp.int32, (rows, 128), 1)
    lower = lane < 64
    near = jnp.where(lower, 2 * lane, 2 * lane - 127)
    far = jnp.where(lower, 2 * lane + 1, 2 * lane - 128)
    evens, odds = [], []
    for k in range(0, x.shape[1], 256):
        first, second = picked(x[:, k : k + 128], near), picked(x[:, k + 128 : k + 256], far)
        evens.append(jnp.where(lower, first, second))
        odds.append(pltpu.roll(jnp.where(lower, second, first), 64, 1))
    return jnp.concatenate(evens, 1), jnp.concatenate(odds, 1)


def merge_by_picks(even, odd):
    rows = even.shape[0]
    lane = lax.broadcasted_iota(jnp.int32, (rows, 128), 1)
    lower = lane < 64
    is_odd = lane % 2 == 1
    half = lane // 2
    near = jnp.where(is_odd, half + 64, half)
    far = jnp.where(is_odd, half, half + 64)
    out = []
    for k in range(0, even.shape[1], 128):
        e, o = even[:, k : k + 128], pltpu.roll(odd[:, k : k + 128], 64, 1)
        out += [picked(jnp.where(lower, e, o), near), picked(jnp.where(lower, o, e), far)]
    return jnp.concatenate(out, 1)


def tiles(width, body):
    def step(t, carry):
        body(t, pl.ds(pl.multiple_of(t * 128, 128), 128))
        return carry

    if width > 640:
        lax.fori_loop(0, width // 128, step, 0)
    else:
        for t in range(width // 128):
            body(t, slice(128 * t, 128 * t + 128))


def joined(ref, rows, width):
    return jnp.concatenate([ref[k, rows] for k in range(width // 128)], 1)


def spread(ref, rows, value):
    for k in range(value.shape[1] // 128):
        ref[k, rows] = value[:, 128 * k : 128 * k + 128]


def ends(axis):
    position = lax.axis_index(axis)
    return position % 2 == 0, position == 0, position == lax.axis_size(axis) - 1


def edges_kernel(x_ref, for_even, for_odd, sems):
    is_even = ends("cols")[0]
    right = jnp.where(is_even, COLS - 128, 0)
    copies = []
    for k, (at, out) in enumerate(((right, for_even), (COLS - 128 - right, for_odd))):
        lanes = pl.ds(pl.multiple_of(at, 128), 128)
        copies.append(pltpu.make_async_copy(x_ref.at[:, lanes], out, sems.at[k]))
        copies[-1].start()
    for copy in copies:
        copy.wait()


def inner_kernel(t_ref, x_ref, e_ref, o_ref, edge_ref, limit_ref):
    for level in range(LEVELS):
        for kind in range(3):
            limit_ref[3 * level + kind : 3 * level + kind + 1, :] = jnp.full((1, 128), t_ref[level, kind])
    e_ref[...], o_ref[...] = split_pairs(x_ref[:, 128 : COLS - 128])
    edge_ref[:, :128] = x_ref[:, :128]
    edge_ref[:, 128:] = x_ref[:, COLS - 128 :]


def columns_kernel(
    e_ref, o_ref, edge_ref, odd_ref, even_ref, for_even, for_odd, low_ref, high_ref, low_low_ref, low_high_ref
):
    is_even, at_start, at_end = ends("cols")
    left = jnp.where(is_even, odd_ref[...], even_ref[...])
    right = jnp.where(is_even, even_ref[...], odd_ref[...])
    first = split_pairs(jnp.concatenate([left, edge_ref[:, :128]], 1))
    last = split_pairs(jnp.concatenate([edge_ref[:, 128:], right], 1))
    low, high = lift_lanes(
        jnp.concatenate([first[0], e_ref[...], last[0]], 1),
        jnp.concatenate([first[1], o_ref[...], last[1]], 1),
        EDGE[0],
        1024,
        at_start,
        at_end,
    )
    spread(low_ref, slice(None), low)
    spread(high_ref, slice(None), high)
    wide = WIDE[1]
    low = jnp.concatenate([low, jnp.zeros((ROWS, 2 * wide - WIDE[0]), jnp.float32)], 1)
    low, high = lift_lanes(*split_pairs(low), EDGE[1], 512, at_start, at_end)
    spread(low_low_ref, slice(None), low)
    spread(low_high_ref, slice(None), high)
    below = ends("rows")[0].astype(jnp.int32)
    for pack, last in ((for_even, below), (for_odd, 1 - below)):
        for t in range(wide // 128):
            pack[t, 0:60] = low_low_ref[t, pl.ds(4 * last, 60)]
            pack[t, 60:72] = low_high_ref[t, pl.ds(52 * last, 12)]
        for j in range(18):
            source = low_ref if j < 9 else high_ref
            t, row = edge_place(j)
            pack[t, row : row + 8] = source[j % 9, pl.ds(56 * last, 8)]


def edge_place(j):
    return j // 4, 72 + 8 * (j % 4)


def edge_at(level, kind, t):
    return 4 * (2 * kind + t) if level == 3 else 32 + 4 * (5 * (kind // 2) + t)


def sides(odd_ref, even_ref):
    is_even = ends("rows")[0]

    def above(*at):
        return jnp.where(is_even, odd_ref[at], even_ref[at])

    def under(*at):
        return jnp.where(is_even, even_ref[at], odd_ref[at])

    return above, under


def lifted(ref, t, tall, begin, own):
    _, at_start, at_end = ends("rows")
    near = neighbours(0, begin, own, at_start, at_end)
    return forward_lift(ref[t, pl.ds(0, tall, stride=2)], ref[t, pl.ds(1, tall, stride=2)], near)


def forward_kernel(limit_ref, own_low, own_high, odd_ref, even_ref, for_even, for_odd, *rest):
    outs, (l_ref, h_ref, ll_ref, lh_ref, b_ref) = rest[:10], rest[10:]
    is_even = ends("rows")[0]
    _, left_end, right_end = ends("cols")
    above, under = sides(odd_ref, even_ref)
    for t in range(WIDE[1] // 128):
        ll_ref[t, 4:64] = above(t, slice(0, 60))
        ll_ref[t, 64:128] = own_low[t]
        ll_ref[t, 128:188] = under(t, slice(0, 60))
        lh_ref[t, 4:16] = above(t, slice(60, 72))
        lh_ref[t, 16:80] = own_high[t]
        lh_ref[t, 80:92] = under(t, slice(60, 72))
        l_ref[t] = lifted(ll_ref, t, 96, 32, 32)[0]
        h_ref[t, 0:48] = lifted(lh_ref, t, 48, 8, 32)[0]

    def limited(coeffs, level, kind):
        if kind == 3:
            return coeffs
        at = 3 * level + kind
        return soften(coeffs, limit_ref[at : at + 1, :])

    def keep(level, kind, t, s, coeffs, begin):
        own = OWN[level]
        coeffs = limited(coeffs[begin - 4 : begin + own + 4], level, kind)
        outs[3 * (level - 1) + kind][:, s] = coeffs
        if level == 3 or (level == 1 and kind != 1):
            first, last = coeffs[4:8], coeffs[own : own + 4]
            at = edge_at(level, kind, t)
            for_even[at : at + 4, :] = jnp.where(is_even, last, first)
            for_odd[at : at + 4, :] = jnp.where(is_even, first, last)

    for level in (1, 2, 3):
        own = OWN[level]
        if level == 1:
            sizes = ((48, 16), (24, 4))
        else:
            rows = (48, 32)[level - 2]
            sizes = ((rows // 2, own),) * 2
            known, wide = WIDE[level - 1], WIDE[level]
            if level == 3:
                b_ref[24:32, :known] = jnp.zeros((8, known), jnp.float32)
            b_ref[0:rows, known : 2 * wide] = jnp.zeros((rows, 2 * wide - known), jnp.float32)
            halves = split_pairs(b_ref[0:rows, : 2 * wide])
            low, high = lift_lanes(*halves, EDGE[level], 1024 >> level, left_end, right_end)
            spread(l_ref, slice(0, rows), low)
            spread(h_ref, slice(0, rows), high)
        for t in range(WIDE[level] // 128):
            s = slice(128 * t, 128 * t + 128)
            low, high = lifted(l_ref, t, *sizes[0], own)
            keep(level, 1, t, s, high, sizes[0][1])
            if level == 3:
                keep(level, 3, t, s, low, sizes[0][1])
            else:
                b_ref[0 : sizes[0][0], s] = low
            low, high = lifted(h_ref, t, *sizes[1], own)
            keep(level, 0, t, s, low, sizes[1][1])
            keep(level, 2, t, s, high, sizes[1][1])


def detail_kernel(limit_ref, own_low, own_high, odd_ref, even_ref, hl_ref, lh_ref, hh_ref, x_ref):
    above, under = sides(odd_ref, even_ref)
    for j in range(18):
        own = own_low if j < 9 else own_high
        t, row = edge_place(j)
        x_ref[j, 0:8] = above(t, slice(row, row + 8))
        x_ref[j, 8:72] = own[j % 9]
        x_ref[j, 72:80] = under(t, slice(row, row + 8))

    def lift(t, s):
        high = lifted(x_ref, t, 40, 4, 32)[1]
        lh_ref[:, s] = soften(high, limit_ref[1:2, :])
        low, high = lifted(x_ref, t + 9, 40, 4, 32)
        hl_ref[:, s] = soften(low, limit_ref[0:1, :])
        hh_ref[:, s] = soften(high, limit_ref[2:3, :])

    tiles(WIDE[0], lift)


def inverse_kernel(odd_ref, even_ref, *rest):
    ins, out_ref, (v_ref, w_ref, r_ref), kept = rest[:13], rest[13], rest[14:17], rest[17:]
    _, at_start, at_end = ends("rows")
    _, left_end, right_end = ends("cols")
    above, under = sides(odd_ref, even_ref)
    for level in range(LEVELS - 1, -1, -1):
        own = OWN[level]
        long = max(own + 8, 16)
        near = neighbours(0, 4, own, at_start, at_end)

        def whole(kind, t, s, level=level, own=own, long=long):
            source = ins[3 * level + kind]
            if level == 2 or level == 0 or (level == 1 and kind == 1):
                return source[0:long, s]
            target, at = kept[kind], slice(edge_at(level, kind, t), edge_at(level, kind, t) + 4)
            target[0 : own + 8, s] = source[:, s]
            target[0:4, s] = above(at)
            target[4 + own : 8 + own, s] = under(at)
            return target[0:long, s]

        def lift_down(t, s, level=level, long=long, near=near, whole=whole):
            low = whole(3, t, s) if level == LEVELS - 1 else r_ref[4 : 4 + long, s]
            even, odd = inverse_lift(low, whole(1, t, s), near)
            v_ref[t, pl.ds(0, long, stride=2)] = even
            v_ref[t, pl.ds(1, long, stride=2)] = odd
            even, odd = inverse_lift(whole(0, t, s), whole(2, t, s), near)
            w_ref[t, pl.ds(0, long, stride=2)] = even
            w_ref[t, pl.ds(1, long, stride=2)] = odd

        wide = WIDE[level]
        tiles(wide, lift_down)
        first, rows = (8, 64) if level == 0 else (0, 2 * long)
        cut = slice(first, first + rows)
        even, odd = joined(v_ref, cut, wide), joined(w_ref, cut, wide)
        both = merge_pairs(
            *lift_lanes(even, odd, EDGE[level], 1024 >> level, left_end, right_end, inverse=True)
        )
        if level:
            r_ref[0:rows, : 2 * wide] = both
        else:
            out_ref[...] = both[:, 128 : 128 + COLS]


def swaps(axis, offset):
    count = lax.axis_size(axis)
    pairs = []
    for i in range(offset, count - 1, 2):
        pairs += [(i, i + 1), (i + 1, i)]
    return pairs


def exchange(for_even, for_odd, axis):
    even = lax.ppermute(for_even, axis, swaps(axis, 0))
    odd = lax.ppermute(for_odd, axis, swaps(axis, 1))
    return odd, even


def f32(*shape):
    return jax.ShapeDtypeStruct(shape, jnp.float32)


def scratch(*shape):
    return pltpu.VMEM(shape, jnp.float32)


def call(kernel, outs, scratches, *args, scalars=0, space=pltpu.VMEM, cost=None):
    vmem = pl.BlockSpec(memory_space=pltpu.VMEM)
    smem = pl.BlockSpec(memory_space=pltpu.SMEM)
    return pl.pallas_call(
        kernel,
        out_shape=outs,
        in_specs=[smem] * scalars + [pl.BlockSpec(memory_space=space)] * (len(args) - scalars),
        out_specs=jax.tree.map(lambda _: vmem, outs),
        scratch_shapes=scratches,
        compiler_params=pltpu.CompilerParams(vmem_limit_bytes=16 * 2**20),
        cost_estimate=cost,
    )(*args)


def local(micrograph, thresholds):
    for_even, for_odd = call(
        edges_kernel,
        (f32(ROWS, 128), f32(ROWS, 128)),
        [pltpu.SemaphoreType.DMA((2,))],
        micrograph,
        space=pltpu.HBM,
    )
    odd, even = exchange(for_even, for_odd, "cols")
    *inner, limits = call(
        inner_kernel,
        (f32(ROWS, 896), f32(ROWS, 896), f32(ROWS, 256), f32(16, 128)),
        [],
        thresholds,
        micrograph,
        scalars=1,
        cost=pl.CostEstimate(flops=2 * 10**9, bytes_accessed=4 * 10**6, transcendentals=0),
    )
    for_even, for_odd, *own = call(
        columns_kernel,
        (f32(5, 104, 128), f32(5, 104, 128))
        + (f32(9, ROWS, 128), f32(9, ROWS, 128), f32(5, ROWS, 128), f32(5, ROWS, 128)),
        [],
        *inner,
        odd,
        even,
    )
    own_low, own_high, own_low_low, own_low_high = own
    odd, even = exchange(for_even, for_odd, "rows")
    shapes = [f32(OWN[level] + 8, WIDE[level]) for level in range(LEVELS) for _ in range(3)]
    shapes.append(shapes[-1])
    for_even, for_odd, *bands = call(
        forward_kernel,
        (f32(72, 128), f32(72, 128), *shapes[3:]),
        [
            scratch(5, 96, 128),
            scratch(5, 96, 128),
            scratch(5, 192, 128),
            scratch(5, 96, 128),
            scratch(48, 768),
        ],
        limits,
        own_low_low,
        own_low_high,
        odd,
        even,
    )
    finest = call(
        detail_kernel,
        tuple(shapes[:3]),
        [scratch(18, 80, 128)],
        limits,
        own_low,
        own_high,
        odd,
        even,
        cost=pl.CostEstimate(flops=2 * 10**9, bytes_accessed=4 * 10**6, transcendentals=0),
    )
    odd, even = exchange(for_even, for_odd, "rows")
    return call(
        inverse_kernel,
        f32(ROWS, COLS),
        [scratch(9, 80, 128), scratch(9, 80, 128), scratch(48, 1280)]
        + [scratch(24, 640), scratch(16, 256), scratch(24, 640), scratch(16, 256)],
        odd,
        even,
        *finest,
        *bands,
    )


def solution(mesh):
    placed = (P("rows", "cols"), P())
    return jax.shard_map(
        local, mesh=mesh, in_specs=placed, out_specs=P("rows", "cols"), check_vma=False
    )
```

time: 43.3 us -> 40.8 us (0.942)
  Pallas kernels: 9.01 us -> 7.04 us
  waiting for transfers between devices: 11.8 us -> 11.3 us
    pallas_call x5 -> x6, Pallas kernels: 9.01 us -> 7.04 us  [call(): pl.pallas_call(kernel, out_shape=outs, in_specs=[smem] * scalars + [pl.Bl...]
    ppermute x3, waiting for transfers between devices: 9.58 us -> 9.09 us  [exchange(): odd = lax.ppermute(for_odd, axis, swaps(axis, 1))]
  transfers between devices with their start and end apart: 6 -> 6, of which waited for: 4 -> 4; matrix products, arithmetic and copies ran while one was open for 0% -> 0% of each run, Pallas kernels for 2% -> 3%
where the time goes in v3:
time: 40.8 us; the launch traced here: 40.5 us
  starting transfers between devices  21 us (51%)
  waiting for transfers between devices  11.3 us (28%)
  Pallas kernels  7.04 us (17%)
  local copies, waits for them, and re-layouts  1.05 us (3%)
    ppermute x3, starting transfers between devices, exchange(): odd = lax.ppermute(for_odd, axis, swaps(axis, 1))  11.2 us
    ppermute x3, starting transfers between devices, exchange(): even = lax.ppermute(for_even, axis, swaps(axis, 0))  9.75 us
    ppermute x3, waiting for transfers between devices, exchange(): odd = lax.ppermute(for_odd, axis, swaps(axis, 1))  9.09 us
    pallas_call x6, Pallas kernels, call(): pl.pallas_call(kernel, out_shape=outs, in_specs=[smem] * scalars + [pl.Bl...  7.04 us
    ppermute x3, waiting for transfers between devices, exchange(): even = lax.ppermute(for_even, axis, swaps(axis, 0))  2.26 us
    unnamed x6, local copies, waits for them, and re-layouts  1.05 us
  transfers between devices with their start and end apart: 6, of which 4 were waited for; matrix products, arithmetic and copies ran while one was open for 0% of the time, Pallas kernels for 3%

profile of v3, /device:TPU:224, one launch (start us, length us, event | category | flops | bytes accessed | tf_op | source)
XLA Modules:
  0.0 40.5 jit_solution(8080436506374184133)
XLA Ops:
  0.0 0.0 copy-start
  0.0 1.0 %copy-done = f32[64,2048]{1,0:T(8,128)S(1)} copy-done((f32[64,2048]{1,0:T(8,128)S(1)}, f32[64,2048]{1,0:T(8,128)}, u32[]{:S(2)}) %copy-start) | copy-done | bytes 524312
  1.0 0.0 copy-start.1
  1.1 0.0 copy-start.2
  1.1 2.1 %collective-permute-start = (f32[64,128]{1,0:T(8,128)S(1)}, f32[64,128]{1,0:T(8,128)S(1)}, u32[]{:S(2)}, u32[]{:S(2)}) collective-permute-start(f32[64,128]{1,0:T(8,128)S(1)} %get-tuple-element.36), channel_id=1, source_target_pairs={{1,2},{2,1},{3,4},{4,3},{5,6},{6,5},{7,8},{8,7},{9,10},{10,9},{11,... | collective-permute-start | bytes 98312 | tf_op jit(solution)/shard_map/ppermute | solution.py:458
  3.2 5.6 %collective-permute-start.1 = (f32[64,128]{1,0:T(8,128)S(1)}, f32[64,128]{1,0:T(8,128)S(1)}, u32[]{:S(2)}, u32[]{:S(2)}) collective-permute-start(f32[64,128]{1,0:T(8,128)S(1)} %get-tuple-element.37), channel_id=1, source_target_pairs={{0,1},{1,0},{2,3},{3,2},{4,5},{5,4},{6,7},{7,6},{8,9},{9,8},{10,11... | collective-permute-start | bytes 98312 | tf_op jit(solution)/shard_map/ppermute | solution.py:457
  8.8 0.0 copy-done.1
  8.8 0.0 copy-done.2
  8.8 0.9 %shard_map.28 = (f32[64,896]{1,0:T(8,128)S(1)}, f32[64,896]{1,0:T(8,128)S(1)}, f32[64,256]{1,0:T(8,128)S(1)}, f32[16,128]{1,0:T(8,128)S(1)}) custom-call(f32[4,3]{1,0:T(4,128)S(1)} %copy-done.2, f32[64,2048]{1,0:T(8,128)S(1)} %copy-done.1), custom_call_target="tpu_custom_call" | custom-call | flops 2000000000 | bytes 4000000 | tf_op jit(solution)/shard_map/pallas_call | solution.py:473
  9.7 0.0 collective-permute-done.odd_ref
  9.7 0.0 collective-permute-done.1.even_ref
  9.7 1.2 %shard_map.30 = (f32[5,104,128]{2,1,0:T(8,128)S(1)}, f32[5,104,128]{2,1,0:T(8,128)S(1)}, f32[9,64,128]{2,1,0:T(8,128)S(1)}, f32[9,64,128]{2,1,0:T(8,128)S(1)}, f...) custom-call(f32[64,896]{1,0:T(8,128)S(1)} %get-tuple-element.33.e_ref, f32[64,896]{1,0:T(8,128)S(1)} %get-tuple-element.34.o_ref, ...), custom_call_target="tpu_custom_call" | custom-call | tf_op jit(solution)/shard_map/pallas_call | solution.py:473
  11.0 4.6 %collective-permute-start.2 = (f32[5,104,128]{2,1,0:T(8,128)S(1)}, f32[5,104,128]{2,1,0:T(8,128)S(1)}, u32[]{:S(2)}, u32[]{:S(2)}) collective-permute-start(f32[5,104,128]{2,1,0:T(8,128)S(1)} %get-tuple-element.40), channel_id=1, source_target_pairs={{16,32},{32,16},{48,64},{64,48},{80,96},{96,80},{112,128},{128,112... | collective-permute-start | bytes 798728 | tf_op jit(solution)/shard_map/ppermute | solution.py:458
  15.5 2.2 %collective-permute-start.3 = (f32[5,104,128]{2,1,0:T(8,128)S(1)}, f32[5,104,128]{2,1,0:T(8,128)S(1)}, u32[]{:S(2)}, u32[]{:S(2)}) collective-permute-start(f32[5,104,128]{2,1,0:T(8,128)S(1)} %get-tuple-element.41), channel_id=1, source_target_pairs={{0,16},{16,0},{32,48},{48,32},{64,80},{80,64},{96,112},{112,96},{1... | collective-permute-start | bytes 798728 | tf_op jit(solution)/shard_map/ppermute | solution.py:457
  17.8 6.9 %collective-permute-done.2.odd_ref = f32[5,104,128]{2,1,0:T(8,128)S(1)} collective-permute-done((f32[5,104,128]{2,1,0:T(8,128)S(1)}, f32[5,104,128]{2,1,0:T(8,128)S(1)}, u32[]{:S(2)}, u32[]{:S(2)}) %collective-permute-start.2) | collective-permute-done | bytes 266272 | tf_op jit(solution)/shard_map/ppermute | solution.py:458
  24.7 1.0 %collective-permute-done.3.even_ref = f32[5,104,128]{2,1,0:T(8,128)S(1)} collective-permute-done((f32[5,104,128]{2,1,0:T(8,128)S(1)}, f32[5,104,128]{2,1,0:T(8,128)S(1)}, u32[]{:S(2)}, u32[]{:S(2)}) %collective-permute-start.3) | collective-permute-done | bytes 266272 | tf_op jit(solution)/shard_map/ppermute | solution.py:457
  25.6 1.1 %shard_map.31 = (f32[72,128]{1,0:T(8,128)S(1)}, f32[72,128]{1,0:T(8,128)S(1)}, f32[24,640]{1,0:T(8,128)S(1)}, f32[24,640]{1,0:T(8,128)S(1)}, f32[24,640]{1,0:T(8...) custom-call(f32[16,128]{1,0:T(8,128)S(1)} %get-tuple-element.32.limi, ...), custom_call_target="tpu_custom_call" | custom-call | tf_op jit(solution)/shard_map/pallas_call | solution.py:473
  26.7 4.6 %collective-permute-start.4 = (f32[72,128]{1,0:T(8,128)S(1)}, f32[72,128]{1,0:T(8,128)S(1)}, u32[]{:S(2)}, u32[]{:S(2)}) collective-permute-start(f32[72,128]{1,0:T(8,128)S(1)} %get-tuple-element.42), channel_id=1, source_target_pairs={{16,32},{32,16},{48,64},{64,48},{80,96},{96,80},{112,128},{128,112... | collective-permute-start | bytes 110600 | tf_op jit(solution)/shard_map/ppermute | solution.py:458
  31.3 1.9 %collective-permute-start.5 = (f32[72,128]{1,0:T(8,128)S(1)}, f32[72,128]{1,0:T(8,128)S(1)}, u32[]{:S(2)}, u32[]{:S(2)}) collective-permute-start(f32[72,128]{1,0:T(8,128)S(1)} %get-tuple-element.43), channel_id=1, source_target_pairs={{0,16},{16,0},{32,48},{48,32},{64,80},{80,64},{96,112},{112,96},{1... | collective-permute-start | bytes 110600 | tf_op jit(solution)/shard_map/ppermute | solution.py:457
  33.3 0.4 %shard_map.32 = (f32[40,1152]{1,0:T(8,128)S(1)}, f32[40,1152]{1,0:T(8,128)S(1)}, f32[40,1152]{1,0:T(8,128)S(1)}) custom-call(f32[16,128]{1,0:T(8,128)S(1)} %get-tuple-element.32.limit_ref, f32[9,64,128]{2,1,0:T(8,128)S(1)} %get-tuple-element.44.own_low, f32[9,64,128]{2,1,0:T(8,128)S(1)} %get-tuple-element.45.own_high, ...), custom_call_target="tpu_custom_call" | custom-call | flops 2000000000 | bytes 4000000 | tf_op jit(solution)/shard_map/pallas_call | solution.py:473
  33.7 2.2 %collective-permute-done.4.odd_ref = f32[72,128]{1,0:T(8,128)S(1)} collective-permute-done((f32[72,128]{1,0:T(8,128)S(1)}, f32[72,128]{1,0:T(8,128)S(1)}, u32[]{:S(2)}, u32[]{:S(2)}) %collective-permute-start.4) | collective-permute-done | bytes 36896 | tf_op jit(solution)/shard_map/ppermute | solution.py:458
  35.9 1.3 %collective-permute-done.5.even_ref = f32[72,128]{1,0:T(8,128)S(1)} collective-permute-done((f32[72,128]{1,0:T(8,128)S(1)}, f32[72,128]{1,0:T(8,128)S(1)}, u32[]{:S(2)}, u32[]{:S(2)}) %collective-permute-start.5) | collective-permute-done | bytes 36896 | tf_op jit(solution)/shard_map/ppermute | solution.py:457
  37.2 3.3 %shard_map.33 = f32[64,2048]{1,0:T(8,128)} custom-call(f32[72,128]{1,0:T(8,128)S(1)} %collective-permute-done.4.odd_ref, f32[72,128]{1,0:T(8,128)S(1)} %collective-permute-done.5.even_ref, f32[40,1152]{1,0:T(8,128)S(1)} %get-tuple-element.46.rest_0_, f32[40,1152]{1,0:T(8,128)S(1)} %get-tuple-element.47.rest_1_, f32[40,1152]{1,0:T(8,128)S(1)} %get-tuple-element.48.rest_2_, ...), custom_call_target="tpu_custom_call" | custom-call | tf_op jit(solution)/shard_map/pallas_call | solution.py:473
  (1 shorter events, 0.0 us)
Async XLA Ops:
  0.0 1.0 %copy-start = (f32[64,2048]{1,0:T(8,128)S(1)}, f32[64,2048]{1,0:T(8,128)}, u32[]{:S(2)}) copy-start(f32[64,2048]{1,0:T(8,128)} %x_ref.3) | copy-start | bytes 1572868
  1.0 7.7 %copy-start.1 = (f32[64,2048]{1,0:T(8,128)S(1)}, f32[64,2048]{1,0:T(8,128)}, u32[]{:S(2)}) copy-start(f32[64,2048]{1,0:T(8,128)} %x_ref.3) | copy-start | bytes 1572868
  1.1 7.7 %copy-start.2 = (f32[4,3]{1,0:T(4,128)S(1)}, f32[4,3]{1,0:T(4,128)}, u32[]{:S(2)}) copy-start(f32[4,3]{1,0:T(4,128)} %t_ref.1) | copy-start | bytes 148
  1.1 8.6 %collective-permute-start = (f32[64,128]{1,0:T(8,128)S(1)}, f32[64,128]{1,0:T(8,128)S(1)}, u32[]{:S(2)}, u32[]{:S(2)}) collective-permute-start(f32[64,128]{1,0:T(8,128)S(1)} %get-tuple-element.36), channel_id=1, source_target_pairs={{1,2},{2,1},{3,4},{4,3},{5,6},{6,5},{7,8},{8,7},{9,10},{10,9},{11,... | collective-permute-start | bytes 98312 | tf_op jit(solution)/shard_map/ppermute | solution.py:458
  3.2 6.6 %collective-permute-start.1 = (f32[64,128]{1,0:T(8,128)S(1)}, f32[64,128]{1,0:T(8,128)S(1)}, u32[]{:S(2)}, u32[]{:S(2)}) collective-permute-start(f32[64,128]{1,0:T(8,128)S(1)} %get-tuple-element.37), channel_id=1, source_target_pairs={{0,1},{1,0},{2,3},{3,2},{4,5},{5,4},{6,7},{7,6},{8,9},{9,8},{10,11... | collective-permute-start | bytes 98312 | tf_op jit(solution)/shard_map/ppermute | solution.py:457
  11.0 13.7 %collective-permute-start.2 = (f32[5,104,128]{2,1,0:T(8,128)S(1)}, f32[5,104,128]{2,1,0:T(8,128)S(1)}, u32[]{:S(2)}, u32[]{:S(2)}) collective-permute-start(f32[5,104,128]{2,1,0:T(8,128)S(1)} %get-tuple-element.40), channel_id=1, source_target_pairs={{16,32},{32,16},{48,64},{64,48},{80,96},{96,80},{112,128},{128,112... | collective-permute-start | bytes 798728 | tf_op jit(solution)/shard_map/ppermute | solution.py:458
  15.5 10.1 %collective-permute-start.3 = (f32[5,104,128]{2,1,0:T(8,128)S(1)}, f32[5,104,128]{2,1,0:T(8,128)S(1)}, u32[]{:S(2)}, u32[]{:S(2)}) collective-permute-start(f32[5,104,128]{2,1,0:T(8,128)S(1)} %get-tuple-element.41), channel_id=1, source_target_pairs={{0,16},{16,0},{32,48},{48,32},{64,80},{80,64},{96,112},{112,96},{1... | collective-permute-start | bytes 798728 | tf_op jit(solution)/shard_map/ppermute | solution.py:457
  26.7 9.2 %collective-permute-start.4 = (f32[72,128]{1,0:T(8,128)S(1)}, f32[72,128]{1,0:T(8,128)S(1)}, u32[]{:S(2)}, u32[]{:S(2)}) collective-permute-start(f32[72,128]{1,0:T(8,128)S(1)} %get-tuple-element.42), channel_id=1, source_target_pairs={{16,32},{32,16},{48,64},{64,48},{80,96},{96,80},{112,128},{128,112... | collective-permute-start | bytes 110600 | tf_op jit(solution)/shard_map/ppermute | solution.py:458
  31.3 5.9 %collective-permute-start.5 = (f32[72,128]{1,0:T(8,128)S(1)}, f32[72,128]{1,0:T(8,128)S(1)}, u32[]{:S(2)}, u32[]{:S(2)}) collective-permute-start(f32[72,128]{1,0:T(8,128)S(1)} %get-tuple-element.43), channel_id=1, source_target_pairs={{0,16},{16,0},{32,48},{48,32},{64,80},{80,64},{96,112},{112,96},{1... | collective-permute-start | bytes 110600 | tf_op jit(solution)/shard_map/ppermute | solution.py:457

commit v4 on v3

--- a/solution.py
+++ b/solution.py
@@ -265,7 +265,8 @@
 
 
 def columns_kernel(
-    e_ref, o_ref, edge_ref, odd_ref, even_ref, for_even, for_odd, low_ref, high_ref, low_low_ref, low_high_ref
+    e_ref, o_ref, edge_ref, odd_ref, even_ref, for_even, for_odd, low_ref, high_ref, low_low_ref, low_high_ref,
+    one_ref, two_ref,
 ):
     is_even, at_start, at_end = ends("cols")
     left = jnp.where(is_even, odd_ref[...], even_ref[...])
@@ -288,18 +289,25 @@
     spread(low_low_ref, slice(None), low)
     spread(low_high_ref, slice(None), high)
     below = ends("rows")[0].astype(jnp.int32)
+    for t in range(wide // 128):
+        one_ref[t] = plain_low(low_low_ref, t, 32)
+        two_ref[t] = plain_low(one_ref, t, 16)
     for pack, last in ((for_even, below), (for_odd, 1 - below)):
         for t in range(wide // 128):
-            pack[t, 0:60] = low_low_ref[t, pl.ds(4 * last, 60)]
-            pack[t, 60:72] = low_high_ref[t, pl.ds(52 * last, 12)]
-        for j in range(18):
-            source = low_ref if j < 9 else high_ref
-            t, row = edge_place(j)
-            pack[t, row : row + 8] = source[j % 9, pl.ds(56 * last, 8)]
-
-
-def edge_place(j):
-    return j // 4, 72 + 8 * (j % 4)
+            pack[PIECE * t : PIECE * t + 8] = low_low_ref[t, pl.ds(56 * last, 8)]
+            pack[PIECE * t + 8 : PIECE * t + 16] = one_ref[t, pl.ds(2 + 20 * last, 8)]
+            pack[PIECE * t + 16 : PIECE * t + 25] = two_ref[t, pl.ds(3 + last, 9)]
+            pack[PIECE * t + 25 : PIECE * t + 37] = low_high_ref[t, pl.ds(52 * last, 12)]
+        for j in range(9):
+            pack[EDGES + 8 * j : EDGES + 8 * j + 8] = high_ref[j, pl.ds(56 * last, 8)]
+
+
+PIECE, EDGES, PACK = 37, 192, 264
+
+
+def plain_low(ref, t, tall):
+    near = (lambda x: pltpu.roll(x, 1, 0)), (lambda x: pltpu.roll(x, tall - 1, 0))
+    return forward_lift(ref[t, pl.ds(0, tall, stride=2)], ref[t, pl.ds(1, tall, stride=2)], near)[0]
 
 
 def edge_at(level, kind, t):
@@ -330,13 +338,19 @@
     _, left_end, right_end = ends("cols")
     above, under = sides(odd_ref, even_ref)
     for t in range(WIDE[1] // 128):
-        ll_ref[t, 4:64] = above(t, slice(0, 60))
-        ll_ref[t, 64:128] = own_low[t]
-        ll_ref[t, 128:188] = under(t, slice(0, 60))
-        lh_ref[t, 4:16] = above(t, slice(60, 72))
+        at = PIECE * t
+        s = slice(128 * t, 128 * t + 128)
+        for first, side in ((0, above), (72, under)):
+            ll_ref[t, first : first + 8] = side(slice(at, at + 8))
+        ll_ref[t, 8:72] = own_low[t]
+        l_ref[t, 8:48] = lifted(ll_ref, t, 40, 4, 32)[0]
+        for first, side in ((2, above), (46, under)):
+            l_ref[t, first : first + 8] = side(slice(at + 8, at + 16))
+        for first, side in ((4, above), (35, under)):
+            b_ref[first : first + 9, s] = side(slice(at + 16, at + 25))
+        for first, side in ((4, above), (80, under)):
+            lh_ref[t, first : first + 12] = side(slice(at + 25, at + 37))
         lh_ref[t, 16:80] = own_high[t]
-        lh_ref[t, 80:92] = under(t, slice(60, 72))
-        l_ref[t] = lifted(ll_ref, t, 96, 32, 32)[0]
         h_ref[t, 0:48] = lifted(lh_ref, t, 48, 8, 32)[0]
 
     def limited(coeffs, level, kind):
@@ -358,7 +372,7 @@
     for level in (1, 2, 3):
         own = OWN[level]
         if level == 1:
-            sizes = ((48, 16), (24, 4))
+            sizes = ((32, 6), (24, 4))
         else:
             rows = (48, 32)[level - 2]
             sizes = ((rows // 2, own),) * 2
@@ -376,8 +390,10 @@
             keep(level, 1, t, s, high, sizes[0][1])
             if level == 3:
                 keep(level, 3, t, s, low, sizes[0][1])
+            elif level == 2:
+                b_ref[0 : sizes[0][0], s] = low
             else:
-                b_ref[0 : sizes[0][0], s] = low
+                b_ref[13:35, s] = low[3:25]
             low, high = lifted(h_ref, t, *sizes[1], own)
             keep(level, 0, t, s, low, sizes[1][1])
             keep(level, 2, t, s, high, sizes[1][1])
@@ -385,12 +401,26 @@
 
 def detail_kernel(limit_ref, own_low, own_high, odd_ref, even_ref, hl_ref, lh_ref, hh_ref, x_ref):
     above, under = sides(odd_ref, even_ref)
-    for j in range(18):
-        own = own_low if j < 9 else own_high
-        t, row = edge_place(j)
-        x_ref[j, 0:8] = above(t, slice(row, row + 8))
-        x_ref[j, 8:72] = own[j % 9]
-        x_ref[j, 72:80] = under(t, slice(row, row + 8))
+    _, at_start, at_end = ends("cols")
+    low, high = (
+        jnp.concatenate(
+            [
+                jnp.concatenate([side(slice(PIECE * t + at, PIECE * t + at + 8)) for t in range(5)], 1)
+                for side, at in sources
+            ],
+            0,
+        )
+        for sources in (((above, 0), (under, 0)), ((above, 29), (under, 25)))
+    )
+    lows = merge_pairs(*lift_lanes(low, high, EDGE[1], 512, at_start, at_end, inverse=True))
+    for j in range(9):
+        x_ref[j, 0:8] = lows[0:8, 128 * j : 128 * j + 128]
+        x_ref[j, 8:72] = own_low[j]
+        x_ref[j, 72:80] = lows[8:16, 128 * j : 128 * j + 128]
+        at = slice(EDGES + 8 * j, EDGES + 8 * j + 8)
+        x_ref[j + 9, 0:8] = above(at)
+        x_ref[j + 9, 8:72] = own_high[j]
+        x_ref[j + 9, 72:80] = under(at)
 
     def lift(t, s):
         high = lifted(x_ref, t, 40, 4, 32)[1]
@@ -501,9 +531,9 @@
     )
     for_even, for_odd, *own = call(
         columns_kernel,
-        (f32(5, 104, 128), f32(5, 104, 128))
+        (f32(PACK, 128), f32(PACK, 128))
         + (f32(9, ROWS, 128), f32(9, ROWS, 128), f32(5, ROWS, 128), f32(5, ROWS, 128)),
-        [],
+        [scratch(5, 32, 128), scratch(5, 16, 128)],
         *inner,
         odd,
         even,
@@ -516,9 +546,9 @@
         forward_kernel,
         (f32(72, 128), f32(72, 128), *shapes[3:]),
         [
+            scratch(5, 64, 128),
             scratch(5, 96, 128),
-            scratch(5, 96, 128),
-            scratch(5, 192, 128),
+            scratch(5, 80, 128),
             scratch(5, 96, 128),
             scratch(48, 768),
         ],

time: 40.8 us -> 38 us (0.931)
  the two profiles are of different devices: /device:TPU:224 before, /device:TPU:222 now
where the time goes in v4:
time: 38 us; the launch traced here: 37.7 us
  starting transfers between devices  20.6 us (54%)
  waiting for transfers between devices  8.57 us (23%)
  Pallas kernels  7.28 us (19%)
  local copies, waits for them, and re-layouts  1.05 us (3%)
    ppermute x3, starting transfers between devices, exchange(): odd = lax.ppermute(for_odd, axis, swaps(axis, 1))  11.2 us
    ppermute x3, starting transfers between devices, exchange(): even = lax.ppermute(for_even, axis, swaps(axis, 0))  9.44 us
    pallas_call x6, Pallas kernels, call(): pl.pallas_call(kernel, out_shape=outs, in_specs=[smem] * scalars + [pl.Bl...  7.28 us
    ppermute x3, waiting for transfers between devices, exchange(): odd = lax.ppermute(for_odd, axis, swaps(axis, 1))  6.31 us
    ppermute x3, waiting for transfers between devices, exchange(): even = lax.ppermute(for_even, axis, swaps(axis, 0))  2.26 us
    unnamed x6, local copies, waits for them, and re-layouts  1.05 us
  transfers between devices with their start and end apart: 6, of which 4 were waited for; matrix products, arithmetic and copies ran while one was open for 0% of the time, Pallas kernels for 4%

profile of v4, /device:TPU:222, one launch (start us, length us, event | category | flops | bytes accessed | tf_op | source)
XLA Modules:
  0.0 37.7 jit_solution(5237838283471959431)
XLA Ops:
  0.0 0.0 copy-start
  0.0 1.0 %copy-done = f32[64,2048]{1,0:T(8,128)S(1)} copy-done((f32[64,2048]{1,0:T(8,128)S(1)}, f32[64,2048]{1,0:T(8,128)}, u32[]{:S(2)}) %copy-start) | copy-done | bytes 524312
  1.0 0.0 copy-start.1
  1.1 0.0 copy-start.2
  1.1 2.1 %collective-permute-start = (f32[64,128]{1,0:T(8,128)S(1)}, f32[64,128]{1,0:T(8,128)S(1)}, u32[]{:S(2)}, u32[]{:S(2)}) collective-permute-start(f32[64,128]{1,0:T(8,128)S(1)} %get-tuple-element.36), channel_id=1, source_target_pairs={{1,2},{2,1},{3,4},{4,3},{5,6},{6,5},{7,8},{8,7},{9,10},{10,9},{11,... | collective-permute-start | bytes 98312 | tf_op jit(solution)/shard_map/ppermute | solution.py:488
  3.2 5.6 %collective-permute-start.1 = (f32[64,128]{1,0:T(8,128)S(1)}, f32[64,128]{1,0:T(8,128)S(1)}, u32[]{:S(2)}, u32[]{:S(2)}) collective-permute-start(f32[64,128]{1,0:T(8,128)S(1)} %get-tuple-element.37), channel_id=1, source_target_pairs={{0,1},{1,0},{2,3},{3,2},{4,5},{5,4},{6,7},{7,6},{8,9},{9,8},{10,11... | collective-permute-start | bytes 98312 | tf_op jit(solution)/shard_map/ppermute | solution.py:487
  8.8 0.0 copy-done.1
  8.8 0.0 copy-done.2
  8.8 0.9 %shard_map.28 = (f32[64,896]{1,0:T(8,128)S(1)}, f32[64,896]{1,0:T(8,128)S(1)}, f32[64,256]{1,0:T(8,128)S(1)}, f32[16,128]{1,0:T(8,128)S(1)}) custom-call(f32[4,3]{1,0:T(4,128)S(1)} %copy-done.2, f32[64,2048]{1,0:T(8,128)S(1)} %copy-done.1), custom_call_target="tpu_custom_call" | custom-call | flops 2000000000 | bytes 4000000 | tf_op jit(solution)/shard_map/pallas_call | solution.py:503
  9.7 0.0 collective-permute-done.odd_ref
  9.7 0.0 collective-permute-done.1.even_ref
  9.7 1.3 %shard_map.30 = (f32[264,128]{1,0:T(8,128)S(1)}, f32[264,128]{1,0:T(8,128)S(1)}, f32[9,64,128]{2,1,0:T(8,128)S(1)}, f32[9,64,128]{2,1,0:T(8,128)S(1)}, f32[5,64,...) custom-call(f32[64,896]{1,0:T(8,128)S(1)} %get-tuple-element.33.e_ref, f32[64,896]{1,0:T(8,128)S(1)} %get-tuple-element.34.o_ref, ...), custom_call_target="tpu_custom_call" | custom-call | tf_op jit(solution)/shard_map/pallas_call | solution.py:503
  11.0 4.6 %collective-permute-start.2 = (f32[264,128]{1,0:T(8,128)S(1)}, f32[264,128]{1,0:T(8,128)S(1)}, u32[]{:S(2)}, u32[]{:S(2)}) collective-permute-start(f32[264,128]{1,0:T(8,128)S(1)} %get-tuple-element.40), channel_id=1, source_target_pairs={{16,32},{32,16},{48,64},{64,48},{80,96},{96,80},{112,128},{128,112... | collective-permute-start | bytes 405512 | tf_op jit(solution)/shard_map/ppermute | solution.py:488
  15.6 1.9 %collective-permute-start.3 = (f32[264,128]{1,0:T(8,128)S(1)}, f32[264,128]{1,0:T(8,128)S(1)}, u32[]{:S(2)}, u32[]{:S(2)}) collective-permute-start(f32[264,128]{1,0:T(8,128)S(1)} %get-tuple-element.41), channel_id=1, source_target_pairs={{0,16},{16,0},{32,48},{48,32},{64,80},{80,64},{96,112},{112,96},{1... | collective-permute-start | bytes 405512 | tf_op jit(solution)/shard_map/ppermute | solution.py:487
  17.6 4.4 %collective-permute-done.2.odd_ref = f32[264,128]{1,0:T(8,128)S(1)} collective-permute-done((f32[264,128]{1,0:T(8,128)S(1)}, f32[264,128]{1,0:T(8,128)S(1)}, u32[]{:S(2)}, u32[]{:S(2)}) %collective-permute-start.2) | collective-permute-done | bytes 135200 | tf_op jit(solution)/shard_map/ppermute | solution.py:488
  21.9 1.0 %collective-permute-done.3.even_ref = f32[264,128]{1,0:T(8,128)S(1)} collective-permute-done((f32[264,128]{1,0:T(8,128)S(1)}, f32[264,128]{1,0:T(8,128)S(1)}, u32[]{:S(2)}, u32[]{:S(2)}) %collective-permute-start.3) | collective-permute-done | bytes 135200 | tf_op jit(solution)/shard_map/ppermute | solution.py:487
  23.0 1.0 %shard_map.31 = (f32[72,128]{1,0:T(8,128)S(1)}, f32[72,128]{1,0:T(8,128)S(1)}, f32[24,640]{1,0:T(8,128)S(1)}, f32[24,640]{1,0:T(8,128)S(1)}, f32[24,640]{1,0:T(8...) custom-call(f32[16,128]{1,0:T(8,128)S(1)} %get-tuple-element.32.limi, ...), custom_call_target="tpu_custom_call" | custom-call | tf_op jit(solution)/shard_map/pallas_call | solution.py:503
  23.9 4.5 %collective-permute-start.4 = (f32[72,128]{1,0:T(8,128)S(1)}, f32[72,128]{1,0:T(8,128)S(1)}, u32[]{:S(2)}, u32[]{:S(2)}) collective-permute-start(f32[72,128]{1,0:T(8,128)S(1)} %get-tuple-element.42), channel_id=1, source_target_pairs={{16,32},{32,16},{48,64},{64,48},{80,96},{96,80},{112,128},{128,112... | collective-permute-start | bytes 110600 | tf_op jit(solution)/shard_map/ppermute | solution.py:488
  28.5 1.9 %collective-permute-start.5 = (f32[72,128]{1,0:T(8,128)S(1)}, f32[72,128]{1,0:T(8,128)S(1)}, u32[]{:S(2)}, u32[]{:S(2)}) collective-permute-start(f32[72,128]{1,0:T(8,128)S(1)} %get-tuple-element.43), channel_id=1, source_target_pairs={{0,16},{16,0},{32,48},{48,32},{64,80},{80,64},{96,112},{112,96},{1... | collective-permute-start | bytes 110600 | tf_op jit(solution)/shard_map/ppermute | solution.py:487
  30.4 0.7 %shard_map.32 = (f32[40,1152]{1,0:T(8,128)S(1)}, f32[40,1152]{1,0:T(8,128)S(1)}, f32[40,1152]{1,0:T(8,128)S(1)}) custom-call(f32[16,128]{1,0:T(8,128)S(1)} %get-tuple-element.32.limit_ref, f32[9,64,128]{2,1,0:T(8,128)S(1)} %get-tuple-element.44.own_low, f32[9,64,128]{2,1,0:T(8,128)S(1)} %get-tuple-element.45.own_high, ...), custom_call_target="tpu_custom_call" | custom-call | flops 2000000000 | bytes 4000000 | tf_op jit(solution)/shard_map/pallas_call | solution.py:503
  31.1 1.9 %collective-permute-done.4.odd_ref = f32[72,128]{1,0:T(8,128)S(1)} collective-permute-done((f32[72,128]{1,0:T(8,128)S(1)}, f32[72,128]{1,0:T(8,128)S(1)}, u32[]{:S(2)}, u32[]{:S(2)}) %collective-permute-start.4) | collective-permute-done | bytes 36896 | tf_op jit(solution)/shard_map/ppermute | solution.py:488
  33.1 1.2 %collective-permute-done.5.even_ref = f32[72,128]{1,0:T(8,128)S(1)} collective-permute-done((f32[72,128]{1,0:T(8,128)S(1)}, f32[72,128]{1,0:T(8,128)S(1)}, u32[]{:S(2)}, u32[]{:S(2)}) %collective-permute-start.5) | collective-permute-done | bytes 36896 | tf_op jit(solution)/shard_map/ppermute | solution.py:487
  34.3 3.3 %shard_map.33 = f32[64,2048]{1,0:T(8,128)} custom-call(f32[72,128]{1,0:T(8,128)S(1)} %collective-permute-done.4.odd_ref, f32[72,128]{1,0:T(8,128)S(1)} %collective-permute-done.5.even_ref, f32[40,1152]{1,0:T(8,128)S(1)} %get-tuple-element.46.rest_0_, f32[40,1152]{1,0:T(8,128)S(1)} %get-tuple-element.47.rest_1_, f32[40,1152]{1,0:T(8,128)S(1)} %get-tuple-element.48.rest_2_, ...), custom_call_target="tpu_custom_call" | custom-call | tf_op jit(solution)/shard_map/pallas_call | solution.py:503
  (1 shorter events, 0.0 us)
Async XLA Ops:
  0.0 1.0 %copy-start = (f32[64,2048]{1,0:T(8,128)S(1)}, f32[64,2048]{1,0:T(8,128)}, u32[]{:S(2)}) copy-start(f32[64,2048]{1,0:T(8,128)} %x_ref.3) | copy-start | bytes 1572868
  1.0 7.7 %copy-start.1 = (f32[64,2048]{1,0:T(8,128)S(1)}, f32[64,2048]{1,0:T(8,128)}, u32[]{:S(2)}) copy-start(f32[64,2048]{1,0:T(8,128)} %x_ref.3) | copy-start | bytes 1572868
  1.1 7.7 %copy-start.2 = (f32[4,3]{1,0:T(4,128)S(1)}, f32[4,3]{1,0:T(4,128)}, u32[]{:S(2)}) copy-start(f32[4,3]{1,0:T(4,128)} %t_ref.1) | copy-start | bytes 148
  1.1 8.6 %collective-permute-start = (f32[64,128]{1,0:T(8,128)S(1)}, f32[64,128]{1,0:T(8,128)S(1)}, u32[]{:S(2)}, u32[]{:S(2)}) collective-permute-start(f32[64,128]{1,0:T(8,128)S(1)} %get-tuple-element.36), channel_id=1, source_target_pairs={{1,2},{2,1},{3,4},{4,3},{5,6},{6,5},{7,8},{8,7},{9,10},{10,9},{11,... | collective-permute-start | bytes 98312 | tf_op jit(solution)/shard_map/ppermute | solution.py:488
  3.2 6.6 %collective-permute-start.1 = (f32[64,128]{1,0:T(8,128)S(1)}, f32[64,128]{1,0:T(8,128)S(1)}, u32[]{:S(2)}, u32[]{:S(2)}) collective-permute-start(f32[64,128]{1,0:T(8,128)S(1)} %get-tuple-element.37), channel_id=1, source_target_pairs={{0,1},{1,0},{2,3},{3,2},{4,5},{5,4},{6,7},{7,6},{8,9},{9,8},{10,11... | collective-permute-start | bytes 98312 | tf_op jit(solution)/shard_map/ppermute | solution.py:487
  11.0 10.9 %collective-permute-start.2 = (f32[264,128]{1,0:T(8,128)S(1)}, f32[264,128]{1,0:T(8,128)S(1)}, u32[]{:S(2)}, u32[]{:S(2)}) collective-permute-start(f32[264,128]{1,0:T(8,128)S(1)} %get-tuple-element.40), channel_id=1, source_target_pairs={{16,32},{32,16},{48,64},{64,48},{80,96},{96,80},{112,128},{128,112... | collective-permute-start | bytes 405512 | tf_op jit(solution)/shard_map/ppermute | solution.py:488
  15.6 7.3 %collective-permute-start.3 = (f32[264,128]{1,0:T(8,128)S(1)}, f32[264,128]{1,0:T(8,128)S(1)}, u32[]{:S(2)}, u32[]{:S(2)}) collective-permute-start(f32[264,128]{1,0:T(8,128)S(1)} %get-tuple-element.41), channel_id=1, source_target_pairs={{0,16},{16,0},{32,48},{48,32},{64,80},{80,64},{96,112},{112,96},{1... | collective-permute-start | bytes 405512 | tf_op jit(solution)/shard_map/ppermute | solution.py:487
  23.9 9.2 %collective-permute-start.4 = (f32[72,128]{1,0:T(8,128)S(1)}, f32[72,128]{1,0:T(8,128)S(1)}, u32[]{:S(2)}, u32[]{:S(2)}) collective-permute-start(f32[72,128]{1,0:T(8,128)S(1)} %get-tuple-element.42), channel_id=1, source_target_pairs={{16,32},{32,16},{48,64},{64,48},{80,96},{96,80},{112,128},{128,112... | collective-permute-start | bytes 110600 | tf_op jit(solution)/shard_map/ppermute | solution.py:488
  28.5 5.9 %collective-permute-start.5 = (f32[72,128]{1,0:T(8,128)S(1)}, f32[72,128]{1,0:T(8,128)S(1)}, u32[]{:S(2)}, u32[]{:S(2)}) collective-permute-start(f32[72,128]{1,0:T(8,128)S(1)} %get-tuple-element.43), channel_id=1, source_target_pairs={{0,16},{16,0},{32,48},{48,32},{64,80},{80,64},{96,112},{112,96},{1... | collective-permute-start | bytes 110600 | tf_op jit(solution)/shard_map/ppermute | solution.py:487

commit v5 on v4

--- a/solution.py
+++ b/solution.py
@@ -53,7 +53,7 @@
 def lift_lanes(even, odd, first, count, at_start, at_end, inverse=False):
     rows, width = even.shape
     if width >= STEPS_FROM:
-        near = neighbours(1, first, count, at_start, at_end)
+        near = neighbours(1, [(first, at_start)], [(first + count - 1, at_end)])
         lift = inverse_lift if inverse else forward_lift
         groups = [slice(k, min(k + GROUP, rows)) for k in range(0, rows, GROUP)]
         parts = [lift(even[g], odd[g], near) for g in groups]
@@ -113,13 +113,18 @@
     return jnp.concatenate(parts, axis) if len(parts) > 1 else tile
 
 
-def neighbours(axis, first, count, at_start, at_end):
+def neighbours(axis, starts, stops):
     def before(odd):
-        return patch(pltpu.roll(odd, 1, axis), odd, axis, first, at_start)
+        rolled = pltpu.roll(odd, 1, axis)
+        for index, flag in starts:
+            rolled = patch(rolled, odd, axis, index, flag)
+        return rolled
 
     def after(even):
         rolled = pltpu.roll(even, even.shape[axis] - 1, axis)
-        return patch(rolled, even, axis, first + count - 1, at_end)
+        for index, flag in stops:
+            rolled = patch(rolled, even, axis, index, flag)
+        return rolled
 
     return before, after
 
@@ -265,8 +270,8 @@
 
 
 def columns_kernel(
-    e_ref, o_ref, edge_ref, odd_ref, even_ref, for_even, for_odd, low_ref, high_ref, low_low_ref, low_high_ref,
-    one_ref, two_ref,
+    e_ref, o_ref, edge_ref, odd_ref, even_ref, for_even, for_odd, for_even_far, for_odd_far,
+    low_ref, high_ref, low_low_ref, low_high_ref, one_ref, two_ref, one_high_ref,
 ):
     is_even, at_start, at_end = ends("cols")
     left = jnp.where(is_even, odd_ref[...], even_ref[...])
@@ -288,21 +293,35 @@
     low, high = lift_lanes(*split_pairs(low), EDGE[1], 512, at_start, at_end)
     spread(low_low_ref, slice(None), low)
     spread(low_high_ref, slice(None), high)
-    below = ends("rows")[0].astype(jnp.int32)
     for t in range(wide // 128):
         one_ref[t] = plain_low(low_low_ref, t, 32)
         two_ref[t] = plain_low(one_ref, t, 16)
+        one_high_ref[t] = plain_low(low_high_ref, t, 32)
+    row = lax.axis_index("rows")
+    below = (row % 2 == 0).astype(jnp.int32)
     for pack, last in ((for_even, below), (for_odd, 1 - below)):
         for t in range(wide // 128):
-            pack[PIECE * t : PIECE * t + 8] = low_low_ref[t, pl.ds(56 * last, 8)]
-            pack[PIECE * t + 8 : PIECE * t + 16] = one_ref[t, pl.ds(2 + 20 * last, 8)]
-            pack[PIECE * t + 16 : PIECE * t + 25] = two_ref[t, pl.ds(3 + last, 9)]
-            pack[PIECE * t + 25 : PIECE * t + 37] = low_high_ref[t, pl.ds(52 * last, 12)]
+            at = PIECE * t
+            pack[at : at + 8] = low_low_ref[t, 0:8]
+            pack[at + 8 : at + 16] = low_low_ref[t, 56:64]
+            pack[at + 16 : at + 24] = one_ref[t, 2:10]
+            pack[at + 24 : at + 32] = one_ref[t, 22:30]
+            pack[at + 32 : at + 42] = two_ref[t, 3:13]
+            pack[at + 42 : at + 50] = low_high_ref[t, pl.ds(56 * last, 8)]
+            pack[at + 50 : at + 58] = one_high_ref[t, pl.ds(2 + 20 * last, 8)]
         for j in range(9):
             pack[EDGES + 8 * j : EDGES + 8 * j + 8] = high_ref[j, pl.ds(56 * last, 8)]
-
-
-PIECE, EDGES, PACK = 37, 192, 264
+    below = (row % 4 < 2).astype(jnp.int32)
+    for pack, last in ((for_even_far, below), (for_odd_far, 1 - below)):
+        for t in range(wide // 128):
+            at = FAR_PIECE * t
+            pack[at : at + 8] = low_low_ref[t, pl.ds(56 * last, 8)]
+            pack[at + 8 : at + 16] = one_ref[t, pl.ds(2 + 20 * last, 8)]
+            pack[at + 16 : at + 25] = two_ref[t, pl.ds(3 + last, 9)]
+
+
+PIECE, EDGES, PACK = 58, 296, 368
+FAR_PIECE, FAR_PACK = 25, 128
 
 
 def plain_low(ref, t, tall):
@@ -310,75 +329,74 @@
     return forward_lift(ref[t, pl.ds(0, tall, stride=2)], ref[t, pl.ds(1, tall, stride=2)], near)[0]
 
 
-def edge_at(level, kind, t):
-    return 4 * (2 * kind + t) if level == 3 else 32 + 4 * (5 * (kind // 2) + t)
-
-
-def sides(odd_ref, even_ref):
-    is_even = ends("rows")[0]
-
+def sides(flag, odd_ref, even_ref):
     def above(*at):
-        return jnp.where(is_even, odd_ref[at], even_ref[at])
+        return jnp.where(flag, odd_ref[at], even_ref[at])
 
     def under(*at):
-        return jnp.where(is_even, even_ref[at], odd_ref[at])
+        return jnp.where(flag, even_ref[at], odd_ref[at])
 
     return above, under
 
 
+def halves_of(ref, t, tall):
+    return ref[t, pl.ds(0, tall, stride=2)], ref[t, pl.ds(1, tall, stride=2)]
+
+
 def lifted(ref, t, tall, begin, own):
-    _, at_start, at_end = ends("rows")
-    near = neighbours(0, begin, own, at_start, at_end)
-    return forward_lift(ref[t, pl.ds(0, tall, stride=2)], ref[t, pl.ds(1, tall, stride=2)], near)
-
-
-def forward_kernel(limit_ref, own_low, own_high, odd_ref, even_ref, for_even, for_odd, *rest):
-    outs, (l_ref, h_ref, ll_ref, lh_ref, b_ref) = rest[:10], rest[10:]
-    is_even = ends("rows")[0]
+    row, count = lax.axis_index("rows"), lax.axis_size("rows")
+    starts, stops = [(begin, row == 0)], [(begin + own - 1, row == count - 1)]
+    if begin >= own:
+        starts.append((begin - own, row == 1))
+        stops.append((begin + 2 * own - 1, row == count - 2))
+    return forward_lift(*halves_of(ref, t, tall), neighbours(0, starts, stops))
+
+
+def forward_part(limits, own_low, own_high, near_sides, far_sides, outs, refs):
+    l_ref, h_ref, ll_ref, lh_ref, f_ref, g_ref, b_ref = refs
+    (above, under), (above_far, under_far) = near_sides, far_sides
+    row, count = lax.axis_index("rows"), lax.axis_size("rows")
     _, left_end, right_end = ends("cols")
-    above, under = sides(odd_ref, even_ref)
     for t in range(WIDE[1] // 128):
-        at = PIECE * t
+        at, far = PIECE * t, FAR_PIECE * t
         s = slice(128 * t, 128 * t + 128)
-        for first, side in ((0, above), (72, under)):
-            ll_ref[t, first : first + 8] = side(slice(at, at + 8))
-        ll_ref[t, 8:72] = own_low[t]
+
+        def part(offset, size=8, at=at):
+            return slice(at + offset, at + offset + size)
+
+        def far_part(offset, size=8, far=far):
+            return slice(far + offset, far + offset + size)
+
+        ll_ref[t, 0:8], ll_ref[t, 8:72], ll_ref[t, 72:80] = above(part(8)), own_low[t], under(part(0))
+        lh_ref[t, 0:8], lh_ref[t, 8:72], lh_ref[t, 72:80] = above(part(42)), own_high[t], under(part(42))
         l_ref[t, 8:48] = lifted(ll_ref, t, 40, 4, 32)[0]
-        for first, side in ((2, above), (46, under)):
-            l_ref[t, first : first + 8] = side(slice(at + 8, at + 16))
-        for first, side in ((4, above), (35, under)):
-            b_ref[first : first + 9, s] = side(slice(at + 16, at + 25))
-        for first, side in ((4, above), (80, under)):
-            lh_ref[t, first : first + 12] = side(slice(at + 25, at + 37))
-        lh_ref[t, 16:80] = own_high[t]
-        h_ref[t, 0:48] = lifted(lh_ref, t, 48, 8, 32)[0]
-
-    def limited(coeffs, level, kind):
-        if kind == 3:
-            return coeffs
-        at = 3 * level + kind
-        return soften(coeffs, limit_ref[at : at + 1, :])
-
-    def keep(level, kind, t, s, coeffs, begin):
-        own = OWN[level]
-        coeffs = limited(coeffs[begin - 4 : begin + own + 4], level, kind)
-        outs[3 * (level - 1) + kind][:, s] = coeffs
-        if level == 3 or (level == 1 and kind != 1):
-            first, last = coeffs[4:8], coeffs[own : own + 4]
-            at = edge_at(level, kind, t)
-            for_even[at : at + 4, :] = jnp.where(is_even, last, first)
-            for_odd[at : at + 4, :] = jnp.where(is_even, first, last)
+        l_ref[t, 2:10], l_ref[t, 46:54] = above(part(24)), under(part(16))
+        h_ref[t, 8:48] = lifted(lh_ref, t, 40, 4, 32)[0]
+        h_ref[t, 2:10], h_ref[t, 46:54] = above(part(50)), under(part(50))
+        f_ref[t, 0:8], f_ref[t, 8:16] = above_far(far_part(0)), above(part(0))
+        f_ref[t, 16:24], f_ref[t, 24:32] = under(part(8)), under_far(far_part(0))
+        near = neighbours(0, [(4, row == 1)], [(11, row == count - 2)])
+        one = forward_lift(*halves_of(f_ref, t, 16), near)[0]
+        g_ref[t, 10:14], g_ref[t, 42:46] = one[2:6], one[10:14]
+        g_ref[t, 2:10], g_ref[t, 14:22] = above_far(far_part(8)), above(part(16))
+        g_ref[t, 34:42], g_ref[t, 46:54] = under(part(24)), under_far(far_part(8))
+        near = neighbours(0, [(6, row == 1)], [(21, row == count - 2)])
+        two = forward_lift(*halves_of(g_ref, t, 32), near)[0]
+        b_ref[0:9, s], b_ref[9:15, s], b_ref[15:25, s] = above_far(far_part(16, 9)), two[3:9], above(part(32, 10))
+        b_ref[47:57, s], b_ref[57:63, s], b_ref[63:72, s] = under(part(32, 10)), two[19:25], under_far(far_part(16, 9))
+
+    def keep(level, kind, s, coeffs, begin):
+        coeffs = coeffs[begin - 4 : begin + OWN[level] + 4]
+        if kind < 3:
+            at = 3 * level + kind
+            coeffs = soften(coeffs, limits[at : at + 1, :])
+        outs[3 * level + kind][0 : OWN[level] + 8, s] = coeffs
 
     for level in (1, 2, 3):
         own = OWN[level]
-        if level == 1:
-            sizes = ((32, 6), (24, 4))
-        else:
-            rows = (48, 32)[level - 2]
-            sizes = ((rows // 2, own),) * 2
-            known, wide = WIDE[level - 1], WIDE[level]
-            if level == 3:
-                b_ref[24:32, :known] = jnp.zeros((8, known), jnp.float32)
+        tall, begin = ((32, 6), (40, 14), (16, 6))[level - 1]
+        if level > 1:
+            rows, known, wide = (72, 32)[level - 2], WIDE[level - 1], WIDE[level]
             b_ref[0:rows, known : 2 * wide] = jnp.zeros((rows, 2 * wide - known), jnp.float32)
             halves = split_pairs(b_ref[0:rows, : 2 * wide])
             low, high = lift_lanes(*halves, EDGE[level], 1024 >> level, left_end, right_end)
@@ -386,21 +404,21 @@
             spread(h_ref, slice(0, rows), high)
         for t in range(WIDE[level] // 128):
             s = slice(128 * t, 128 * t + 128)
-            low, high = lifted(l_ref, t, *sizes[0], own)
-            keep(level, 1, t, s, high, sizes[0][1])
-            if level == 3:
-                keep(level, 3, t, s, low, sizes[0][1])
+            low, high = lifted(l_ref, t, tall, begin, own)
+            keep(level, 1, s, high, begin)
+            if level == 1:
+                b_ref[25:47, s] = low[3:25]
             elif level == 2:
-                b_ref[0 : sizes[0][0], s] = low
+                b_ref[0:32, s] = low[2:34]
             else:
-                b_ref[13:35, s] = low[3:25]
-            low, high = lifted(h_ref, t, *sizes[1], own)
-            keep(level, 0, t, s, low, sizes[1][1])
-            keep(level, 2, t, s, high, sizes[1][1])
-
-
-def detail_kernel(limit_ref, own_low, own_high, odd_ref, even_ref, hl_ref, lh_ref, hh_ref, x_ref):
-    above, under = sides(odd_ref, even_ref)
+                keep(level, 3, s, low, begin)
+            low, high = lifted(h_ref, t, tall, begin, own)
+            keep(level, 0, s, low, begin)
+            keep(level, 2, s, high, begin)
+
+
+def detail_part(limits, own_low, own_high, near_sides, outs, x_ref):
+    above, under = near_sides
     _, at_start, at_end = ends("cols")
     low, high = (
         jnp.concatenate(
@@ -410,7 +428,7 @@
             ],
             0,
         )
-        for sources in (((above, 0), (under, 0)), ((above, 29), (under, 25)))
+        for sources in (((above, 8), (under, 0)), ((above, 42), (under, 42)))
     )
     lows = merge_pairs(*lift_lanes(low, high, EDGE[1], 512, at_start, at_end, inverse=True))
     for j in range(9):
@@ -424,40 +442,29 @@
 
     def lift(t, s):
         high = lifted(x_ref, t, 40, 4, 32)[1]
-        lh_ref[:, s] = soften(high, limit_ref[1:2, :])
+        outs[1][:, s] = soften(high, limits[1:2, :])
         low, high = lifted(x_ref, t + 9, 40, 4, 32)
-        hl_ref[:, s] = soften(low, limit_ref[0:1, :])
-        hh_ref[:, s] = soften(high, limit_ref[2:3, :])
+        outs[0][:, s] = soften(low, limits[0:1, :])
+        outs[2][:, s] = soften(high, limits[2:3, :])
 
     tiles(WIDE[0], lift)
 
 
-def inverse_kernel(odd_ref, even_ref, *rest):
-    ins, out_ref, (v_ref, w_ref, r_ref), kept = rest[:13], rest[13], rest[14:17], rest[17:]
+def inverse_part(ins, out_ref, v_ref, w_ref, r_ref):
     _, at_start, at_end = ends("rows")
     _, left_end, right_end = ends("cols")
-    above, under = sides(odd_ref, even_ref)
     for level in range(LEVELS - 1, -1, -1):
         own = OWN[level]
         long = max(own + 8, 16)
-        near = neighbours(0, 4, own, at_start, at_end)
-
-        def whole(kind, t, s, level=level, own=own, long=long):
-            source = ins[3 * level + kind]
-            if level == 2 or level == 0 or (level == 1 and kind == 1):
-                return source[0:long, s]
-            target, at = kept[kind], slice(edge_at(level, kind, t), edge_at(level, kind, t) + 4)
-            target[0 : own + 8, s] = source[:, s]
-            target[0:4, s] = above(at)
-            target[4 + own : 8 + own, s] = under(at)
-            return target[0:long, s]
-
-        def lift_down(t, s, level=level, long=long, near=near, whole=whole):
-            low = whole(3, t, s) if level == LEVELS - 1 else r_ref[4 : 4 + long, s]
-            even, odd = inverse_lift(low, whole(1, t, s), near)
+        near = neighbours(0, [(4, at_start)], [(3 + own, at_end)])
+        hl, lh, hh = ins[3 * level : 3 * level + 3]
+
+        def lift_down(t, s, level=level, long=long, near=near, hl=hl, lh=lh, hh=hh):
+            low = ins[12][0:long, s] if level == LEVELS - 1 else r_ref[4 : 4 + long, s]
+            even, odd = inverse_lift(low, lh[0:long, s], near)
             v_ref[t, pl.ds(0, long, stride=2)] = even
             v_ref[t, pl.ds(1, long, stride=2)] = odd
-            even, odd = inverse_lift(whole(0, t, s), whole(2, t, s), near)
+            even, odd = inverse_lift(hl[0:long, s], hh[0:long, s], near)
             w_ref[t, pl.ds(0, long, stride=2)] = even
             w_ref[t, pl.ds(1, long, stride=2)] = odd
 
@@ -475,17 +482,30 @@
             out_ref[...] = both[:, 128 : 128 + COLS]
 
 
-def swaps(axis, offset):
+def rows_kernel(
+    limits, own_low, own_high, own_low_low, own_low_high, odd_ref, even_ref, odd_far, even_far, out_ref, *refs
+):
+    bands, refs = refs[:13], refs[13:]
+    row = lax.axis_index("rows")
+    near_sides = sides(row % 2 == 0, odd_ref, even_ref)
+    far_sides = sides(row % 4 < 2, odd_far, even_far)
+    forward_part(limits, own_low_low, own_low_high, near_sides, far_sides, bands, refs[:7])
+    detail_part(limits, own_low, own_high, near_sides, bands, refs[7])
+    inverse_part(bands, out_ref, *refs[8:])
+
+
+def swaps(axis, offset, apart):
     count = lax.axis_size(axis)
     pairs = []
-    for i in range(offset, count - 1, 2):
-        pairs += [(i, i + 1), (i + 1, i)]
+    for block in range(offset, count, 2 * apart):
+        for i in range(block, min(block + apart, count - apart)):
+            pairs += [(i, i + apart), (i + apart, i)]
     return pairs
 
 
-def exchange(for_even, for_odd, axis):
-    even = lax.ppermute(for_even, axis, swaps(axis, 0))
-    odd = lax.ppermute(for_odd, axis, swaps(axis, 1))
+def exchange(for_even, for_odd, axis, apart=1):
+    even = lax.ppermute(for_even, axis, swaps(axis, 0, apart))
+    odd = lax.ppermute(for_odd, axis, swaps(axis, apart, apart))
     return odd, even
 
 
@@ -529,56 +549,28 @@
         scalars=1,
         cost=pl.CostEstimate(flops=2 * 10**9, bytes_accessed=4 * 10**6, transcendentals=0),
     )
-    for_even, for_odd, *own = call(
+    for_even, for_odd, for_even_far, for_odd_far, *own = call(
         columns_kernel,
-        (f32(PACK, 128), f32(PACK, 128))
+        (f32(PACK, 128), f32(PACK, 128), f32(FAR_PACK, 128), f32(FAR_PACK, 128))
         + (f32(9, ROWS, 128), f32(9, ROWS, 128), f32(5, ROWS, 128), f32(5, ROWS, 128)),
-        [scratch(5, 32, 128), scratch(5, 16, 128)],
+        [scratch(5, 32, 128), scratch(5, 16, 128), scratch(5, 32, 128)],
         *inner,
         odd,
         even,
     )
-    own_low, own_high, own_low_low, own_low_high = own
-    odd, even = exchange(for_even, for_odd, "rows")
-    shapes = [f32(OWN[level] + 8, WIDE[level]) for level in range(LEVELS) for _ in range(3)]
-    shapes.append(shapes[-1])
-    for_even, for_odd, *bands = call(
-        forward_kernel,
-        (f32(72, 128), f32(72, 128), *shapes[3:]),
-        [
-            scratch(5, 64, 128),
-            scratch(5, 96, 128),
-            scratch(5, 80, 128),
-            scratch(5, 96, 128),
-            scratch(48, 768),
-        ],
+    received = exchange(for_even, for_odd, "rows")
+    received += exchange(for_even_far, for_odd_far, "rows", 2)
+    bands = [scratch(max(OWN[level] + 8, 16), WIDE[level]) for level in range(LEVELS) for _ in range(3)]
+    return call(
+        rows_kernel,
+        f32(ROWS, COLS),
+        [*bands, bands[-1]]
+        + [scratch(5, 80, 128), scratch(5, 80, 128), scratch(5, 80, 128), scratch(5, 80, 128)]
+        + [scratch(5, 32, 128), scratch(5, 64, 128), scratch(72, 768), scratch(18, 80, 128)]
+        + [scratch(9, 80, 128), scratch(9, 80, 128), scratch(48, 1280)],
         limits,
-        own_low_low,
-        own_low_high,
-        odd,
-        even,
-    )
-    finest = call(
-        detail_kernel,
-        tuple(shapes[:3]),
-        [scratch(18, 80, 128)],
-        limits,
-        own_low,
-        own_high,
-        odd,
-        even,
-        cost=pl.CostEstimate(flops=2 * 10**9, bytes_accessed=4 * 10**6, transcendentals=0),
-    )
-    odd, even = exchange(for_even, for_odd, "rows")
-    return call(
-        inverse_kernel,
-        f32(ROWS, COLS),
-        [scratch(9, 80, 128), scratch(9, 80, 128), scratch(48, 1280)]
-        + [scratch(24, 640), scratch(16, 256), scratch(24, 640), scratch(16, 256)],
-        odd,
-        even,
-        *finest,
-        *bands,
+        *own,
+        *received,
     )
 
 

time: 38 us -> 36.6 us (0.963)
  waiting for transfers between devices: 8.57 us -> 5.75 us
  starting transfers between devices: 20.6 us -> 22.1 us
    ppermute x6, waiting for transfers between devices: 8.57 us -> 5.75 us  [the longest x3 3.91 us: exchange(): even = lax.ppermute(for_even, axis, swaps(axis, 0, apart))]
    ppermute x6, starting transfers between devices: 20.6 us -> 22.1 us  [the longest x3 12.7 us: exchange(): odd = lax.ppermute(for_odd, axis, swaps(axis, apart, apart))]
    pallas_call x6 -> x4, Pallas kernels: 7.28 us -> 7.35 us  [call(): pl.pallas_call(kernel, out_shape=outs, in_specs=[smem] * scalars + [pl.Bl...]
  transfers between devices with their start and end apart: 6 -> 6, of which waited for: 4 -> 2; matrix products, arithmetic and copies ran while one was open for 0% -> 0% of each run, Pallas kernels for 4% -> 3%
where the time goes in v5:
time: 36.6 us; the launch traced here: 36.4 us
  starting transfers between devices  22.1 us (60%)
  Pallas kernels  7.35 us (20%)
  waiting for transfers between devices  5.75 us (16%)
  local copies, waits for them, and re-layouts  1.05 us (3%)
    ppermute x3, starting transfers between devices, exchange(): odd = lax.ppermute(for_odd, axis, swaps(axis, apart, apart))  12.7 us
    ppermute x3, starting transfers between devices, exchange(): even = lax.ppermute(for_even, axis, swaps(axis, 0, apart))  9.44 us
    pallas_call x4, Pallas kernels, call(): pl.pallas_call(kernel, out_shape=outs, in_specs=[smem] * scalars + [pl.Bl...  7.35 us
    ppermute x3, waiting for transfers between devices, exchange(): even = lax.ppermute(for_even, axis, swaps(axis, 0, apart))  3.91 us
    ppermute x3, waiting for transfers between devices, exchange(): odd = lax.ppermute(for_odd, axis, swaps(axis, apart, apart))  1.83 us
    unnamed x6, local copies, waits for them, and re-layouts  1.05 us
  transfers between devices with their start and end apart: 6, of which 2 were waited for; matrix products, arithmetic and copies ran while one was open for 0% of the time, Pallas kernels for 3%

profile of v5, /device:TPU:222, one launch (start us, length us, event | category | flops | bytes accessed | tf_op | source)
XLA Modules:
  0.0 36.4 jit_solution(4638329508546771792)
XLA Ops:
  0.0 0.0 copy-start
  0.0 1.0 %copy-done = f32[64,2048]{1,0:T(8,128)S(1)} copy-done((f32[64,2048]{1,0:T(8,128)S(1)}, f32[64,2048]{1,0:T(8,128)}, u32[]{:S(2)}) %copy-start) | copy-done | bytes 524312
  1.0 0.0 copy-start.1
  1.1 0.0 copy-start.2
  1.1 2.1 %collective-permute-start = (f32[64,128]{1,0:T(8,128)S(1)}, f32[64,128]{1,0:T(8,128)S(1)}, u32[]{:S(2)}, u32[]{:S(2)}) collective-permute-start(f32[64,128]{1,0:T(8,128)S(1)} %get-tuple-element.23), channel_id=1, source_target_pairs={{1,2},{2,1},{3,4},{4,3},{5,6},{6,5},{7,8},{8,7},{9,10},{10,9},{11,... | collective-permute-start | bytes 98312 | tf_op jit(solution)/shard_map/ppermute | solution.py:508
  3.2 5.6 %collective-permute-start.1 = (f32[64,128]{1,0:T(8,128)S(1)}, f32[64,128]{1,0:T(8,128)S(1)}, u32[]{:S(2)}, u32[]{:S(2)}) collective-permute-start(f32[64,128]{1,0:T(8,128)S(1)} %get-tuple-element.24), channel_id=1, source_target_pairs={{0,1},{1,0},{2,3},{3,2},{4,5},{5,4},{6,7},{7,6},{8,9},{9,8},{10,11... | collective-permute-start | bytes 98312 | tf_op jit(solution)/shard_map/ppermute | solution.py:507
  8.8 0.0 copy-done.1
  8.8 0.0 copy-done.2
  8.8 0.9 %shard_map.28 = (f32[64,896]{1,0:T(8,128)S(1)}, f32[64,896]{1,0:T(8,128)S(1)}, f32[64,256]{1,0:T(8,128)S(1)}, f32[16,128]{1,0:T(8,128)S(1)}) custom-call(f32[4,3]{1,0:T(4,128)S(1)} %copy-done.2, f32[64,2048]{1,0:T(8,128)S(1)} %copy-done.1), custom_call_target="tpu_custom_call" | custom-call | flops 2000000000 | bytes 4000000 | tf_op jit(solution)/shard_map/pallas_call | solution.py:523
  9.7 0.0 collective-permute-done.odd_ref
  9.7 0.0 collective-permute-done.1.even_ref
  9.7 1.3 %shard_map.30 = (f32[368,128]{1,0:T(8,128)S(1)}, f32[368,128]{1,0:T(8,128)S(1)}, f32[128,128]{1,0:T(8,128)S(1)}, f32[128,128]{1,0:T(8,128)S(1)}, f32[9,64,128]{2...) custom-call(f32[64,896]{1,0:T(8,128)S(1)} %get-tuple-element.20.e_ref, ...), custom_call_target="tpu_custom_call" | custom-call | tf_op jit(solution)/shard_map/pallas_call | solution.py:523
  11.1 4.6 %collective-permute-start.2 = (f32[368,128]{1,0:T(8,128)S(1)}, f32[368,128]{1,0:T(8,128)S(1)}, u32[]{:S(2)}, u32[]{:S(2)}) collective-permute-start(f32[368,128]{1,0:T(8,128)S(1)} %get-tuple-element.29), channel_id=1, source_target_pairs={{16,32},{32,16},{48,64},{64,48},{80,96},{96,80},{112,128},{128,112... | collective-permute-start | bytes 565256 | tf_op jit(solution)/shard_map/ppermute | solution.py:508
  15.7 1.9 %collective-permute-start.3 = (f32[368,128]{1,0:T(8,128)S(1)}, f32[368,128]{1,0:T(8,128)S(1)}, u32[]{:S(2)}, u32[]{:S(2)}) collective-permute-start(f32[368,128]{1,0:T(8,128)S(1)} %get-tuple-element.30), channel_id=1, source_target_pairs={{0,16},{16,0},{32,48},{48,32},{64,80},{80,64},{96,112},{112,96},{1... | collective-permute-start | bytes 565256 | tf_op jit(solution)/shard_map/ppermute | solution.py:507
  17.6 6.0 %collective-permute-start.4 = (f32[128,128]{1,0:T(8,128)S(1)}, f32[128,128]{1,0:T(8,128)S(1)}, u32[]{:S(2)}, u32[]{:S(2)}) collective-permute-start(f32[128,128]{1,0:T(8,128)S(1)} %get-tuple-element.31), channel_id=1, source_target_pairs={{32,64},{64,32},{48,80},{80,48},{96,128},{128,96},{112,144},{144,1... | collective-permute-start | bytes 196616 | tf_op jit(solution)/shard_map/ppermute | solution.py:508
  23.6 1.9 %collective-permute-start.5 = (f32[128,128]{1,0:T(8,128)S(1)}, f32[128,128]{1,0:T(8,128)S(1)}, u32[]{:S(2)}, u32[]{:S(2)}) collective-permute-start(f32[128,128]{1,0:T(8,128)S(1)} %get-tuple-element.32), channel_id=1, source_target_pairs={{0,32},{32,0},{16,48},{48,16},{64,96},{96,64},{80,112},{112,80},{1... | collective-permute-start | bytes 196616 | tf_op jit(solution)/shard_map/ppermute | solution.py:507
  25.6 1.8 %collective-permute-done.4.odd_far = f32[128,128]{1,0:T(8,128)S(1)} collective-permute-done((f32[128,128]{1,0:T(8,128)S(1)}, f32[128,128]{1,0:T(8,128)S(1)}, u32[]{:S(2)}, u32[]{:S(2)}) %collective-permute-start.4) | collective-permute-done | bytes 65568 | tf_op jit(solution)/shard_map/ppermute | solution.py:508
  27.4 3.9 %collective-permute-done.5.even_far = f32[128,128]{1,0:T(8,128)S(1)} collective-permute-done((f32[128,128]{1,0:T(8,128)S(1)}, f32[128,128]{1,0:T(8,128)S(1)}, u32[]{:S(2)}, u32[]{:S(2)}) %collective-permute-start.5) | collective-permute-done | bytes 65568 | tf_op jit(solution)/shard_map/ppermute | solution.py:507
  31.3 0.0 collective-permute-done.2.odd_ref
  31.3 0.0 collective-permute-done.3.even_ref
  31.3 5.0 %shard_map.31 = f32[64,2048]{1,0:T(8,128)} custom-call(f32[16,128]{1,0:T(8,128)S(1)} %get-tuple-element.19.limits, f32[9,64,128]{2,1,0:T(8,128)S(1)} %get-tuple-element.25.own_low, f32[9,64,128]{2,1,0:T(8,128)S(1)} %get-tuple-element.26.own_high, f32[5,64,128]{2,1,0:T(8,128)S(1)} %get-tuple-element.27.own_low_low, ...), custom_call_target="tpu_custom_call" | custom-call | tf_op jit(solution)/shard_map/pallas_call | solution.py:523
  (1 shorter events, 0.0 us)
Async XLA Ops:
  0.0 1.0 %copy-start = (f32[64,2048]{1,0:T(8,128)S(1)}, f32[64,2048]{1,0:T(8,128)}, u32[]{:S(2)}) copy-start(f32[64,2048]{1,0:T(8,128)} %x_ref.3) | copy-start | bytes 1572868
  1.0 7.7 %copy-start.1 = (f32[64,2048]{1,0:T(8,128)S(1)}, f32[64,2048]{1,0:T(8,128)}, u32[]{:S(2)}) copy-start(f32[64,2048]{1,0:T(8,128)} %x_ref.3) | copy-start | bytes 1572868
  1.1 7.7 %copy-start.2 = (f32[4,3]{1,0:T(4,128)S(1)}, f32[4,3]{1,0:T(4,128)}, u32[]{:S(2)}) copy-start(f32[4,3]{1,0:T(4,128)} %t_ref.1) | copy-start | bytes 148
  1.1 8.6 %collective-permute-start = (f32[64,128]{1,0:T(8,128)S(1)}, f32[64,128]{1,0:T(8,128)S(1)}, u32[]{:S(2)}, u32[]{:S(2)}) collective-permute-start(f32[64,128]{1,0:T(8,128)S(1)} %get-tuple-element.23), channel_id=1, source_target_pairs={{1,2},{2,1},{3,4},{4,3},{5,6},{6,5},{7,8},{8,7},{9,10},{10,9},{11,... | collective-permute-start | bytes 98312 | tf_op jit(solution)/shard_map/ppermute | solution.py:508
  3.2 6.6 %collective-permute-start.1 = (f32[64,128]{1,0:T(8,128)S(1)}, f32[64,128]{1,0:T(8,128)S(1)}, u32[]{:S(2)}, u32[]{:S(2)}) collective-permute-start(f32[64,128]{1,0:T(8,128)S(1)} %get-tuple-element.24), channel_id=1, source_target_pairs={{0,1},{1,0},{2,3},{3,2},{4,5},{5,4},{6,7},{7,6},{8,9},{9,8},{10,11... | collective-permute-start | bytes 98312 | tf_op jit(solution)/shard_map/ppermute | solution.py:507
  11.1 20.2 %collective-permute-start.2 = (f32[368,128]{1,0:T(8,128)S(1)}, f32[368,128]{1,0:T(8,128)S(1)}, u32[]{:S(2)}, u32[]{:S(2)}) collective-permute-start(f32[368,128]{1,0:T(8,128)S(1)} %get-tuple-element.29), channel_id=1, source_target_pairs={{16,32},{32,16},{48,64},{64,48},{80,96},{96,80},{112,128},{128,112... | collective-permute-start | bytes 565256 | tf_op jit(solution)/shard_map/ppermute | solution.py:508
  15.7 15.6 %collective-permute-start.3 = (f32[368,128]{1,0:T(8,128)S(1)}, f32[368,128]{1,0:T(8,128)S(1)}, u32[]{:S(2)}, u32[]{:S(2)}) collective-permute-start(f32[368,128]{1,0:T(8,128)S(1)} %get-tuple-element.30), channel_id=1, source_target_pairs={{0,16},{16,0},{32,48},{48,32},{64,80},{80,64},{96,112},{112,96},{1... | collective-permute-start | bytes 565256 | tf_op jit(solution)/shard_map/ppermute | solution.py:507
  17.6 9.8 %collective-permute-start.4 = (f32[128,128]{1,0:T(8,128)S(1)}, f32[128,128]{1,0:T(8,128)S(1)}, u32[]{:S(2)}, u32[]{:S(2)}) collective-permute-start(f32[128,128]{1,0:T(8,128)S(1)} %get-tuple-element.31), channel_id=1, source_target_pairs={{32,64},{64,32},{48,80},{80,48},{96,128},{128,96},{112,144},{144,1... | collective-permute-start | bytes 196616 | tf_op jit(solution)/shard_map/ppermute | solution.py:508
  23.6 7.7 %collective-permute-start.5 = (f32[128,128]{1,0:T(8,128)S(1)}, f32[128,128]{1,0:T(8,128)S(1)}, u32[]{:S(2)}, u32[]{:S(2)}) collective-permute-start(f32[128,128]{1,0:T(8,128)S(1)} %get-tuple-element.32), channel_id=1, source_target_pairs={{0,32},{32,0},{16,48},{48,16},{64,96},{96,64},{80,112},{112,80},{1... | collective-permute-start | bytes 196616 | tf_op jit(solution)/shard_map/ppermute | solution.py:507

commit v6 on v5

--- a/solution.py
+++ b/solution.py
@@ -158,14 +158,17 @@
 
 def permuted(x, matrix):
     rows = x.shape[0]
-    high = x.astype(jnp.bfloat16)
-    rest = x - high.astype(jnp.float32)
-    middle = rest.astype(jnp.bfloat16)
-    last = (rest - middle.astype(jnp.float32)).astype(jnp.bfloat16)
-    out = jnp.dot(
-        jnp.concatenate([high, middle, last], 0), matrix, preferred_element_type=jnp.float32
-    )
-    return (out[:rows] + out[rows : 2 * rows]) + out[2 * rows :]
+    high = x.astype(jnp.bfloat16).astype(jnp.float32)
+    rest = x - high
+    middle = rest.astype(jnp.bfloat16).astype(jnp.float32)
+    pieces = [high, middle, rest - middle]
+    if rows % 16:
+        pieces.append(jnp.zeros((-3 * rows % 16, x.shape[1]), jnp.float32))
+        pieces = [jnp.concatenate(pieces, 0).astype(jnp.bfloat16)]
+    else:
+        pieces = [jnp.concatenate([piece.astype(jnp.bfloat16) for piece in pieces], 0)]
+    out = jnp.dot(pieces[0], matrix, preferred_element_type=jnp.float32)
+    return (out[:rows] + out[rows : 2 * rows]) + out[2 * rows : 3 * rows]
 
 
 def picked(x, index):
@@ -352,27 +355,109 @@
     return forward_lift(*halves_of(ref, t, tall), neighbours(0, starts, stops))
 
 
-def forward_part(limits, own_low, own_high, near_sides, far_sides, outs, refs):
-    l_ref, h_ref, ll_ref, lh_ref, f_ref, g_ref, b_ref = refs
-    (above, under), (above_far, under_far) = near_sides, far_sides
-    row, count = lax.axis_index("rows"), lax.axis_size("rows")
-    _, left_end, right_end = ends("cols")
+def across(level, low, high):
+    _, at_start, at_end = ends("cols")
+    halves = lift_lanes(low, high, EDGE[level], 1024 >> level, at_start, at_end, inverse=True)
+    return merge_pairs(*halves)
+
+
+def split_lanes(level, band):
+    _, at_start, at_end = ends("cols")
+    wide = WIDE[level]
+    pad = jnp.zeros((band.shape[0], 2 * wide - band.shape[1]), jnp.float32)
+    halves = split_pairs(jnp.concatenate([band, pad], 1))
+    return lift_lanes(*halves, EDGE[level], 1024 >> level, at_start, at_end)
+
+
+def limited(limits, level, kind, coeffs):
+    at = 3 * level + kind
+    return soften(coeffs, limits[at : at + 1, :])
+
+
+def near_kernel(
+    limits, own_low, own_high, own_low_low, own_low_high, odd_ref, even_ref,
+    hl0_ref, vh0_ref, hl1_ref, vh1_ref, hl2_ref, vh2_ref, next_ref,
+    l_ref, h_ref, b_ref, x_ref, lh_ref, hh_ref,
+):
+    above, under = sides(lax.axis_index("rows") % 2 == 0, odd_ref, even_ref)
     for t in range(WIDE[1] // 128):
-        at, far = PIECE * t, FAR_PIECE * t
+        at = PIECE * t
         s = slice(128 * t, 128 * t + 128)
 
         def part(offset, size=8, at=at):
             return slice(at + offset, at + offset + size)
 
-        def far_part(offset, size=8, far=far):
-            return slice(far + offset, far + offset + size)
-
-        ll_ref[t, 0:8], ll_ref[t, 8:72], ll_ref[t, 72:80] = above(part(8)), own_low[t], under(part(0))
-        lh_ref[t, 0:8], lh_ref[t, 8:72], lh_ref[t, 72:80] = above(part(42)), own_high[t], under(part(42))
-        l_ref[t, 8:48] = lifted(ll_ref, t, 40, 4, 32)[0]
+        x_ref[0, 0:8], x_ref[0, 8:72], x_ref[0, 72:80] = above(part(8)), own_low_low[t], under(part(0))
+        x_ref[1, 0:8], x_ref[1, 8:72], x_ref[1, 72:80] = above(part(42)), own_low_high[t], under(part(42))
+        l_ref[t, 8:48] = lifted(x_ref, 0, 40, 4, 32)[0]
         l_ref[t, 2:10], l_ref[t, 46:54] = above(part(24)), under(part(16))
-        h_ref[t, 8:48] = lifted(lh_ref, t, 40, 4, 32)[0]
+        h_ref[t, 8:48] = lifted(x_ref, 1, 40, 4, 32)[0]
         h_ref[t, 2:10], h_ref[t, 46:54] = above(part(50)), under(part(50))
+        low, high = lifted(l_ref, t, 32, 6, 16)
+        lh_ref[0:24, s] = limited(limits, 1, 1, high[2:26])
+        b_ref[3:13, s], b_ref[13:35, s], b_ref[35:45, s] = above(part(32, 10)), low[3:25], under(part(32, 10))
+        low, high = lifted(h_ref, t, 32, 6, 16)
+        hl1_ref[:, s] = limited(limits, 1, 0, low[2:26])
+        hh_ref[0:24, s] = limited(limits, 1, 2, high[2:26])
+    vh1_ref[...] = across(1, lh_ref[0:24, :640], hh_ref[0:24, :640])[:, :1152]
+    low, high = split_lanes(2, b_ref[...])
+    spread(next_ref, slice(None), low)
+    spread(h_ref, slice(0, 48), high)
+    for t in range(WIDE[2] // 128):
+        s = slice(128 * t, 128 * t + 128)
+        high = lifted(next_ref, t, 24, 8, 8)[1]
+        lh_ref[0:16, s] = limited(limits, 2, 1, high[4:20])
+        low, high = lifted(h_ref, t, 24, 8, 8)
+        hl2_ref[:, s] = limited(limits, 2, 0, low[4:20])
+        hh_ref[0:16, s] = limited(limits, 2, 2, high[4:20])
+    vh2_ref[...] = across(2, lh_ref[0:16, :384], hh_ref[0:16, :384])[:, :640]
+    low, high = (
+        jnp.concatenate(
+            [
+                jnp.concatenate([side(slice(PIECE * t + at, PIECE * t + at + 8)) for t in range(5)], 1)
+                for side, at in sources
+            ],
+            0,
+        )
+        for sources in (((above, 8), (under, 0)), ((above, 42), (under, 42)))
+    )
+    lows = across(1, low, high)
+    for j in range(9):
+        x_ref[j, 0:8] = lows[0:8, 128 * j : 128 * j + 128]
+        x_ref[j, 8:72] = own_low[j]
+        x_ref[j, 72:80] = lows[8:16, 128 * j : 128 * j + 128]
+        at = slice(EDGES + 8 * j, EDGES + 8 * j + 8)
+        x_ref[j + 9, 0:8] = above(at)
+        x_ref[j + 9, 8:72] = own_high[j]
+        x_ref[j + 9, 72:80] = under(at)
+
+    def lift(t, s):
+        high = lifted(x_ref, t, 40, 4, 32)[1]
+        lh_ref[:, s] = limited(limits, 0, 1, high)
+        low, high = lifted(x_ref, t + 9, 40, 4, 32)
+        hl0_ref[:, s] = limited(limits, 0, 0, low)
+        hh_ref[:, s] = limited(limits, 0, 2, high)
+
+    tiles(WIDE[0], lift)
+    vh0_ref[...] = across(0, lh_ref[...], hh_ref[...])[:, 128 : 128 + COLS]
+
+
+def far_kernel(
+    limits, hl0_ref, vh0_ref, hl1_ref, vh1_ref, hl2_ref, vh2_ref, next_ref,
+    odd_ref, even_ref, odd_far, even_far, out_ref, f_ref, g_ref, l_ref, h_ref, b_ref, v_ref, r_ref, o_ref,
+):
+    row, count = lax.axis_index("rows"), lax.axis_size("rows")
+    above, under = sides(row % 2 == 0, odd_ref, even_ref)
+    above_far, under_far = sides(row % 4 < 2, odd_far, even_far)
+    for t in range(WIDE[1] // 128):
+        s = slice(128 * t, 128 * t + 128)
+
+        def part(offset, at=PIECE * t):
+            return slice(at + offset, at + offset + 8)
+
+        def far_part(offset, size=8, at=FAR_PIECE * t):
+            return slice(at + offset, at + offset + size)
+
         f_ref[t, 0:8], f_ref[t, 8:16] = above_far(far_part(0)), above(part(0))
         f_ref[t, 16:24], f_ref[t, 24:32] = under(part(8)), under_far(far_part(0))
         near = neighbours(0, [(4, row == 1)], [(11, row == count - 2)])
@@ -382,116 +467,54 @@
         g_ref[t, 34:42], g_ref[t, 46:54] = under(part(24)), under_far(far_part(8))
         near = neighbours(0, [(6, row == 1)], [(21, row == count - 2)])
         two = forward_lift(*halves_of(g_ref, t, 32), near)[0]
-        b_ref[0:9, s], b_ref[9:15, s], b_ref[15:25, s] = above_far(far_part(16, 9)), two[3:9], above(part(32, 10))
-        b_ref[47:57, s], b_ref[57:63, s], b_ref[63:72, s] = under(part(32, 10)), two[19:25], under_far(far_part(16, 9))
-
-    def keep(level, kind, s, coeffs, begin):
-        coeffs = coeffs[begin - 4 : begin + OWN[level] + 4]
-        if kind < 3:
-            at = 3 * level + kind
-            coeffs = soften(coeffs, limits[at : at + 1, :])
-        outs[3 * level + kind][0 : OWN[level] + 8, s] = coeffs
-
-    for level in (1, 2, 3):
-        own = OWN[level]
-        tall, begin = ((32, 6), (40, 14), (16, 6))[level - 1]
-        if level > 1:
-            rows, known, wide = (72, 32)[level - 2], WIDE[level - 1], WIDE[level]
-            b_ref[0:rows, known : 2 * wide] = jnp.zeros((rows, 2 * wide - known), jnp.float32)
-            halves = split_pairs(b_ref[0:rows, : 2 * wide])
-            low, high = lift_lanes(*halves, EDGE[level], 1024 >> level, left_end, right_end)
-            spread(l_ref, slice(0, rows), low)
-            spread(h_ref, slice(0, rows), high)
-        for t in range(WIDE[level] // 128):
-            s = slice(128 * t, 128 * t + 128)
-            low, high = lifted(l_ref, t, tall, begin, own)
-            keep(level, 1, s, high, begin)
-            if level == 1:
-                b_ref[25:47, s] = low[3:25]
-            elif level == 2:
-                b_ref[0:32, s] = low[2:34]
-            else:
-                keep(level, 3, s, low, begin)
-            low, high = lifted(h_ref, t, tall, begin, own)
-            keep(level, 0, s, low, begin)
-            keep(level, 2, s, high, begin)
-
-
-def detail_part(limits, own_low, own_high, near_sides, outs, x_ref):
-    above, under = near_sides
-    _, at_start, at_end = ends("cols")
-    low, high = (
-        jnp.concatenate(
-            [
-                jnp.concatenate([side(slice(PIECE * t + at, PIECE * t + at + 8)) for t in range(5)], 1)
-                for side, at in sources
-            ],
-            0,
-        )
-        for sources in (((above, 8), (under, 0)), ((above, 42), (under, 42)))
-    )
-    lows = merge_pairs(*lift_lanes(low, high, EDGE[1], 512, at_start, at_end, inverse=True))
-    for j in range(9):
-        x_ref[j, 0:8] = lows[0:8, 128 * j : 128 * j + 128]
-        x_ref[j, 8:72] = own_low[j]
-        x_ref[j, 72:80] = lows[8:16, 128 * j : 128 * j + 128]
-        at = slice(EDGES + 8 * j, EDGES + 8 * j + 8)
-        x_ref[j + 9, 0:8] = above(at)
-        x_ref[j + 9, 8:72] = own_high[j]
-        x_ref[j + 9, 72:80] = under(at)
-
-    def lift(t, s):
-        high = lifted(x_ref, t, 40, 4, 32)[1]
-        outs[1][:, s] = soften(high, limits[1:2, :])
-        low, high = lifted(x_ref, t + 9, 40, 4, 32)
-        outs[0][:, s] = soften(low, limits[0:1, :])
-        outs[2][:, s] = soften(high, limits[2:3, :])
-
-    tiles(WIDE[0], lift)
-
-
-def inverse_part(ins, out_ref, v_ref, w_ref, r_ref):
+        b_ref[0:9, s], b_ref[9:15, s] = above_far(far_part(16, 9)), two[3:9]
+        b_ref[16:22, s], b_ref[22:31, s] = two[19:25], under_far(far_part(16, 9))
+    low = split_lanes(2, b_ref[0:32, :640])[0]
+    for t in range(WIDE[2] // 128):
+        s = slice(128 * t, 128 * t + 128)
+        l_ref[t, 0:15], l_ref[t, 15:57], l_ref[t, 57:72] = low[0:15, s], next_ref[t, 3:45], low[16:31, s]
+        b_ref[0:32, s] = lifted(l_ref, t, 40, 14, 8)[0][2:34]
+    low, high = split_lanes(3, b_ref[0:32, :384])
+    spread(l_ref, slice(0, 32), low)
+    spread(h_ref, slice(0, 32), high)
+    for t in range(WIDE[3] // 128):
+        s = slice(128 * t, 128 * t + 128)
+        low, high = lifted(l_ref, t, 16, 6, 4)
+        v_ref[0:12, s] = low[2:14]
+        v_ref[16:28, s] = limited(limits, 3, 1, high[2:14])
+        low, high = lifted(h_ref, t, 16, 6, 4)
+        r_ref[0:12, s] = limited(limits, 3, 0, low[2:14])
+        r_ref[16:28, s] = limited(limits, 3, 2, high[2:14])
+    both = across(3, v_ref[0:32, :256], r_ref[0:32, :256])[:, :384]
+    low, high = both[0:16], both[16:32]
     _, at_start, at_end = ends("rows")
-    _, left_end, right_end = ends("cols")
-    for level in range(LEVELS - 1, -1, -1):
+    for level in (3, 2, 1):
         own = OWN[level]
         long = max(own + 8, 16)
         near = neighbours(0, [(4, at_start)], [(3 + own, at_end)])
-        hl, lh, hh = ins[3 * level : 3 * level + 3]
-
-        def lift_down(t, s, level=level, long=long, near=near, hl=hl, lh=lh, hh=hh):
-            low = ins[12][0:long, s] if level == LEVELS - 1 else r_ref[4 : 4 + long, s]
-            even, odd = inverse_lift(low, lh[0:long, s], near)
-            v_ref[t, pl.ds(0, long, stride=2)] = even
-            v_ref[t, pl.ds(1, long, stride=2)] = odd
-            even, odd = inverse_lift(hl[0:long, s], hh[0:long, s], near)
-            w_ref[t, pl.ds(0, long, stride=2)] = even
-            w_ref[t, pl.ds(1, long, stride=2)] = odd
-
-        wide = WIDE[level]
-        tiles(wide, lift_down)
-        first, rows = (8, 64) if level == 0 else (0, 2 * long)
-        cut = slice(first, first + rows)
-        even, odd = joined(v_ref, cut, wide), joined(w_ref, cut, wide)
-        both = merge_pairs(
-            *lift_lanes(even, odd, EDGE[level], 1024 >> level, left_end, right_end, inverse=True)
-        )
-        if level:
-            r_ref[0:rows, : 2 * wide] = both
-        else:
-            out_ref[...] = both[:, 128 : 128 + COLS]
-
-
-def rows_kernel(
-    limits, own_low, own_high, own_low_low, own_low_high, odd_ref, even_ref, odd_far, even_far, out_ref, *refs
-):
-    bands, refs = refs[:13], refs[13:]
-    row = lax.axis_index("rows")
-    near_sides = sides(row % 2 == 0, odd_ref, even_ref)
-    far_sides = sides(row % 4 < 2, odd_far, even_far)
-    forward_part(limits, own_low_low, own_low_high, near_sides, far_sides, bands, refs[:7])
-    detail_part(limits, own_low, own_high, near_sides, bands, refs[7])
-    inverse_part(bands, out_ref, *refs[8:])
+        for t in range(low.shape[1] // 128):
+            s = slice(128 * t, 128 * t + 128)
+            even, odd = inverse_lift(low[0:long, s], high[0:long, s], near)
+            o_ref[t, pl.ds(0, long, stride=2)] = even
+            o_ref[t, pl.ds(1, long, stride=2)] = odd
+        size = OWN[level - 1] + 8
+        low = joined(o_ref, slice(4, 4 + size), low.shape[1])
+        hl, high = ((hl0_ref, vh0_ref), (hl1_ref, vh1_ref), (hl2_ref, vh2_ref))[level - 1]
+        low = across(level - 1, low, hl[...])
+        low = low[:, 128 : 128 + COLS] if level == 1 else low[:, : high.shape[1]]
+    v_ref[...] = low
+    near = neighbours(0, [(4, at_start)], [(35, at_end)])
+
+    def finish(i, carry):
+        for t in (2 * i, 2 * i + 1):
+            s = pl.ds(pl.multiple_of(128 * t, 128), 128)
+            even, odd = inverse_lift(v_ref[:, s], vh0_ref[:, s], near)
+            o_ref[t, pl.ds(0, 40, stride=2)] = even
+            o_ref[t, pl.ds(1, 40, stride=2)] = odd
+            out_ref[:, s] = o_ref[t, 8:72]
+        return carry
+
+    lax.fori_loop(0, COLS // 256, finish, 0)
 
 
 def swaps(axis, offset, apart):
@@ -558,19 +581,27 @@
         odd,
         even,
     )
-    received = exchange(for_even, for_odd, "rows")
-    received += exchange(for_even_far, for_odd_far, "rows", 2)
-    bands = [scratch(max(OWN[level] + 8, 16), WIDE[level]) for level in range(LEVELS) for _ in range(3)]
-    return call(
-        rows_kernel,
-        f32(ROWS, COLS),
-        [*bands, bands[-1]]
-        + [scratch(5, 80, 128), scratch(5, 80, 128), scratch(5, 80, 128), scratch(5, 80, 128)]
-        + [scratch(5, 32, 128), scratch(5, 64, 128), scratch(72, 768), scratch(18, 80, 128)]
-        + [scratch(9, 80, 128), scratch(9, 80, 128), scratch(48, 1280)],
+    near = exchange(for_even, for_odd, "rows")
+    far = exchange(for_even_far, for_odd_far, "rows", 2)
+    known = call(
+        near_kernel,
+        (f32(40, 1152), f32(40, COLS), f32(24, 640), f32(24, 1152), f32(16, 384), f32(16, 640), f32(3, 48, 128)),
+        [scratch(5, 64, 128), scratch(5, 64, 128), scratch(48, 640), scratch(18, 80, 128)]
+        + [scratch(40, 1152), scratch(40, 1152)],
         limits,
         *own,
-        *received,
+        *near,
+        cost=pl.CostEstimate(flops=2 * 10**9, bytes_accessed=4 * 10**6, transcendentals=0),
+    )
+    return call(
+        far_kernel,
+        f32(ROWS, COLS),
+        [scratch(5, 32, 128), scratch(5, 64, 128), scratch(3, 80, 128), scratch(3, 80, 128)]
+        + [scratch(32, 640), scratch(40, COLS), scratch(32, 256), scratch(16, 80, 128)],
+        limits,
+        *known,
+        *near,
+        *far,
     )
 
 

time: 36.6 us -> 35.1 us (0.959)
  waiting for transfers between devices: 5.75 us -> 3.32 us
  Pallas kernels: 7.35 us -> 8.17 us
    ppermute x3, waiting for transfers between devices: 1.83 us -> 0.01 us  [exchange(): odd = lax.ppermute(for_odd, axis, swaps(axis, apart, apart))]
    pallas_call x4 -> x5, Pallas kernels: 7.35 us -> 8.17 us  [call(): pl.pallas_call(kernel, out_shape=outs, in_specs=[smem] * scalars + [pl.Bl...]
    ppermute x3, waiting for transfers between devices: 3.91 us -> 3.31 us  [exchange(): even = lax.ppermute(for_even, axis, swaps(axis, 0, apart))]
  transfers between devices with their start and end apart: 6 -> 6, of which waited for: 2 -> 1; matrix products, arithmetic and copies ran while one was open for 0% -> 0% of each run, Pallas kernels for 3% -> 10%
where the time goes in v6:
time: 35.1 us; the launch traced here: 34.8 us
  starting transfers between devices  22.1 us (63%)
  Pallas kernels  8.17 us (23%)
  waiting for transfers between devices  3.32 us (9%)
  local copies, waits for them, and re-layouts  1.05 us (3%)
    ppermute x3, starting transfers between devices, exchange(): odd = lax.ppermute(for_odd, axis, swaps(axis, apart, apart))  12.7 us
    ppermute x3, starting transfers between devices, exchange(): even = lax.ppermute(for_even, axis, swaps(axis, 0, apart))  9.44 us
    pallas_call x5, Pallas kernels, call(): pl.pallas_call(kernel, out_shape=outs, in_specs=[smem] * scalars + [pl.Bl...  8.17 us
    ppermute x3, waiting for transfers between devices, exchange(): even = lax.ppermute(for_even, axis, swaps(axis, 0, apart))  3.31 us
    unnamed x6, local copies, waits for them, and re-layouts  1.05 us
  transfers between devices with their start and end apart: 6, of which 1 were waited for; matrix products, arithmetic and copies ran while one was open for 0% of the time, Pallas kernels for 10%

profile of v6, /device:TPU:222, one launch (start us, length us, event | category | flops | bytes accessed | tf_op | source)
XLA Modules:
  0.0 34.8 jit_solution(2796059338700959992)
XLA Ops:
  0.0 0.0 copy-start
  0.0 1.0 %copy-done = f32[64,2048]{1,0:T(8,128)S(1)} copy-done((f32[64,2048]{1,0:T(8,128)S(1)}, f32[64,2048]{1,0:T(8,128)}, u32[]{:S(2)}) %copy-start) | copy-done | bytes 524312
  1.0 0.0 copy-start.1
  1.1 0.0 copy-start.2
  1.1 2.1 %collective-permute-start = (f32[64,128]{1,0:T(8,128)S(1)}, f32[64,128]{1,0:T(8,128)S(1)}, u32[]{:S(2)}, u32[]{:S(2)}) collective-permute-start(f32[64,128]{1,0:T(8,128)S(1)} %get-tuple-element.30), channel_id=1, source_target_pairs={{1,2},{2,1},{3,4},{4,3},{5,6},{6,5},{7,8},{8,7},{9,10},{10,9},{11,... | collective-permute-start | bytes 98312 | tf_op jit(solution)/shard_map/ppermute | solution.py:531
  3.2 5.6 %collective-permute-start.1 = (f32[64,128]{1,0:T(8,128)S(1)}, f32[64,128]{1,0:T(8,128)S(1)}, u32[]{:S(2)}, u32[]{:S(2)}) collective-permute-start(f32[64,128]{1,0:T(8,128)S(1)} %get-tuple-element.31), channel_id=1, source_target_pairs={{0,1},{1,0},{2,3},{3,2},{4,5},{5,4},{6,7},{7,6},{8,9},{9,8},{10,11... | collective-permute-start | bytes 98312 | tf_op jit(solution)/shard_map/ppermute | solution.py:530
  8.8 0.0 copy-done.1
  8.8 0.0 copy-done.2
  8.8 0.9 %shard_map.28 = (f32[64,896]{1,0:T(8,128)S(1)}, f32[64,896]{1,0:T(8,128)S(1)}, f32[64,256]{1,0:T(8,128)S(1)}, f32[16,128]{1,0:T(8,128)S(1)}) custom-call(f32[4,3]{1,0:T(4,128)S(1)} %copy-done.2, f32[64,2048]{1,0:T(8,128)S(1)} %copy-done.1), custom_call_target="tpu_custom_call" | custom-call | flops 2000000000 | bytes 4000000 | tf_op jit(solution)/shard_map/pallas_call | solution.py:546
  9.7 0.0 collective-permute-done.odd_ref
  9.7 0.0 collective-permute-done.1.even_ref
  9.7 1.3 %shard_map.30 = (f32[368,128]{1,0:T(8,128)S(1)}, f32[368,128]{1,0:T(8,128)S(1)}, f32[128,128]{1,0:T(8,128)S(1)}, f32[128,128]{1,0:T(8,128)S(1)}, f32[9,64,128]{2...) custom-call(f32[64,896]{1,0:T(8,128)S(1)} %get-tuple-element.27.e_ref, ...), custom_call_target="tpu_custom_call" | custom-call | tf_op jit(solution)/shard_map/pallas_call | solution.py:546
  11.1 4.6 %collective-permute-start.2 = (f32[368,128]{1,0:T(8,128)S(1)}, f32[368,128]{1,0:T(8,128)S(1)}, u32[]{:S(2)}, u32[]{:S(2)}) collective-permute-start(f32[368,128]{1,0:T(8,128)S(1)} %get-tuple-element.36), channel_id=1, source_target_pairs={{16,32},{32,16},{48,64},{64,48},{80,96},{96,80},{112,128},{128,112... | collective-permute-start | bytes 565256 | tf_op jit(solution)/shard_map/ppermute | solution.py:531
  15.7 1.9 %collective-permute-start.3 = (f32[368,128]{1,0:T(8,128)S(1)}, f32[368,128]{1,0:T(8,128)S(1)}, u32[]{:S(2)}, u32[]{:S(2)}) collective-permute-start(f32[368,128]{1,0:T(8,128)S(1)} %get-tuple-element.37), channel_id=1, source_target_pairs={{0,16},{16,0},{32,48},{48,32},{64,80},{80,64},{96,112},{112,96},{1... | collective-permute-start | bytes 565256 | tf_op jit(solution)/shard_map/ppermute | solution.py:530
  17.6 6.0 %collective-permute-start.4 = (f32[128,128]{1,0:T(8,128)S(1)}, f32[128,128]{1,0:T(8,128)S(1)}, u32[]{:S(2)}, u32[]{:S(2)}) collective-permute-start(f32[128,128]{1,0:T(8,128)S(1)} %get-tuple-element.45), channel_id=1, source_target_pairs={{32,64},{64,32},{48,80},{80,48},{96,128},{128,96},{112,144},{144,1... | collective-permute-start | bytes 196616 | tf_op jit(solution)/shard_map/ppermute | solution.py:531
  23.6 1.9 %collective-permute-start.5 = (f32[128,128]{1,0:T(8,128)S(1)}, f32[128,128]{1,0:T(8,128)S(1)}, u32[]{:S(2)}, u32[]{:S(2)}) collective-permute-start(f32[128,128]{1,0:T(8,128)S(1)} %get-tuple-element.46), channel_id=1, source_target_pairs={{0,32},{32,0},{16,48},{48,16},{64,96},{96,64},{80,112},{112,80},{1... | collective-permute-start | bytes 196616 | tf_op jit(solution)/shard_map/ppermute | solution.py:530
  25.6 0.0 collective-permute-done.2.odd_ref
  25.6 0.0 collective-permute-done.3.even_ref
  25.6 2.4 %shard_map.31 = (f32[40,1152]{1,0:T(8,128)S(1)}, f32[40,2048]{1,0:T(8,128)S(1)}, f32[24,640]{1,0:T(8,128)S(1)}, f32[24,1152]{1,0:T(8,128)S(1)}, f32[16,384]{1,0:...) custom-call(f32[16,128]{1,0:T(8,128)S(1)} %get-tuple-element.26.limits, ...), custom_call_target="tpu_custom_call" | custom-call | flops 2000000000 | bytes 4000000 | tf_op jit(solution)/shard_map/pallas_call | solution.py:546
  28.0 0.0 collective-permute-done.4.odd_far
  28.0 3.3 %collective-permute-done.5.even_far = f32[128,128]{1,0:T(8,128)S(1)} collective-permute-done((f32[128,128]{1,0:T(8,128)S(1)}, f32[128,128]{1,0:T(8,128)S(1)}, u32[]{:S(2)}, u32[]{:S(2)}) %collective-permute-start.5) | collective-permute-done | bytes 65568 | tf_op jit(solution)/shard_map/ppermute | solution.py:530
  31.3 3.5 %shard_map.32 = f32[64,2048]{1,0:T(8,128)} custom-call(f32[16,128]{1,0:T(8,128)S(1)} %get-tuple-element.26.limits, f32[40,1152]{1,0:T(8,128)S(1)} %get-tuple-element.38.hl0_ref, f32[40,2048]{1,0:T(8,128)S(1)} %get-tuple-element.39.vh0_ref, f32[24,640]{1,0:T(8,128)S(1)} %get-tuple-element.40.hl1_ref, f32[24,1152]{1,0:T(8,128)S(1)} %get-tuple-element.41.vh1_ref, ...), custom_call_target="tpu_custom_call" | custom-call | tf_op jit(solution)/shard_map/pallas_call | solution.py:546
  (1 shorter events, 0.0 us)
Async XLA Ops:
  0.0 1.0 %copy-start = (f32[64,2048]{1,0:T(8,128)S(1)}, f32[64,2048]{1,0:T(8,128)}, u32[]{:S(2)}) copy-start(f32[64,2048]{1,0:T(8,128)} %x_ref.3) | copy-start | bytes 1572868
  1.0 7.7 %copy-start.1 = (f32[64,2048]{1,0:T(8,128)S(1)}, f32[64,2048]{1,0:T(8,128)}, u32[]{:S(2)}) copy-start(f32[64,2048]{1,0:T(8,128)} %x_ref.3) | copy-start | bytes 1572868
  1.1 7.7 %copy-start.2 = (f32[4,3]{1,0:T(4,128)S(1)}, f32[4,3]{1,0:T(4,128)}, u32[]{:S(2)}) copy-start(f32[4,3]{1,0:T(4,128)} %t_ref.1) | copy-start | bytes 148
  1.1 8.6 %collective-permute-start = (f32[64,128]{1,0:T(8,128)S(1)}, f32[64,128]{1,0:T(8,128)S(1)}, u32[]{:S(2)}, u32[]{:S(2)}) collective-permute-start(f32[64,128]{1,0:T(8,128)S(1)} %get-tuple-element.30), channel_id=1, source_target_pairs={{1,2},{2,1},{3,4},{4,3},{5,6},{6,5},{7,8},{8,7},{9,10},{10,9},{11,... | collective-permute-start | bytes 98312 | tf_op jit(solution)/shard_map/ppermute | solution.py:531
  3.2 6.6 %collective-permute-start.1 = (f32[64,128]{1,0:T(8,128)S(1)}, f32[64,128]{1,0:T(8,128)S(1)}, u32[]{:S(2)}, u32[]{:S(2)}) collective-permute-start(f32[64,128]{1,0:T(8,128)S(1)} %get-tuple-element.31), channel_id=1, source_target_pairs={{0,1},{1,0},{2,3},{3,2},{4,5},{5,4},{6,7},{7,6},{8,9},{9,8},{10,11... | collective-permute-start | bytes 98312 | tf_op jit(solution)/shard_map/ppermute | solution.py:530
  11.1 14.5 %collective-permute-start.2 = (f32[368,128]{1,0:T(8,128)S(1)}, f32[368,128]{1,0:T(8,128)S(1)}, u32[]{:S(2)}, u32[]{:S(2)}) collective-permute-start(f32[368,128]{1,0:T(8,128)S(1)} %get-tuple-element.36), channel_id=1, source_target_pairs={{16,32},{32,16},{48,64},{64,48},{80,96},{96,80},{112,128},{128,112... | collective-permute-start | bytes 565256 | tf_op jit(solution)/shard_map/ppermute | solution.py:531
  15.7 9.9 %collective-permute-start.3 = (f32[368,128]{1,0:T(8,128)S(1)}, f32[368,128]{1,0:T(8,128)S(1)}, u32[]{:S(2)}, u32[]{:S(2)}) collective-permute-start(f32[368,128]{1,0:T(8,128)S(1)} %get-tuple-element.37), channel_id=1, source_target_pairs={{0,16},{16,0},{32,48},{48,32},{64,80},{80,64},{96,112},{112,96},{1... | collective-permute-start | bytes 565256 | tf_op jit(solution)/shard_map/ppermute | solution.py:530
  17.6 10.4 %collective-permute-start.4 = (f32[128,128]{1,0:T(8,128)S(1)}, f32[128,128]{1,0:T(8,128)S(1)}, u32[]{:S(2)}, u32[]{:S(2)}) collective-permute-start(f32[128,128]{1,0:T(8,128)S(1)} %get-tuple-element.45), channel_id=1, source_target_pairs={{32,64},{64,32},{48,80},{80,48},{96,128},{128,96},{112,144},{144,1... | collective-permute-start | bytes 196616 | tf_op jit(solution)/shard_map/ppermute | solution.py:531
  23.6 7.7 %collective-permute-start.5 = (f32[128,128]{1,0:T(8,128)S(1)}, f32[128,128]{1,0:T(8,128)S(1)}, u32[]{:S(2)}, u32[]{:S(2)}) collective-permute-start(f32[128,128]{1,0:T(8,128)S(1)} %get-tuple-element.46), channel_id=1, source_target_pairs={{0,32},{32,0},{16,48},{48,16},{64,96},{96,64},{80,112},{112,80},{1... | collective-permute-start | bytes 196616 | tf_op jit(solution)/shard_map/ppermute | solution.py:530

commit v7 on v6

--- a/solution.py
+++ b/solution.py
@@ -444,7 +444,7 @@
 
 def far_kernel(
     limits, hl0_ref, vh0_ref, hl1_ref, vh1_ref, hl2_ref, vh2_ref, next_ref,
-    odd_ref, even_ref, odd_far, even_far, out_ref, f_ref, g_ref, l_ref, h_ref, b_ref, v_ref, r_ref, o_ref,
+    odd_ref, even_ref, even_far, odd_far, out_ref, f_ref, g_ref, l_ref, h_ref, b_ref, v_ref, r_ref, o_ref, sems,
 ):
     row, count = lax.axis_index("rows"), lax.axis_size("rows")
     above, under = sides(row % 2 == 0, odd_ref, even_ref)
@@ -511,10 +511,13 @@
             even, odd = inverse_lift(v_ref[:, s], vh0_ref[:, s], near)
             o_ref[t, pl.ds(0, 40, stride=2)] = even
             o_ref[t, pl.ds(1, 40, stride=2)] = odd
-            out_ref[:, s] = o_ref[t, 8:72]
+            pltpu.make_async_copy(o_ref.at[t, 8:72], out_ref.at[:, s], sems.at[t]).start()
         return carry
 
     lax.fori_loop(0, COLS // 256, finish, 0)
+    for t in range(COLS // 128):
+        lanes = slice(128 * t, 128 * t + 128)
+        pltpu.make_async_copy(o_ref.at[t, 8:72], out_ref.at[:, lanes], sems.at[t]).wait()
 
 
 def swaps(axis, offset, apart):
@@ -540,14 +543,14 @@
     return pltpu.VMEM(shape, jnp.float32)
 
 
-def call(kernel, outs, scratches, *args, scalars=0, space=pltpu.VMEM, cost=None):
+def call(kernel, outs, scratches, *args, scalars=0, space=pltpu.VMEM, out_space=pltpu.VMEM, cost=None):
     vmem = pl.BlockSpec(memory_space=pltpu.VMEM)
     smem = pl.BlockSpec(memory_space=pltpu.SMEM)
     return pl.pallas_call(
         kernel,
         out_shape=outs,
         in_specs=[smem] * scalars + [pl.BlockSpec(memory_space=space)] * (len(args) - scalars),
-        out_specs=jax.tree.map(lambda _: vmem, outs),
+        out_specs=jax.tree.map(lambda _: pl.BlockSpec(memory_space=out_space), outs),
         scratch_shapes=scratches,
         compiler_params=pltpu.CompilerParams(vmem_limit_bytes=16 * 2**20),
         cost_estimate=cost,
@@ -597,11 +600,14 @@
         far_kernel,
         f32(ROWS, COLS),
         [scratch(5, 32, 128), scratch(5, 64, 128), scratch(3, 80, 128), scratch(3, 80, 128)]
-        + [scratch(32, 640), scratch(40, COLS), scratch(32, 256), scratch(16, 80, 128)],
+        + [scratch(32, 640), scratch(40, COLS), scratch(32, 256), scratch(16, 80, 128)]
+        + [pltpu.SemaphoreType.DMA((16,))],
         limits,
         *known,
         *near,
-        *far,
+        far[1],
+        far[0],
+        out_space=pl.ANY,
     )
 
 

time: 35.1 us -> 36 us (1.026)
  the two profiles are of different devices: /device:TPU:222 before, /device:TPU:216 now
where the time goes in v7:
time: 36 us; the launch traced here: 35.7 us
  starting transfers between devices  22.2 us (62%)
  Pallas kernels  8.09 us (22%)
  waiting for transfers between devices  4.22 us (12%)
  local copies, waits for them, and re-layouts  1.05 us (3%)
    ppermute x3, starting transfers between devices, exchange(): even = lax.ppermute(for_even, axis, swaps(axis, 0, apart))  13.7 us
    ppermute x3, starting transfers between devices, exchange(): odd = lax.ppermute(for_odd, axis, swaps(axis, apart, apart))  8.52 us
    pallas_call x5, Pallas kernels, call(): pl.pallas_call(kernel, out_shape=outs, in_specs=[smem] * scalars + [pl.Bl...  8.09 us
    ppermute x3, waiting for transfers between devices, exchange(): odd = lax.ppermute(for_odd, axis, swaps(axis, apart, apart))  4.21 us
    unnamed x6, local copies, waits for them, and re-layouts  1.05 us
  transfers between devices with their start and end apart: 6, of which 1 were waited for; matrix products, arithmetic and copies ran while one was open for 0% of the time, Pallas kernels for 9%

profile of v7, /device:TPU:216, one launch (start us, length us, event | category | flops | bytes accessed | tf_op | source)
XLA Modules:
  0.0 35.7 jit_solution(14617580000255437682)
XLA Ops:
  0.0 0.0 copy-start
  0.0 1.0 %copy-done = f32[64,2048]{1,0:T(8,128)S(1)} copy-done((f32[64,2048]{1,0:T(8,128)S(1)}, f32[64,2048]{1,0:T(8,128)}, u32[]{:S(2)}) %copy-start) | copy-done | bytes 524312
  1.0 0.0 copy-start.1
  1.1 0.0 copy-start.2
  1.1 2.1 %collective-permute-start = (f32[64,128]{1,0:T(8,128)S(1)}, f32[64,128]{1,0:T(8,128)S(1)}, u32[]{:S(2)}, u32[]{:S(2)}) collective-permute-start(f32[64,128]{1,0:T(8,128)S(1)} %get-tuple-element.30), channel_id=1, source_target_pairs={{1,2},{2,1},{3,4},{4,3},{5,6},{6,5},{7,8},{8,7},{9,10},{10,9},{11,... | collective-permute-start | bytes 98312 | tf_op jit(solution)/shard_map/ppermute | solution.py:534
  3.2 5.6 %collective-permute-start.1 = (f32[64,128]{1,0:T(8,128)S(1)}, f32[64,128]{1,0:T(8,128)S(1)}, u32[]{:S(2)}, u32[]{:S(2)}) collective-permute-start(f32[64,128]{1,0:T(8,128)S(1)} %get-tuple-element.31), channel_id=1, source_target_pairs={{0,1},{1,0},{2,3},{3,2},{4,5},{5,4},{6,7},{7,6},{8,9},{9,8},{10,11... | collective-permute-start | bytes 98312 | tf_op jit(solution)/shard_map/ppermute | solution.py:533
  8.8 0.0 copy-done.1
  8.8 0.0 copy-done.2
  8.8 0.9 %shard_map.28 = (f32[64,896]{1,0:T(8,128)S(1)}, f32[64,896]{1,0:T(8,128)S(1)}, f32[64,256]{1,0:T(8,128)S(1)}, f32[16,128]{1,0:T(8,128)S(1)}) custom-call(f32[4,3]{1,0:T(4,128)S(1)} %copy-done.2, f32[64,2048]{1,0:T(8,128)S(1)} %copy-done.1), custom_call_target="tpu_custom_call" | custom-call | flops 2000000000 | bytes 4000000 | tf_op jit(solution)/shard_map/pallas_call | solution.py:549
  9.7 0.0 collective-permute-done.odd_ref
  9.7 0.0 collective-permute-done.1.even_ref
  9.7 1.3 %shard_map.30 = (f32[368,128]{1,0:T(8,128)S(1)}, f32[368,128]{1,0:T(8,128)S(1)}, f32[128,128]{1,0:T(8,128)S(1)}, f32[128,128]{1,0:T(8,128)S(1)}, f32[9,64,128]{2...) custom-call(f32[64,896]{1,0:T(8,128)S(1)} %get-tuple-element.27.e_ref, ...), custom_call_target="tpu_custom_call" | custom-call | tf_op jit(solution)/shard_map/pallas_call | solution.py:549
  11.1 4.5 %collective-permute-start.2 = (f32[368,128]{1,0:T(8,128)S(1)}, f32[368,128]{1,0:T(8,128)S(1)}, u32[]{:S(2)}, u32[]{:S(2)}) collective-permute-start(f32[368,128]{1,0:T(8,128)S(1)} %get-tuple-element.36), channel_id=1, source_target_pairs={{16,32},{32,16},{48,64},{64,48},{80,96},{96,80},{112,128},{128,112... | collective-permute-start | bytes 565256 | tf_op jit(solution)/shard_map/ppermute | solution.py:534
  15.6 2.2 %collective-permute-start.3 = (f32[368,128]{1,0:T(8,128)S(1)}, f32[368,128]{1,0:T(8,128)S(1)}, u32[]{:S(2)}, u32[]{:S(2)}) collective-permute-start(f32[368,128]{1,0:T(8,128)S(1)} %get-tuple-element.37), channel_id=1, source_target_pairs={{0,16},{16,0},{32,48},{48,32},{64,80},{80,64},{96,112},{112,96},{1... | collective-permute-start | bytes 565256 | tf_op jit(solution)/shard_map/ppermute | solution.py:533
  17.9 5.8 %collective-permute-start.4 = (f32[128,128]{1,0:T(8,128)S(1)}, f32[128,128]{1,0:T(8,128)S(1)}, u32[]{:S(2)}, u32[]{:S(2)}) collective-permute-start(f32[128,128]{1,0:T(8,128)S(1)} %get-tuple-element.45), channel_id=1, source_target_pairs={{0,32},{32,0},{16,48},{48,16},{64,96},{96,64},{80,112},{112,80},{1... | collective-permute-start | bytes 196616 | tf_op jit(solution)/shard_map/ppermute | solution.py:533
  23.8 1.9 %collective-permute-start.5 = (f32[128,128]{1,0:T(8,128)S(1)}, f32[128,128]{1,0:T(8,128)S(1)}, u32[]{:S(2)}, u32[]{:S(2)}) collective-permute-start(f32[128,128]{1,0:T(8,128)S(1)} %get-tuple-element.46), channel_id=1, source_target_pairs={{32,64},{64,32},{48,80},{80,48},{96,128},{128,96},{112,144},{144,1... | collective-permute-start | bytes 196616 | tf_op jit(solution)/shard_map/ppermute | solution.py:534
  25.7 0.0 collective-permute-done.2.odd_ref
  25.7 0.0 collective-permute-done.3.even_ref
  25.7 2.4 %shard_map.31 = (f32[40,1152]{1,0:T(8,128)S(1)}, f32[40,2048]{1,0:T(8,128)S(1)}, f32[24,640]{1,0:T(8,128)S(1)}, f32[24,1152]{1,0:T(8,128)S(1)}, f32[16,384]{1,0:...) custom-call(f32[16,128]{1,0:T(8,128)S(1)} %get-tuple-element.26.limits, ...), custom_call_target="tpu_custom_call" | custom-call | flops 2000000000 | bytes 4000000 | tf_op jit(solution)/shard_map/pallas_call | solution.py:549
  28.1 0.0 collective-permute-done.4.even_far
  28.1 4.2 %collective-permute-done.5.odd_far = f32[128,128]{1,0:T(8,128)S(1)} collective-permute-done((f32[128,128]{1,0:T(8,128)S(1)}, f32[128,128]{1,0:T(8,128)S(1)}, u32[]{:S(2)}, u32[]{:S(2)}) %collective-permute-start.5) | collective-permute-done | bytes 65568 | tf_op jit(solution)/shard_map/ppermute | solution.py:534
  32.3 3.4 %shard_map.32 = f32[64,2048]{1,0:T(8,128)} custom-call(f32[16,128]{1,0:T(8,128)S(1)} %get-tuple-element.26.limits, f32[40,1152]{1,0:T(8,128)S(1)} %get-tuple-element.38.hl0_ref, f32[40,2048]{1,0:T(8,128)S(1)} %get-tuple-element.39.vh0_ref, f32[24,640]{1,0:T(8,128)S(1)} %get-tuple-element.40.hl1_ref, f32[24,1152]{1,0:T(8,128)S(1)} %get-tuple-element.41.vh1_ref, ...), custom_call_target="tpu_custom_call" | custom-call | tf_op jit(solution)/shard_map/pallas_call | solution.py:549
  (1 shorter events, 0.0 us)
Async XLA Ops:
  0.0 1.0 %copy-start = (f32[64,2048]{1,0:T(8,128)S(1)}, f32[64,2048]{1,0:T(8,128)}, u32[]{:S(2)}) copy-start(f32[64,2048]{1,0:T(8,128)} %x_ref.3) | copy-start | bytes 1572868
  1.0 7.7 %copy-start.1 = (f32[64,2048]{1,0:T(8,128)S(1)}, f32[64,2048]{1,0:T(8,128)}, u32[]{:S(2)}) copy-start(f32[64,2048]{1,0:T(8,128)} %x_ref.3) | copy-start | bytes 1572868
  1.1 7.7 %copy-start.2 = (f32[4,3]{1,0:T(4,128)S(1)}, f32[4,3]{1,0:T(4,128)}, u32[]{:S(2)}) copy-start(f32[4,3]{1,0:T(4,128)} %t_ref.1) | copy-start | bytes 148
  1.1 8.6 %collective-permute-start = (f32[64,128]{1,0:T(8,128)S(1)}, f32[64,128]{1,0:T(8,128)S(1)}, u32[]{:S(2)}, u32[]{:S(2)}) collective-permute-start(f32[64,128]{1,0:T(8,128)S(1)} %get-tuple-element.30), channel_id=1, source_target_pairs={{1,2},{2,1},{3,4},{4,3},{5,6},{6,5},{7,8},{8,7},{9,10},{10,9},{11,... | collective-permute-start | bytes 98312 | tf_op jit(solution)/shard_map/ppermute | solution.py:534
  3.2 6.6 %collective-permute-start.1 = (f32[64,128]{1,0:T(8,128)S(1)}, f32[64,128]{1,0:T(8,128)S(1)}, u32[]{:S(2)}, u32[]{:S(2)}) collective-permute-start(f32[64,128]{1,0:T(8,128)S(1)} %get-tuple-element.31), channel_id=1, source_target_pairs={{0,1},{1,0},{2,3},{3,2},{4,5},{5,4},{6,7},{7,6},{8,9},{9,8},{10,11... | collective-permute-start | bytes 98312 | tf_op jit(solution)/shard_map/ppermute | solution.py:533
  11.1 14.6 %collective-permute-start.2 = (f32[368,128]{1,0:T(8,128)S(1)}, f32[368,128]{1,0:T(8,128)S(1)}, u32[]{:S(2)}, u32[]{:S(2)}) collective-permute-start(f32[368,128]{1,0:T(8,128)S(1)} %get-tuple-element.36), channel_id=1, source_target_pairs={{16,32},{32,16},{48,64},{64,48},{80,96},{96,80},{112,128},{128,112... | collective-permute-start | bytes 565256 | tf_op jit(solution)/shard_map/ppermute | solution.py:534
  15.6 10.0 %collective-permute-start.3 = (f32[368,128]{1,0:T(8,128)S(1)}, f32[368,128]{1,0:T(8,128)S(1)}, u32[]{:S(2)}, u32[]{:S(2)}) collective-permute-start(f32[368,128]{1,0:T(8,128)S(1)} %get-tuple-element.37), channel_id=1, source_target_pairs={{0,16},{16,0},{32,48},{48,32},{64,80},{80,64},{96,112},{112,96},{1... | collective-permute-start | bytes 565256 | tf_op jit(solution)/shard_map/ppermute | solution.py:533
  17.9 10.2 %collective-permute-start.4 = (f32[128,128]{1,0:T(8,128)S(1)}, f32[128,128]{1,0:T(8,128)S(1)}, u32[]{:S(2)}, u32[]{:S(2)}) collective-permute-start(f32[128,128]{1,0:T(8,128)S(1)} %get-tuple-element.45), channel_id=1, source_target_pairs={{0,32},{32,0},{16,48},{48,16},{64,96},{96,64},{80,112},{112,80},{1... | collective-permute-start | bytes 196616 | tf_op jit(solution)/shard_map/ppermute | solution.py:533
  23.8 8.6 %collective-permute-start.5 = (f32[128,128]{1,0:T(8,128)S(1)}, f32[128,128]{1,0:T(8,128)S(1)}, u32[]{:S(2)}, u32[]{:S(2)}) collective-permute-start(f32[128,128]{1,0:T(8,128)S(1)} %get-tuple-element.46), channel_id=1, source_target_pairs={{32,64},{64,32},{48,80},{80,48},{96,128},{128,96},{112,144},{144,1... | collective-permute-start | bytes 196616 | tf_op jit(solution)/shard_map/ppermute | solution.py:534

commit v8 on v7

--- a/solution.py
+++ b/solution.py
@@ -275,6 +275,7 @@
 def columns_kernel(
     e_ref, o_ref, edge_ref, odd_ref, even_ref, for_even, for_odd, for_even_far, for_odd_far,
     low_ref, high_ref, low_low_ref, low_high_ref, one_ref, two_ref, one_high_ref,
+    x_ref, y_ref,
 ):
     is_even, at_start, at_end = ends("cols")
     left = jnp.where(is_even, odd_ref[...], even_ref[...])
@@ -314,17 +315,23 @@
             pack[at + 50 : at + 58] = one_high_ref[t, pl.ds(2 + 20 * last, 8)]
         for j in range(9):
             pack[EDGES + 8 * j : EDGES + 8 * j + 8] = high_ref[j, pl.ds(56 * last, 8)]
+    for t in range(wide // 128):
+        s = slice(128 * t, 128 * t + 128)
+        x_ref[0:8, s], x_ref[8:16, s] = low_low_ref[t, 0:8], low_low_ref[t, 56:64]
+        x_ref[16:24, s], x_ref[24:32, s] = one_ref[t, 2:10], one_ref[t, 22:30]
+        x_ref[32:42, s] = two_ref[t, 3:13]
+    spread(y_ref, slice(None), split_lanes(2, x_ref[...])[0])
     below = (row % 4 < 2).astype(jnp.int32)
     for pack, last in ((for_even_far, below), (for_odd_far, 1 - below)):
-        for t in range(wide // 128):
+        for t in range(WIDE[2] // 128):
             at = FAR_PIECE * t
-            pack[at : at + 8] = low_low_ref[t, pl.ds(56 * last, 8)]
-            pack[at + 8 : at + 16] = one_ref[t, pl.ds(2 + 20 * last, 8)]
-            pack[at + 16 : at + 25] = two_ref[t, pl.ds(3 + last, 9)]
+            pack[at : at + 8] = y_ref[t, pl.ds(8 * last, 8)]
+            pack[at + 8 : at + 16] = y_ref[t, pl.ds(16 + 8 * last, 8)]
+            pack[at + 16 : at + 25] = y_ref[t, pl.ds(32 + last, 9)]
 
 
 PIECE, EDGES, PACK = 58, 296, 368
-FAR_PIECE, FAR_PACK = 25, 128
+FAR_PIECE, FAR_PACK = 25, 80
 
 
 def plain_low(ref, t, tall):
@@ -376,7 +383,7 @@
 
 def near_kernel(
     limits, own_low, own_high, own_low_low, own_low_high, odd_ref, even_ref,
-    hl0_ref, vh0_ref, hl1_ref, vh1_ref, hl2_ref, vh2_ref, next_ref,
+    hl0_ref, vh0_ref, hl1_ref, vh1_ref, hl2_ref, vh2_ref, next_ref, edge_ref,
     l_ref, h_ref, b_ref, x_ref, lh_ref, hh_ref,
 ):
     above, under = sides(lax.axis_index("rows") % 2 == 0, odd_ref, even_ref)
@@ -396,13 +403,16 @@
         low, high = lifted(l_ref, t, 32, 6, 16)
         lh_ref[0:24, s] = limited(limits, 1, 1, high[2:26])
         b_ref[3:13, s], b_ref[13:35, s], b_ref[35:45, s] = above(part(32, 10)), low[3:25], under(part(32, 10))
+        b_ref[48:56, s], b_ref[56:64, s] = above(part(0)), under(part(8))
+        b_ref[64:72, s], b_ref[72:80, s] = above(part(16)), under(part(24))
         low, high = lifted(h_ref, t, 32, 6, 16)
         hl1_ref[:, s] = limited(limits, 1, 0, low[2:26])
         hh_ref[0:24, s] = limited(limits, 1, 2, high[2:26])
     vh1_ref[...] = across(1, lh_ref[0:24, :640], hh_ref[0:24, :640])[:, :1152]
     low, high = split_lanes(2, b_ref[...])
-    spread(next_ref, slice(None), low)
-    spread(h_ref, slice(0, 48), high)
+    spread(next_ref, slice(None), low[0:48])
+    spread(edge_ref, slice(None), low[48:80])
+    spread(h_ref, slice(0, 48), high[0:48])
     for t in range(WIDE[2] // 128):
         s = slice(128 * t, 128 * t + 128)
         high = lifted(next_ref, t, 24, 8, 8)[1]
@@ -443,36 +453,30 @@
 
 
 def far_kernel(
-    limits, hl0_ref, vh0_ref, hl1_ref, vh1_ref, hl2_ref, vh2_ref, next_ref,
-    odd_ref, even_ref, even_far, odd_far, out_ref, f_ref, g_ref, l_ref, h_ref, b_ref, v_ref, r_ref, o_ref, sems,
+    limits, hl0_ref, vh0_ref, hl1_ref, vh1_ref, hl2_ref, vh2_ref, next_ref, edge_ref,
+    odd_far, even_far, out_ref, f_ref, g_ref, l_ref, h_ref, b_ref, v_ref, r_ref, o_ref, sems,
 ):
     row, count = lax.axis_index("rows"), lax.axis_size("rows")
-    above, under = sides(row % 2 == 0, odd_ref, even_ref)
     above_far, under_far = sides(row % 4 < 2, odd_far, even_far)
-    for t in range(WIDE[1] // 128):
+    for t in range(WIDE[2] // 128):
         s = slice(128 * t, 128 * t + 128)
-
-        def part(offset, at=PIECE * t):
-            return slice(at + offset, at + offset + 8)
 
         def far_part(offset, size=8, at=FAR_PIECE * t):
             return slice(at + offset, at + offset + size)
 
-        f_ref[t, 0:8], f_ref[t, 8:16] = above_far(far_part(0)), above(part(0))
-        f_ref[t, 16:24], f_ref[t, 24:32] = under(part(8)), under_far(far_part(0))
+        f_ref[t, 0:8], f_ref[t, 8:24], f_ref[t, 24:32] = (
+            above_far(far_part(0)), edge_ref[t, 0:16], under_far(far_part(0))
+        )
         near = neighbours(0, [(4, row == 1)], [(11, row == count - 2)])
         one = forward_lift(*halves_of(f_ref, t, 16), near)[0]
         g_ref[t, 10:14], g_ref[t, 42:46] = one[2:6], one[10:14]
-        g_ref[t, 2:10], g_ref[t, 14:22] = above_far(far_part(8)), above(part(16))
-        g_ref[t, 34:42], g_ref[t, 46:54] = under(part(24)), under_far(far_part(8))
+        g_ref[t, 2:10], g_ref[t, 14:22] = above_far(far_part(8)), edge_ref[t, 16:24]
+        g_ref[t, 34:42], g_ref[t, 46:54] = edge_ref[t, 24:32], under_far(far_part(8))
         near = neighbours(0, [(6, row == 1)], [(21, row == count - 2)])
         two = forward_lift(*halves_of(g_ref, t, 32), near)[0]
-        b_ref[0:9, s], b_ref[9:15, s] = above_far(far_part(16, 9)), two[3:9]
-        b_ref[16:22, s], b_ref[22:31, s] = two[19:25], under_far(far_part(16, 9))
-    low = split_lanes(2, b_ref[0:32, :640])[0]
-    for t in range(WIDE[2] // 128):
-        s = slice(128 * t, 128 * t + 128)
-        l_ref[t, 0:15], l_ref[t, 15:57], l_ref[t, 57:72] = low[0:15, s], next_ref[t, 3:45], low[16:31, s]
+        l_ref[t, 0:9], l_ref[t, 9:15] = above_far(far_part(16, 9)), two[3:9]
+        l_ref[t, 15:57] = next_ref[t, 3:45]
+        l_ref[t, 57:63], l_ref[t, 63:72] = two[19:25], under_far(far_part(16, 9))
         b_ref[0:32, s] = lifted(l_ref, t, 40, 14, 8)[0][2:34]
     low, high = split_lanes(3, b_ref[0:32, :384])
     spread(l_ref, slice(0, 32), low)
@@ -579,7 +583,7 @@
         columns_kernel,
         (f32(PACK, 128), f32(PACK, 128), f32(FAR_PACK, 128), f32(FAR_PACK, 128))
         + (f32(9, ROWS, 128), f32(9, ROWS, 128), f32(5, ROWS, 128), f32(5, ROWS, 128)),
-        [scratch(5, 32, 128), scratch(5, 16, 128), scratch(5, 32, 128)],
+        [scratch(5, 32, 128), scratch(5, 16, 128), scratch(5, 32, 128), scratch(48, 640), scratch(3, 48, 128)],
         *inner,
         odd,
         even,
@@ -588,8 +592,9 @@
     far = exchange(for_even_far, for_odd_far, "rows", 2)
     known = call(
         near_kernel,
-        (f32(40, 1152), f32(40, COLS), f32(24, 640), f32(24, 1152), f32(16, 384), f32(16, 640), f32(3, 48, 128)),
-        [scratch(5, 64, 128), scratch(5, 64, 128), scratch(48, 640), scratch(18, 80, 128)]
+        (f32(40, 1152), f32(40, COLS), f32(24, 640), f32(24, 1152), f32(16, 384), f32(16, 640))
+        + (f32(3, 48, 128), f32(3, 32, 128)),
+        [scratch(5, 64, 128), scratch(5, 64, 128), scratch(80, 640), scratch(18, 80, 128)]
         + [scratch(40, 1152), scratch(40, 1152)],
         limits,
         *own,
@@ -599,14 +604,12 @@
     return call(
         far_kernel,
         f32(ROWS, COLS),
-        [scratch(5, 32, 128), scratch(5, 64, 128), scratch(3, 80, 128), scratch(3, 80, 128)]
-        + [scratch(32, 640), scratch(40, COLS), scratch(32, 256), scratch(16, 80, 128)]
+        [scratch(3, 32, 128), scratch(3, 64, 128), scratch(3, 80, 128), scratch(3, 80, 128)]
+        + [scratch(32, 384), scratch(40, COLS), scratch(32, 256), scratch(16, 80, 128)]
         + [pltpu.SemaphoreType.DMA((16,))],
         limits,
         *known,
-        *near,
-        far[1],
-        far[0],
+        *far,
         out_space=pl.ANY,
     )
 

time: 36 us -> 34.7 us (0.964)
  the two profiles are of different devices: /device:TPU:216 before, /device:TPU:222 now
where the time goes in v8:
time: 34.7 us; the launch traced here: 34.4 us
  starting transfers between devices  22.1 us (64%)
  Pallas kernels  8.16 us (24%)
  waiting for transfers between devices  2.97 us (9%)
  local copies, waits for them, and re-layouts  1.05 us (3%)
    ppermute x3, starting transfers between devices, exchange(): odd = lax.ppermute(for_odd, axis, swaps(axis, apart, apart))  12.7 us
    ppermute x3, starting transfers between devices, exchange(): even = lax.ppermute(for_even, axis, swaps(axis, 0, apart))  9.44 us
    pallas_call x5, Pallas kernels, call(): pl.pallas_call(kernel, out_shape=outs, in_specs=[smem] * scalars + [pl.Bl...  8.16 us
    ppermute x3, waiting for transfers between devices, exchange(): even = lax.ppermute(for_even, axis, swaps(axis, 0, apart))  2.96 us
    unnamed x6, local copies, waits for them, and re-layouts  1.05 us
  transfers between devices with their start and end apart: 6, of which 1 were waited for; matrix products, arithmetic and copies ran while one was open for 0% of the time, Pallas kernels for 10%

profile of v8, /device:TPU:222, one launch (start us, length us, event | category | flops | bytes accessed | tf_op | source)
XLA Modules:
  0.0 34.4 jit_solution(11776118640252177397)
XLA Ops:
  0.0 0.0 copy-start
  0.0 1.0 %copy-done = f32[64,2048]{1,0:T(8,128)S(1)} copy-done((f32[64,2048]{1,0:T(8,128)S(1)}, f32[64,2048]{1,0:T(8,128)}, u32[]{:S(2)}) %copy-start) | copy-done | bytes 524312
  1.0 0.0 copy-start.1
  1.1 0.0 copy-start.2
  1.1 2.1 %collective-permute-start = (f32[64,128]{1,0:T(8,128)S(1)}, f32[64,128]{1,0:T(8,128)S(1)}, u32[]{:S(2)}, u32[]{:S(2)}) collective-permute-start(f32[64,128]{1,0:T(8,128)S(1)} %get-tuple-element.31), channel_id=1, source_target_pairs={{1,2},{2,1},{3,4},{4,3},{5,6},{6,5},{7,8},{8,7},{9,10},{10,9},{11,... | collective-permute-start | bytes 98312 | tf_op jit(solution)/shard_map/ppermute | solution.py:538
  3.2 5.6 %collective-permute-start.1 = (f32[64,128]{1,0:T(8,128)S(1)}, f32[64,128]{1,0:T(8,128)S(1)}, u32[]{:S(2)}, u32[]{:S(2)}) collective-permute-start(f32[64,128]{1,0:T(8,128)S(1)} %get-tuple-element.32), channel_id=1, source_target_pairs={{0,1},{1,0},{2,3},{3,2},{4,5},{5,4},{6,7},{7,6},{8,9},{9,8},{10,11... | collective-permute-start | bytes 98312 | tf_op jit(solution)/shard_map/ppermute | solution.py:537
  8.8 0.0 copy-done.1
  8.8 0.0 copy-done.2
  8.8 0.9 %shard_map.28 = (f32[64,896]{1,0:T(8,128)S(1)}, f32[64,896]{1,0:T(8,128)S(1)}, f32[64,256]{1,0:T(8,128)S(1)}, f32[16,128]{1,0:T(8,128)S(1)}) custom-call(f32[4,3]{1,0:T(4,128)S(1)} %copy-done.2, f32[64,2048]{1,0:T(8,128)S(1)} %copy-done.1), custom_call_target="tpu_custom_call" | custom-call | flops 2000000000 | bytes 4000000 | tf_op jit(solution)/shard_map/pallas_call | solution.py:553
  9.7 0.0 collective-permute-done.odd_ref
  9.7 0.0 collective-permute-done.1.even_ref
  9.7 1.6 %shard_map.30 = (f32[368,128]{1,0:T(8,128)S(1)}, f32[368,128]{1,0:T(8,128)S(1)}, f32[80,128]{1,0:T(8,128)S(1)}, f32[80,128]{1,0:T(8,128)S(1)}, f32[9,64,128]{2,1...) custom-call(f32[64,896]{1,0:T(8,128)S(1)} %get-tuple-element.28.e_ref, ...), custom_call_target="tpu_custom_call" | custom-call | tf_op jit(solution)/shard_map/pallas_call | solution.py:553
  11.4 4.6 %collective-permute-start.2 = (f32[368,128]{1,0:T(8,128)S(1)}, f32[368,128]{1,0:T(8,128)S(1)}, u32[]{:S(2)}, u32[]{:S(2)}) collective-permute-start(f32[368,128]{1,0:T(8,128)S(1)} %get-tuple-element.37), channel_id=1, source_target_pairs={{16,32},{32,16},{48,64},{64,48},{80,96},{96,80},{112,128},{128,112... | collective-permute-start | bytes 565256 | tf_op jit(solution)/shard_map/ppermute | solution.py:538
  16.0 1.9 %collective-permute-start.3 = (f32[368,128]{1,0:T(8,128)S(1)}, f32[368,128]{1,0:T(8,128)S(1)}, u32[]{:S(2)}, u32[]{:S(2)}) collective-permute-start(f32[368,128]{1,0:T(8,128)S(1)} %get-tuple-element.38), channel_id=1, source_target_pairs={{0,16},{16,0},{32,48},{48,32},{64,80},{80,64},{96,112},{112,96},{1... | collective-permute-start | bytes 565256 | tf_op jit(solution)/shard_map/ppermute | solution.py:537
  17.9 6.0 %collective-permute-start.4 = (f32[80,128]{1,0:T(8,128)S(1)}, f32[80,128]{1,0:T(8,128)S(1)}, u32[]{:S(2)}, u32[]{:S(2)}) collective-permute-start(f32[80,128]{1,0:T(8,128)S(1)} %get-tuple-element.47), channel_id=1, source_target_pairs={{32,64},{64,32},{48,80},{80,48},{96,128},{128,96},{112,144},{144,1... | collective-permute-start | bytes 122888 | tf_op jit(solution)/shard_map/ppermute | solution.py:538
  23.9 1.9 %collective-permute-start.5 = (f32[80,128]{1,0:T(8,128)S(1)}, f32[80,128]{1,0:T(8,128)S(1)}, u32[]{:S(2)}, u32[]{:S(2)}) collective-permute-start(f32[80,128]{1,0:T(8,128)S(1)} %get-tuple-element.48), channel_id=1, source_target_pairs={{0,32},{32,0},{16,48},{48,16},{64,96},{96,64},{80,112},{112,80},{1... | collective-permute-start | bytes 122888 | tf_op jit(solution)/shard_map/ppermute | solution.py:537
  25.9 0.0 collective-permute-done.2.odd_ref
  25.9 0.0 collective-permute-done.3.even_ref
  25.9 2.5 %shard_map.31 = (f32[40,1152]{1,0:T(8,128)S(1)}, f32[40,2048]{1,0:T(8,128)S(1)}, f32[24,640]{1,0:T(8,128)S(1)}, f32[24,1152]{1,0:T(8,128)S(1)}, f32[16,384]{1,0:...) custom-call(f32[16,128]{1,0:T(8,128)S(1)} %get-tuple-element.27.limits, ...), custom_call_target="tpu_custom_call" | custom-call | flops 2000000000 | bytes 4000000 | tf_op jit(solution)/shard_map/pallas_call | solution.py:553
  28.4 0.0 collective-permute-done.4.odd_far
  28.4 3.0 %collective-permute-done.5.even_far = f32[80,128]{1,0:T(8,128)S(1)} collective-permute-done((f32[80,128]{1,0:T(8,128)S(1)}, f32[80,128]{1,0:T(8,128)S(1)}, u32[]{:S(2)}, u32[]{:S(2)}) %collective-permute-start.5) | collective-permute-done | bytes 40992 | tf_op jit(solution)/shard_map/ppermute | solution.py:537
  31.3 3.1 %shard_map.32 = f32[64,2048]{1,0:T(8,128)} custom-call(f32[16,128]{1,0:T(8,128)S(1)} %get-tuple-element.27.limits, f32[40,1152]{1,0:T(8,128)S(1)} %get-tuple-element.39.hl0_ref, f32[40,2048]{1,0:T(8,128)S(1)} %get-tuple-element.40.vh0_ref, f32[24,640]{1,0:T(8,128)S(1)} %get-tuple-element.41.hl1_ref, f32[24,1152]{1,0:T(8,128)S(1)} %get-tuple-element.42.vh1_ref, ...), custom_call_target="tpu_custom_call" | custom-call | tf_op jit(solution)/shard_map/pallas_call | solution.py:553
  (1 shorter events, 0.0 us)
Async XLA Ops:
  0.0 1.0 %copy-start = (f32[64,2048]{1,0:T(8,128)S(1)}, f32[64,2048]{1,0:T(8,128)}, u32[]{:S(2)}) copy-start(f32[64,2048]{1,0:T(8,128)} %x_ref.3) | copy-start | bytes 1572868
  1.0 7.7 %copy-start.1 = (f32[64,2048]{1,0:T(8,128)S(1)}, f32[64,2048]{1,0:T(8,128)}, u32[]{:S(2)}) copy-start(f32[64,2048]{1,0:T(8,128)} %x_ref.3) | copy-start | bytes 1572868
  1.1 7.7 %copy-start.2 = (f32[4,3]{1,0:T(4,128)S(1)}, f32[4,3]{1,0:T(4,128)}, u32[]{:S(2)}) copy-start(f32[4,3]{1,0:T(4,128)} %t_ref.1) | copy-start | bytes 148
  1.1 8.6 %collective-permute-start = (f32[64,128]{1,0:T(8,128)S(1)}, f32[64,128]{1,0:T(8,128)S(1)}, u32[]{:S(2)}, u32[]{:S(2)}) collective-permute-start(f32[64,128]{1,0:T(8,128)S(1)} %get-tuple-element.31), channel_id=1, source_target_pairs={{1,2},{2,1},{3,4},{4,3},{5,6},{6,5},{7,8},{8,7},{9,10},{10,9},{11,... | collective-permute-start | bytes 98312 | tf_op jit(solution)/shard_map/ppermute | solution.py:538
  3.2 6.6 %collective-permute-start.1 = (f32[64,128]{1,0:T(8,128)S(1)}, f32[64,128]{1,0:T(8,128)S(1)}, u32[]{:S(2)}, u32[]{:S(2)}) collective-permute-start(f32[64,128]{1,0:T(8,128)S(1)} %get-tuple-element.32), channel_id=1, source_target_pairs={{0,1},{1,0},{2,3},{3,2},{4,5},{5,4},{6,7},{7,6},{8,9},{9,8},{10,11... | collective-permute-start | bytes 98312 | tf_op jit(solution)/shard_map/ppermute | solution.py:537
  11.4 14.5 %collective-permute-start.2 = (f32[368,128]{1,0:T(8,128)S(1)}, f32[368,128]{1,0:T(8,128)S(1)}, u32[]{:S(2)}, u32[]{:S(2)}) collective-permute-start(f32[368,128]{1,0:T(8,128)S(1)} %get-tuple-element.37), channel_id=1, source_target_pairs={{16,32},{32,16},{48,64},{64,48},{80,96},{96,80},{112,128},{128,112... | collective-permute-start | bytes 565256 | tf_op jit(solution)/shard_map/ppermute | solution.py:538
  16.0 9.9 %collective-permute-start.3 = (f32[368,128]{1,0:T(8,128)S(1)}, f32[368,128]{1,0:T(8,128)S(1)}, u32[]{:S(2)}, u32[]{:S(2)}) collective-permute-start(f32[368,128]{1,0:T(8,128)S(1)} %get-tuple-element.38), channel_id=1, source_target_pairs={{0,16},{16,0},{32,48},{48,32},{64,80},{80,64},{96,112},{112,96},{1... | collective-permute-start | bytes 565256 | tf_op jit(solution)/shard_map/ppermute | solution.py:537
  17.9 10.5 %collective-permute-start.4 = (f32[80,128]{1,0:T(8,128)S(1)}, f32[80,128]{1,0:T(8,128)S(1)}, u32[]{:S(2)}, u32[]{:S(2)}) collective-permute-start(f32[80,128]{1,0:T(8,128)S(1)} %get-tuple-element.47), channel_id=1, source_target_pairs={{32,64},{64,32},{48,80},{80,48},{96,128},{128,96},{112,144},{144,1... | collective-permute-start | bytes 122888 | tf_op jit(solution)/shard_map/ppermute | solution.py:538
  23.9 7.4 %collective-permute-start.5 = (f32[80,128]{1,0:T(8,128)S(1)}, f32[80,128]{1,0:T(8,128)S(1)}, u32[]{:S(2)}, u32[]{:S(2)}) collective-permute-start(f32[80,128]{1,0:T(8,128)S(1)} %get-tuple-element.48), channel_id=1, source_target_pairs={{0,32},{32,0},{16,48},{48,16},{64,96},{96,64},{80,112},{112,80},{1... | collective-permute-start | bytes 122888 | tf_op jit(solution)/shard_map/ppermute | solution.py:537

commit v9 on v8

--- a/solution.py
+++ b/solution.py
@@ -51,40 +51,46 @@
 
 
 def lift_lanes(even, odd, first, count, at_start, at_end, inverse=False):
-    rows, width = even.shape
-    if width >= STEPS_FROM:
+    rows, width = (odd if even is None else even).shape
+    if width >= STEPS_FROM and even is not None and odd is not None:
         near = neighbours(1, [(first, at_start)], [(first + count - 1, at_end)])
         lift = inverse_lift if inverse else forward_lift
         groups = [slice(k, min(k + GROUP, rows)) for k in range(0, rows, GROUP)]
         parts = [lift(even[g], odd[g], near) for g in groups]
         return [jnp.concatenate(x, 0) if len(x) > 1 else x[0] for x in zip(*parts)]
     last = first + count - 1
-    e, o = {0: even}, {0: odd}
-    for x in (e, o):
-        width = x[0].shape[1]
-        for offset in (-2, -1, 1, 2):
-            x[offset] = pltpu.roll(x[0], -offset % width, 1)
-    fixed = lambda x, source, lane, flag: patch(x, source, 1, lane, flag)
-    ends_of = {
-        ("even", -1): [(e[1], first, at_start)],
-        ("even", -2): [(e[2], first, at_start), (e[0], first + 1, at_start)],
-        ("even", 1): [(e[0], last, at_end)],
-        ("even", 2): [(e[-1], last, at_end), (e[1], last - 1, at_end)],
-        ("odd", -1): [(o[0], first, at_start)],
-        ("odd", -2): [(o[1], first, at_start), (o[-1], first + 1, at_start)],
-        ("odd", 1): [(o[-1], last, at_end)],
-        ("odd", 2): [(o[-2], last, at_end), (o[0], last - 1, at_end)],
-    }
-    shifted = {("even", 0): even, ("odd", 0): odd}
-    for (sequence, offset), patches in ends_of.items():
-        x = (e if sequence == "even" else o)[offset]
-        for patch_of in patches:
-            x = fixed(x, *patch_of)
-        shifted[sequence, offset] = x
+    shifted = {}
+    for name, half in (("even", even), ("odd", odd)):
+        if half is None:
+            continue
+        x = {offset: pltpu.roll(half, -offset % width, 1) for offset in (-2, -1, 1, 2)}
+        x[0] = half
+        if name == "even":
+            mirrored = {
+                -1: [(1, first, at_start)],
+                -2: [(2, first, at_start), (0, first + 1, at_start)],
+                1: [(0, last, at_end)],
+                2: [(-1, last, at_end), (1, last - 1, at_end)],
+            }
+        else:
+            mirrored = {
+                -1: [(0, first, at_start)],
+                -2: [(1, first, at_start), (-1, first + 1, at_start)],
+                1: [(-1, last, at_end)],
+                2: [(-2, last, at_end), (0, last - 1, at_end)],
+            }
+        shifted[name, 0] = half
+        for offset, patches in mirrored.items():
+            moved = x[offset]
+            for source, lane, flag in patches:
+                moved = patch(moved, x[source], 1, lane, flag)
+            shifted[name, offset] = moved
     out = []
     for taps in lifted_taps(inverse):
         by_tap = {}
         for key, tap in sorted(taps.items()):
+            if key not in shifted:
+                continue
             by_tap.setdefault(round(tap, 9), []).append((tap, shifted[key]))
         total = None
         for group in by_tap.values():
@@ -383,8 +389,8 @@
 
 def near_kernel(
     limits, own_low, own_high, own_low_low, own_low_high, odd_ref, even_ref,
-    hl0_ref, vh0_ref, hl1_ref, vh1_ref, hl2_ref, vh2_ref, next_ref, edge_ref,
-    l_ref, h_ref, b_ref, x_ref, lh_ref, hh_ref,
+    ah0_ref, vh0_ref, ah1_ref, vh1_ref, ah2_ref, vh2_ref, next_ref, edge_ref,
+    l_ref, h_ref, b_ref, x_ref, lh_ref, hh_ref, hl_ref,
 ):
     above, under = sides(lax.axis_index("rows") % 2 == 0, odd_ref, even_ref)
     for t in range(WIDE[1] // 128):
@@ -406,8 +412,9 @@
         b_ref[48:56, s], b_ref[56:64, s] = above(part(0)), under(part(8))
         b_ref[64:72, s], b_ref[72:80, s] = above(part(16)), under(part(24))
         low, high = lifted(h_ref, t, 32, 6, 16)
-        hl1_ref[:, s] = limited(limits, 1, 0, low[2:26])
+        hl_ref[0:24, s] = limited(limits, 1, 0, low[2:26])
         hh_ref[0:24, s] = limited(limits, 1, 2, high[2:26])
+    ah1_ref[...] = across(1, None, hl_ref[0:24, :640])[:, :1152]
     vh1_ref[...] = across(1, lh_ref[0:24, :640], hh_ref[0:24, :640])[:, :1152]
     low, high = split_lanes(2, b_ref[...])
     spread(next_ref, slice(None), low[0:48])
@@ -418,8 +425,9 @@
         high = lifted(next_ref, t, 24, 8, 8)[1]
         lh_ref[0:16, s] = limited(limits, 2, 1, high[4:20])
         low, high = lifted(h_ref, t, 24, 8, 8)
-        hl2_ref[:, s] = limited(limits, 2, 0, low[4:20])
+        hl_ref[0:16, s] = limited(limits, 2, 0, low[4:20])
         hh_ref[0:16, s] = limited(limits, 2, 2, high[4:20])
+    ah2_ref[...] = across(2, None, hl_ref[0:16, :384])[:, :640]
     vh2_ref[...] = across(2, lh_ref[0:16, :384], hh_ref[0:16, :384])[:, :640]
     low, high = (
         jnp.concatenate(
@@ -445,15 +453,16 @@
         high = lifted(x_ref, t, 40, 4, 32)[1]
         lh_ref[:, s] = limited(limits, 0, 1, high)
         low, high = lifted(x_ref, t + 9, 40, 4, 32)
-        hl0_ref[:, s] = limited(limits, 0, 0, low)
+        hl_ref[:, s] = limited(limits, 0, 0, low)
         hh_ref[:, s] = limited(limits, 0, 2, high)
 
     tiles(WIDE[0], lift)
+    ah0_ref[...] = across(0, None, hl_ref[...])[:, 128 : 128 + COLS]
     vh0_ref[...] = across(0, lh_ref[...], hh_ref[...])[:, 128 : 128 + COLS]
 
 
 def far_kernel(
-    limits, hl0_ref, vh0_ref, hl1_ref, vh1_ref, hl2_ref, vh2_ref, next_ref, edge_ref,
+    limits, ah0_ref, vh0_ref, ah1_ref, vh1_ref, ah2_ref, vh2_ref, next_ref, edge_ref,
     odd_far, even_far, out_ref, f_ref, g_ref, l_ref, h_ref, b_ref, v_ref, r_ref, o_ref, sems,
 ):
     row, count = lax.axis_index("rows"), lax.axis_size("rows")
@@ -503,9 +512,10 @@
             o_ref[t, pl.ds(1, long, stride=2)] = odd
         size = OWN[level - 1] + 8
         low = joined(o_ref, slice(4, 4 + size), low.shape[1])
-        hl, high = ((hl0_ref, vh0_ref), (hl1_ref, vh1_ref), (hl2_ref, vh2_ref))[level - 1]
-        low = across(level - 1, low, hl[...])
+        added, high = ((ah0_ref, vh0_ref), (ah1_ref, vh1_ref), (ah2_ref, vh2_ref))[level - 1]
+        low = across(level - 1, low, None)
         low = low[:, 128 : 128 + COLS] if level == 1 else low[:, : high.shape[1]]
+        low = low + added[...]
     v_ref[...] = low
     near = neighbours(0, [(4, at_start)], [(35, at_end)])
 
@@ -592,10 +602,10 @@
     far = exchange(for_even_far, for_odd_far, "rows", 2)
     known = call(
         near_kernel,
-        (f32(40, 1152), f32(40, COLS), f32(24, 640), f32(24, 1152), f32(16, 384), f32(16, 640))
+        (f32(40, COLS), f32(40, COLS), f32(24, 1152), f32(24, 1152), f32(16, 640), f32(16, 640))
         + (f32(3, 48, 128), f32(3, 32, 128)),
         [scratch(5, 64, 128), scratch(5, 64, 128), scratch(80, 640), scratch(18, 80, 128)]
-        + [scratch(40, 1152), scratch(40, 1152)],
+        + [scratch(40, 1152), scratch(40, 1152), scratch(40, 1152)],
         limits,
         *own,
         *near,

time: 34.7 us -> 34.5 us (level)
  waiting for transfers between devices: 2.97 us -> 2.56 us
    ppermute x3, waiting for transfers between devices: 2.96 us -> 2.55 us  [exchange(): even = lax.ppermute(for_even, axis, swaps(axis, 0, apart))]
  transfers between devices with their start and end apart: 6 -> 6, of which waited for: 1 -> 1; matrix products, arithmetic and copies ran while one was open for 0% -> 0% of each run, Pallas kernels for 10% -> 11%
where the time goes in v9:
time: 34.5 us; the launch traced here: 34.2 us
  starting transfers between devices  22.1 us (64%)
  Pallas kernels  8.33 us (24%)
  waiting for transfers between devices  2.56 us (7%)
  local copies, waits for them, and re-layouts  1.05 us (3%)
    ppermute x3, starting transfers between devices, exchange(): odd = lax.ppermute(for_odd, axis, swaps(axis, apart, apart))  12.7 us
    ppermute x3, starting transfers between devices, exchange(): even = lax.ppermute(for_even, axis, swaps(axis, 0, apart))  9.44 us
    pallas_call x5, Pallas kernels, call(): pl.pallas_call(kernel, out_shape=outs, in_specs=[smem] * scalars + [pl.Bl...  8.33 us
    ppermute x3, waiting for transfers between devices, exchange(): even = lax.ppermute(for_even, axis, swaps(axis, 0, apart))  2.55 us
    unnamed x6, local copies, waits for them, and re-layouts  1.05 us
  transfers between devices with their start and end apart: 6, of which 1 were waited for; matrix products, arithmetic and copies ran while one was open for 0% of the time, Pallas kernels for 11%

profile of v9, /device:TPU:222, one launch (start us, length us, event | category | flops | bytes accessed | tf_op | source)
XLA Modules:
  0.0 34.2 jit_solution(366262954172592713)
XLA Ops:
  0.0 0.0 copy-start
  0.0 1.0 %copy-done = f32[64,2048]{1,0:T(8,128)S(1)} copy-done((f32[64,2048]{1,0:T(8,128)S(1)}, f32[64,2048]{1,0:T(8,128)}, u32[]{:S(2)}) %copy-start) | copy-done | bytes 524312
  1.0 0.0 copy-start.1
  1.1 0.0 copy-start.2
  1.1 2.1 %collective-permute-start = (f32[64,128]{1,0:T(8,128)S(1)}, f32[64,128]{1,0:T(8,128)S(1)}, u32[]{:S(2)}, u32[]{:S(2)}) collective-permute-start(f32[64,128]{1,0:T(8,128)S(1)} %get-tuple-element.31), channel_id=1, source_target_pairs={{1,2},{2,1},{3,4},{4,3},{5,6},{6,5},{7,8},{8,7},{9,10},{10,9},{11,... | collective-permute-start | bytes 98312 | tf_op jit(solution)/shard_map/ppermute | solution.py:548
  3.2 5.6 %collective-permute-start.1 = (f32[64,128]{1,0:T(8,128)S(1)}, f32[64,128]{1,0:T(8,128)S(1)}, u32[]{:S(2)}, u32[]{:S(2)}) collective-permute-start(f32[64,128]{1,0:T(8,128)S(1)} %get-tuple-element.32), channel_id=1, source_target_pairs={{0,1},{1,0},{2,3},{3,2},{4,5},{5,4},{6,7},{7,6},{8,9},{9,8},{10,11... | collective-permute-start | bytes 98312 | tf_op jit(solution)/shard_map/ppermute | solution.py:547
  8.8 0.0 copy-done.1
  8.8 0.0 copy-done.2
  8.8 0.9 %shard_map.28 = (f32[64,896]{1,0:T(8,128)S(1)}, f32[64,896]{1,0:T(8,128)S(1)}, f32[64,256]{1,0:T(8,128)S(1)}, f32[16,128]{1,0:T(8,128)S(1)}) custom-call(f32[4,3]{1,0:T(4,128)S(1)} %copy-done.2, f32[64,2048]{1,0:T(8,128)S(1)} %copy-done.1), custom_call_target="tpu_custom_call" | custom-call | flops 2000000000 | bytes 4000000 | tf_op jit(solution)/shard_map/pallas_call | solution.py:563
  9.7 0.0 collective-permute-done.odd_ref
  9.7 0.0 collective-permute-done.1.even_ref
  9.7 1.6 %shard_map.30 = (f32[368,128]{1,0:T(8,128)S(1)}, f32[368,128]{1,0:T(8,128)S(1)}, f32[80,128]{1,0:T(8,128)S(1)}, f32[80,128]{1,0:T(8,128)S(1)}, f32[9,64,128]{2,1...) custom-call(f32[64,896]{1,0:T(8,128)S(1)} %get-tuple-element.28.e_ref, ...), custom_call_target="tpu_custom_call" | custom-call | tf_op jit(solution)/shard_map/pallas_call | solution.py:563
  11.4 4.6 %collective-permute-start.2 = (f32[368,128]{1,0:T(8,128)S(1)}, f32[368,128]{1,0:T(8,128)S(1)}, u32[]{:S(2)}, u32[]{:S(2)}) collective-permute-start(f32[368,128]{1,0:T(8,128)S(1)} %get-tuple-element.37), channel_id=1, source_target_pairs={{16,32},{32,16},{48,64},{64,48},{80,96},{96,80},{112,128},{128,112... | collective-permute-start | bytes 565256 | tf_op jit(solution)/shard_map/ppermute | solution.py:548
  16.0 1.9 %collective-permute-start.3 = (f32[368,128]{1,0:T(8,128)S(1)}, f32[368,128]{1,0:T(8,128)S(1)}, u32[]{:S(2)}, u32[]{:S(2)}) collective-permute-start(f32[368,128]{1,0:T(8,128)S(1)} %get-tuple-element.38), channel_id=1, source_target_pairs={{0,16},{16,0},{32,48},{48,32},{64,80},{80,64},{96,112},{112,96},{1... | collective-permute-start | bytes 565256 | tf_op jit(solution)/shard_map/ppermute | solution.py:547
  17.9 6.0 %collective-permute-start.4 = (f32[80,128]{1,0:T(8,128)S(1)}, f32[80,128]{1,0:T(8,128)S(1)}, u32[]{:S(2)}, u32[]{:S(2)}) collective-permute-start(f32[80,128]{1,0:T(8,128)S(1)} %get-tuple-element.47), channel_id=1, source_target_pairs={{32,64},{64,32},{48,80},{80,48},{96,128},{128,96},{112,144},{144,1... | collective-permute-start | bytes 122888 | tf_op jit(solution)/shard_map/ppermute | solution.py:548
  23.9 1.9 %collective-permute-start.5 = (f32[80,128]{1,0:T(8,128)S(1)}, f32[80,128]{1,0:T(8,128)S(1)}, u32[]{:S(2)}, u32[]{:S(2)}) collective-permute-start(f32[80,128]{1,0:T(8,128)S(1)} %get-tuple-element.48), channel_id=1, source_target_pairs={{0,32},{32,0},{16,48},{48,16},{64,96},{96,64},{80,112},{112,80},{1... | collective-permute-start | bytes 122888 | tf_op jit(solution)/shard_map/ppermute | solution.py:547
  25.9 0.0 collective-permute-done.2.odd_ref
  25.9 0.0 collective-permute-done.3.even_ref
  25.9 2.9 %shard_map.31 = (f32[40,2048]{1,0:T(8,128)S(1)}, f32[40,2048]{1,0:T(8,128)S(1)}, f32[24,1152]{1,0:T(8,128)S(1)}, f32[24,1152]{1,0:T(8,128)S(1)}, f32[16,640]{1,0...) custom-call(f32[16,128]{1,0:T(8,128)S(1)} %get-tuple-element.27.limits, ...), custom_call_target="tpu_custom_call" | custom-call | flops 2000000000 | bytes 4000000 | tf_op jit(solution)/shard_map/pallas_call | solution.py:563
  28.8 0.0 collective-permute-done.4.odd_far
  28.8 2.5 %collective-permute-done.5.even_far = f32[80,128]{1,0:T(8,128)S(1)} collective-permute-done((f32[80,128]{1,0:T(8,128)S(1)}, f32[80,128]{1,0:T(8,128)S(1)}, u32[]{:S(2)}, u32[]{:S(2)}) %collective-permute-start.5) | collective-permute-done | bytes 40992 | tf_op jit(solution)/shard_map/ppermute | solution.py:547
  31.3 2.8 %shard_map.32 = f32[64,2048]{1,0:T(8,128)} custom-call(f32[16,128]{1,0:T(8,128)S(1)} %get-tuple-element.27.limits, f32[40,2048]{1,0:T(8,128)S(1)} %get-tuple-element.39.ah0_ref, f32[40,2048]{1,0:T(8,128)S(1)} %get-tuple-element.40.vh0_ref, f32[24,1152]{1,0:T(8,128)S(1)} %get-tuple-element.41.ah1_ref, f32[24,1152]{1,0:T(8,128)S(1)} %get-tuple-element.42.vh1_ref, ...), custom_call_target="tpu_custom_call" | custom-call | tf_op jit(solution)/shard_map/pallas_call | solution.py:563
  (1 shorter events, 0.0 us)
Async XLA Ops:
  0.0 1.0 %copy-start = (f32[64,2048]{1,0:T(8,128)S(1)}, f32[64,2048]{1,0:T(8,128)}, u32[]{:S(2)}) copy-start(f32[64,2048]{1,0:T(8,128)} %x_ref.3) | copy-start | bytes 1572868
  1.0 7.7 %copy-start.1 = (f32[64,2048]{1,0:T(8,128)S(1)}, f32[64,2048]{1,0:T(8,128)}, u32[]{:S(2)}) copy-start(f32[64,2048]{1,0:T(8,128)} %x_ref.3) | copy-start | bytes 1572868
  1.1 7.7 %copy-start.2 = (f32[4,3]{1,0:T(4,128)S(1)}, f32[4,3]{1,0:T(4,128)}, u32[]{:S(2)}) copy-start(f32[4,3]{1,0:T(4,128)} %t_ref.1) | copy-start | bytes 148
  1.1 8.6 %collective-permute-start = (f32[64,128]{1,0:T(8,128)S(1)}, f32[64,128]{1,0:T(8,128)S(1)}, u32[]{:S(2)}, u32[]{:S(2)}) collective-permute-start(f32[64,128]{1,0:T(8,128)S(1)} %get-tuple-element.31), channel_id=1, source_target_pairs={{1,2},{2,1},{3,4},{4,3},{5,6},{6,5},{7,8},{8,7},{9,10},{10,9},{11,... | collective-permute-start | bytes 98312 | tf_op jit(solution)/shard_map/ppermute | solution.py:548
  3.2 6.6 %collective-permute-start.1 = (f32[64,128]{1,0:T(8,128)S(1)}, f32[64,128]{1,0:T(8,128)S(1)}, u32[]{:S(2)}, u32[]{:S(2)}) collective-permute-start(f32[64,128]{1,0:T(8,128)S(1)} %get-tuple-element.32), channel_id=1, source_target_pairs={{0,1},{1,0},{2,3},{3,2},{4,5},{5,4},{6,7},{7,6},{8,9},{9,8},{10,11... | collective-permute-start | bytes 98312 | tf_op jit(solution)/shard_map/ppermute | solution.py:547
  11.4 14.5 %collective-permute-start.2 = (f32[368,128]{1,0:T(8,128)S(1)}, f32[368,128]{1,0:T(8,128)S(1)}, u32[]{:S(2)}, u32[]{:S(2)}) collective-permute-start(f32[368,128]{1,0:T(8,128)S(1)} %get-tuple-element.37), channel_id=1, source_target_pairs={{16,32},{32,16},{48,64},{64,48},{80,96},{96,80},{112,128},{128,112... | collective-permute-start | bytes 565256 | tf_op jit(solution)/shard_map/ppermute | solution.py:548
  16.0 9.9 %collective-permute-start.3 = (f32[368,128]{1,0:T(8,128)S(1)}, f32[368,128]{1,0:T(8,128)S(1)}, u32[]{:S(2)}, u32[]{:S(2)}) collective-permute-start(f32[368,128]{1,0:T(8,128)S(1)} %get-tuple-element.38), channel_id=1, source_target_pairs={{0,16},{16,0},{32,48},{48,32},{64,80},{80,64},{96,112},{112,96},{1... | collective-permute-start | bytes 565256 | tf_op jit(solution)/shard_map/ppermute | solution.py:547
  17.9 10.9 %collective-permute-start.4 = (f32[80,128]{1,0:T(8,128)S(1)}, f32[80,128]{1,0:T(8,128)S(1)}, u32[]{:S(2)}, u32[]{:S(2)}) collective-permute-start(f32[80,128]{1,0:T(8,128)S(1)} %get-tuple-element.47), channel_id=1, source_target_pairs={{32,64},{64,32},{48,80},{80,48},{96,128},{128,96},{112,144},{144,1... | collective-permute-start | bytes 122888 | tf_op jit(solution)/shard_map/ppermute | solution.py:548
  23.9 7.4 %collective-permute-start.5 = (f32[80,128]{1,0:T(8,128)S(1)}, f32[80,128]{1,0:T(8,128)S(1)}, u32[]{:S(2)}, u32[]{:S(2)}) collective-permute-start(f32[80,128]{1,0:T(8,128)S(1)} %get-tuple-element.48), channel_id=1, source_target_pairs={{0,32},{32,0},{16,48},{48,16},{64,96},{96,64},{80,112},{112,80},{1... | collective-permute-start | bytes 122888 | tf_op jit(solution)/shard_map/ppermute | solution.py:547

commit v10 on v9

--- a/solution.py
+++ b/solution.py
@@ -22,7 +22,7 @@
 OWN = (32, 16, 8, 4)
 
 
-STEPS_FROM = 1152
+STEPS_FROM = 640
 GROUP = 64
 MATRIX_FROM = 640
 

time: 34.5 us -> 34.3 us (level)
  no operation moved by 1% of the time
where the time goes in v10:
time: 34.3 us; the launch traced here: 34.1 us
  starting transfers between devices  22.1 us (64%)
  Pallas kernels  8.17 us (24%)
  waiting for transfers between devices  2.61 us (8%)
  local copies, waits for them, and re-layouts  1.05 us (3%)
    ppermute x3, starting transfers between devices, exchange(): odd = lax.ppermute(for_odd, axis, swaps(axis, apart, apart))  12.7 us
    ppermute x3, starting transfers between devices, exchange(): even = lax.ppermute(for_even, axis, swaps(axis, 0, apart))  9.44 us
    pallas_call x5, Pallas kernels, call(): pl.pallas_call(kernel, out_shape=outs, in_specs=[smem] * scalars + [pl.Bl...  8.17 us
    ppermute x3, waiting for transfers between devices, exchange(): even = lax.ppermute(for_even, axis, swaps(axis, 0, apart))  2.6 us
    unnamed x6, local copies, waits for them, and re-layouts  1.05 us
  transfers between devices with their start and end apart: 6, of which 1 were waited for; matrix products, arithmetic and copies ran while one was open for 0% of the time, Pallas kernels for 11%

profile of v10, /device:TPU:222, one launch (start us, length us, event | category | flops | bytes accessed | tf_op | source)
XLA Modules:
  0.0 34.1 jit_solution(12833276890860152447)
XLA Ops:
  0.0 0.0 copy-start
  0.0 1.0 %copy-done = f32[64,2048]{1,0:T(8,128)S(1)} copy-done((f32[64,2048]{1,0:T(8,128)S(1)}, f32[64,2048]{1,0:T(8,128)}, u32[]{:S(2)}) %copy-start) | copy-done | bytes 524312
  1.0 0.0 copy-start.1
  1.1 0.0 copy-start.2
  1.1 2.1 %collective-permute-start = (f32[64,128]{1,0:T(8,128)S(1)}, f32[64,128]{1,0:T(8,128)S(1)}, u32[]{:S(2)}, u32[]{:S(2)}) collective-permute-start(f32[64,128]{1,0:T(8,128)S(1)} %get-tuple-element.31), channel_id=1, source_target_pairs={{1,2},{2,1},{3,4},{4,3},{5,6},{6,5},{7,8},{8,7},{9,10},{10,9},{11,... | collective-permute-start | bytes 98312 | tf_op jit(solution)/shard_map/ppermute | solution.py:548
  3.2 5.6 %collective-permute-start.1 = (f32[64,128]{1,0:T(8,128)S(1)}, f32[64,128]{1,0:T(8,128)S(1)}, u32[]{:S(2)}, u32[]{:S(2)}) collective-permute-start(f32[64,128]{1,0:T(8,128)S(1)} %get-tuple-element.32), channel_id=1, source_target_pairs={{0,1},{1,0},{2,3},{3,2},{4,5},{5,4},{6,7},{7,6},{8,9},{9,8},{10,11... | collective-permute-start | bytes 98312 | tf_op jit(solution)/shard_map/ppermute | solution.py:547
  8.8 0.0 copy-done.1
  8.8 0.0 copy-done.2
  8.8 0.9 %shard_map.28 = (f32[64,896]{1,0:T(8,128)S(1)}, f32[64,896]{1,0:T(8,128)S(1)}, f32[64,256]{1,0:T(8,128)S(1)}, f32[16,128]{1,0:T(8,128)S(1)}) custom-call(f32[4,3]{1,0:T(4,128)S(1)} %copy-done.2, f32[64,2048]{1,0:T(8,128)S(1)} %copy-done.1), custom_call_target="tpu_custom_call" | custom-call | flops 2000000000 | bytes 4000000 | tf_op jit(solution)/shard_map/pallas_call | solution.py:563
  9.7 0.0 collective-permute-done.odd_ref
  9.7 0.0 collective-permute-done.1.even_ref
  9.7 1.5 %shard_map.30 = (f32[368,128]{1,0:T(8,128)S(1)}, f32[368,128]{1,0:T(8,128)S(1)}, f32[80,128]{1,0:T(8,128)S(1)}, f32[80,128]{1,0:T(8,128)S(1)}, f32[9,64,128]{2,1...) custom-call(f32[64,896]{1,0:T(8,128)S(1)} %get-tuple-element.28.e_ref, ...), custom_call_target="tpu_custom_call" | custom-call | tf_op jit(solution)/shard_map/pallas_call | solution.py:563
  11.3 4.6 %collective-permute-start.2 = (f32[368,128]{1,0:T(8,128)S(1)}, f32[368,128]{1,0:T(8,128)S(1)}, u32[]{:S(2)}, u32[]{:S(2)}) collective-permute-start(f32[368,128]{1,0:T(8,128)S(1)} %get-tuple-element.37), channel_id=1, source_target_pairs={{16,32},{32,16},{48,64},{64,48},{80,96},{96,80},{112,128},{128,112... | collective-permute-start | bytes 565256 | tf_op jit(solution)/shard_map/ppermute | solution.py:548
  15.9 1.9 %collective-permute-start.3 = (f32[368,128]{1,0:T(8,128)S(1)}, f32[368,128]{1,0:T(8,128)S(1)}, u32[]{:S(2)}, u32[]{:S(2)}) collective-permute-start(f32[368,128]{1,0:T(8,128)S(1)} %get-tuple-element.38), channel_id=1, source_target_pairs={{0,16},{16,0},{32,48},{48,32},{64,80},{80,64},{96,112},{112,96},{1... | collective-permute-start | bytes 565256 | tf_op jit(solution)/shard_map/ppermute | solution.py:547
  17.8 6.0 %collective-permute-start.4 = (f32[80,128]{1,0:T(8,128)S(1)}, f32[80,128]{1,0:T(8,128)S(1)}, u32[]{:S(2)}, u32[]{:S(2)}) collective-permute-start(f32[80,128]{1,0:T(8,128)S(1)} %get-tuple-element.47), channel_id=1, source_target_pairs={{32,64},{64,32},{48,80},{80,48},{96,128},{128,96},{112,144},{144,1... | collective-permute-start | bytes 122888 | tf_op jit(solution)/shard_map/ppermute | solution.py:548
  23.8 1.9 %collective-permute-start.5 = (f32[80,128]{1,0:T(8,128)S(1)}, f32[80,128]{1,0:T(8,128)S(1)}, u32[]{:S(2)}, u32[]{:S(2)}) collective-permute-start(f32[80,128]{1,0:T(8,128)S(1)} %get-tuple-element.48), channel_id=1, source_target_pairs={{0,32},{32,0},{16,48},{48,16},{64,96},{96,64},{80,112},{112,80},{1... | collective-permute-start | bytes 122888 | tf_op jit(solution)/shard_map/ppermute | solution.py:547
  25.7 0.0 collective-permute-done.2.odd_ref
  25.8 0.0 collective-permute-done.3.even_ref
  25.8 2.8 %shard_map.31 = (f32[40,2048]{1,0:T(8,128)S(1)}, f32[40,2048]{1,0:T(8,128)S(1)}, f32[24,1152]{1,0:T(8,128)S(1)}, f32[24,1152]{1,0:T(8,128)S(1)}, f32[16,640]{1,0...) custom-call(f32[16,128]{1,0:T(8,128)S(1)} %get-tuple-element.27.limits, ...), custom_call_target="tpu_custom_call" | custom-call | flops 2000000000 | bytes 4000000 | tf_op jit(solution)/shard_map/pallas_call | solution.py:563
  28.6 0.0 collective-permute-done.4.odd_far
  28.6 2.6 %collective-permute-done.5.even_far = f32[80,128]{1,0:T(8,128)S(1)} collective-permute-done((f32[80,128]{1,0:T(8,128)S(1)}, f32[80,128]{1,0:T(8,128)S(1)}, u32[]{:S(2)}, u32[]{:S(2)}) %collective-permute-start.5) | collective-permute-done | bytes 40992 | tf_op jit(solution)/shard_map/ppermute | solution.py:547
  31.2 2.8 %shard_map.32 = f32[64,2048]{1,0:T(8,128)} custom-call(f32[16,128]{1,0:T(8,128)S(1)} %get-tuple-element.27.limits, f32[40,2048]{1,0:T(8,128)S(1)} %get-tuple-element.39.ah0_ref, f32[40,2048]{1,0:T(8,128)S(1)} %get-tuple-element.40.vh0_ref, f32[24,1152]{1,0:T(8,128)S(1)} %get-tuple-element.41.ah1_ref, f32[24,1152]{1,0:T(8,128)S(1)} %get-tuple-element.42.vh1_ref, ...), custom_call_target="tpu_custom_call" | custom-call | tf_op jit(solution)/shard_map/pallas_call | solution.py:563
  (1 shorter events, 0.0 us)
Async XLA Ops:
  0.0 1.0 %copy-start = (f32[64,2048]{1,0:T(8,128)S(1)}, f32[64,2048]{1,0:T(8,128)}, u32[]{:S(2)}) copy-start(f32[64,2048]{1,0:T(8,128)} %x_ref.3) | copy-start | bytes 1572868
  1.0 7.7 %copy-start.1 = (f32[64,2048]{1,0:T(8,128)S(1)}, f32[64,2048]{1,0:T(8,128)}, u32[]{:S(2)}) copy-start(f32[64,2048]{1,0:T(8,128)} %x_ref.3) | copy-start | bytes 1572868
  1.1 7.7 %copy-start.2 = (f32[4,3]{1,0:T(4,128)S(1)}, f32[4,3]{1,0:T(4,128)}, u32[]{:S(2)}) copy-start(f32[4,3]{1,0:T(4,128)} %t_ref.1) | copy-start | bytes 148
  1.1 8.6 %collective-permute-start = (f32[64,128]{1,0:T(8,128)S(1)}, f32[64,128]{1,0:T(8,128)S(1)}, u32[]{:S(2)}, u32[]{:S(2)}) collective-permute-start(f32[64,128]{1,0:T(8,128)S(1)} %get-tuple-element.31), channel_id=1, source_target_pairs={{1,2},{2,1},{3,4},{4,3},{5,6},{6,5},{7,8},{8,7},{9,10},{10,9},{11,... | collective-permute-start | bytes 98312 | tf_op jit(solution)/shard_map/ppermute | solution.py:548
  3.2 6.6 %collective-permute-start.1 = (f32[64,128]{1,0:T(8,128)S(1)}, f32[64,128]{1,0:T(8,128)S(1)}, u32[]{:S(2)}, u32[]{:S(2)}) collective-permute-start(f32[64,128]{1,0:T(8,128)S(1)} %get-tuple-element.32), channel_id=1, source_target_pairs={{0,1},{1,0},{2,3},{3,2},{4,5},{5,4},{6,7},{7,6},{8,9},{9,8},{10,11... | collective-permute-start | bytes 98312 | tf_op jit(solution)/shard_map/ppermute | solution.py:547
  11.3 14.5 %collective-permute-start.2 = (f32[368,128]{1,0:T(8,128)S(1)}, f32[368,128]{1,0:T(8,128)S(1)}, u32[]{:S(2)}, u32[]{:S(2)}) collective-permute-start(f32[368,128]{1,0:T(8,128)S(1)} %get-tuple-element.37), channel_id=1, source_target_pairs={{16,32},{32,16},{48,64},{64,48},{80,96},{96,80},{112,128},{128,112... | collective-permute-start | bytes 565256 | tf_op jit(solution)/shard_map/ppermute | solution.py:548
  15.9 9.9 %collective-permute-start.3 = (f32[368,128]{1,0:T(8,128)S(1)}, f32[368,128]{1,0:T(8,128)S(1)}, u32[]{:S(2)}, u32[]{:S(2)}) collective-permute-start(f32[368,128]{1,0:T(8,128)S(1)} %get-tuple-element.38), channel_id=1, source_target_pairs={{0,16},{16,0},{32,48},{48,32},{64,80},{80,64},{96,112},{112,96},{1... | collective-permute-start | bytes 565256 | tf_op jit(solution)/shard_map/ppermute | solution.py:547
  17.8 10.8 %collective-permute-start.4 = (f32[80,128]{1,0:T(8,128)S(1)}, f32[80,128]{1,0:T(8,128)S(1)}, u32[]{:S(2)}, u32[]{:S(2)}) collective-permute-start(f32[80,128]{1,0:T(8,128)S(1)} %get-tuple-element.47), channel_id=1, source_target_pairs={{32,64},{64,32},{48,80},{80,48},{96,128},{128,96},{112,144},{144,1... | collective-permute-start | bytes 122888 | tf_op jit(solution)/shard_map/ppermute | solution.py:548
  23.8 7.4 %collective-permute-start.5 = (f32[80,128]{1,0:T(8,128)S(1)}, f32[80,128]{1,0:T(8,128)S(1)}, u32[]{:S(2)}, u32[]{:S(2)}) collective-permute-start(f32[80,128]{1,0:T(8,128)S(1)} %get-tuple-element.48), channel_id=1, source_target_pairs={{0,32},{32,0},{16,48},{48,16},{64,96},{96,64},{80,112},{112,80},{1... | collective-permute-start | bytes 122888 | tf_op jit(solution)/shard_map/ppermute | solution.py:547
